TPU v7x, 32 devices: a whole 2x2x4 slice. The times are simulated.
32 devices in a mesh: tower: 2 (over x), batch: 16 (over z, y, core).
Axes of the slice: x: 2, y: 2, z: 4, core: 2. Of those that a mesh axis runs over, the one named last changes fastest.
Arguments:
- tokens: bfloat16 [2, 64, 256, 768], P('tower', 'batch'), may hold values from -6 to 6
- lengths: int32 [2, 64], P('tower', 'batch'), may hold values from 8 to 256, as said below
- positives: int32 [64], P('batch'), may hold values from 0 to 63, each once
- datasets: int32 [64], P('batch'), may hold values from 0 to 3
- w_qkv: bfloat16 [2, 768, 2304], P('tower'), may hold values from -0.21875 to 0.21875
- w_attn_out: bfloat16 [2, 768, 768], P('tower'), may hold values from -0.625 to 0.625
- w_ffn_in: bfloat16 [2, 768, 3072], P('tower'), may hold values from -0.21875 to 0.21875
- w_ffn_out: bfloat16 [2, 3072, 768], P('tower'), may hold values from -0.109375 to 0.109375
- b_ffn_in: float32 [2, 3072], P('tower'), may hold values from -1.2 to 1.2
- biases: float32 [2, 6, 768], P('tower'), may hold values from -1.2 to 1.2
- gains: float32 [2, 2, 768], P('tower'), may hold values from 0.5 to 1.5
Outputs:
- pooled_vectors: float32 [2, 64, 768], P('tower', 'batch')
- grad_tokens: float32 [2, 64, 256, 768], P('tower', 'batch')
- grad_w_qkv: float32 [2, 768, 2304], P('tower', 'batch')
- grad_w_attn_out: float32 [2, 768, 768], P('tower', 'batch')
- grad_w_ffn_in: float32 [2, 768, 3072], P('tower', 'batch')
- grad_w_ffn_out: float32 [2, 3072, 768], P('tower', 'batch')
- grad_b_ffn_in: float32 [2, 3072], P('tower', 'batch')
- grad_biases: float32 [2, 6, 768], P('tower', None, 'batch')
- grad_gains: float32 [2, 2, 768], P('tower', None, 'batch')
Inputs may be any that keep to these rules, and one draw needn't show every extreme that they name: Row 0 holds question lengths, at most 64 and one exactly 64; row 1 holds passage lengths, one exactly 256.
All inputs are finite; a program needn't handle non-finite values.
Results may differ from a plain program's by a relative error of at most 0.02.
Values may be sent and summed in bfloat16 or wider, within the bound.
A program may use at most 192 MiB of HBM per device.

v0:
```python
from functools import partial

import jax
import jax.numpy as jnp
from jax import lax
from jax.sharding import PartitionSpec as P

HEADS = 12


EPS = 1e-12
SCALE = 4.0
HIGH = lax.Precision.HIGHEST


def from_behind(value, axis, steps):
    count = lax.axis_size(axis)
    leading, last = (max(0, -steps), min(count, count - steps))
    return lax.ppermute(value, axis, [(source, source + steps) for source in range(leading, last)])


def product(left, right):
    return jnp.dot(left, right, preferred_element_type=jnp.float32)


def transposed_left(left, right):
    return lax.dot_general(
        left, right, (((0,), (0,)), ((), ())), preferred_element_type=jnp.float32
    )


def transposed_right(left, right):
    return lax.dot_general(
        left, right, (((1,), (1,)), ((), ())), preferred_element_type=jnp.float32
    )


def norm_forward(total, gain, shift):
    mean = jnp.mean(total, axis=-1, keepdims=True)
    centered = total - mean
    inverse = lax.rsqrt(jnp.mean(centered * centered, axis=-1, keepdims=True) + EPS)
    normed = centered * inverse
    return (normed * gain + shift, normed, inverse)


def norm_backward(grad, normed, inverse, gain):
    scaled = grad * gain
    first_mean = jnp.mean(scaled, axis=-1, keepdims=True)
    second_mean = jnp.mean(scaled * normed, axis=-1, keepdims=True)
    d_total = inverse * (scaled - first_mean - normed * second_mean)
    return (d_total, jnp.sum(grad * normed, axis=0), jnp.sum(grad, axis=0))


def scores_of(query_heads, key_heads, keep):
    raw = (
        jnp.einsum("sqhe,skhe->shqk", query_heads, key_heads, preferred_element_type=jnp.float32)
        * 0.125
    )
    return jnp.where(keep[:, None, None, :], raw, -1000000000.0)


def per_device(
    tokens,
    lengths,
    positives,
    datasets,
    w_qkv,
    w_attn_out,
    w_ffn_in,
    w_ffn_out,
    b_ffn_in,
    biases,
    gains,
):
    seq_count, seq_len, width = (tokens.shape[1], tokens.shape[2], tokens.shape[3])
    head_size = width // HEADS
    rows = seq_count * seq_len
    inputs = tokens[0].reshape(rows, width)
    lens = lengths[0]
    weight_qkv = w_qkv[0]
    weight_attn = w_attn_out[0]
    weight_in = w_ffn_in[0]
    weight_out = w_ffn_out[0]
    bias_in = b_ffn_in[0]
    vectors = biases[0]
    scales = gains[0]
    positions = lax.broadcasted_iota(jnp.int32, (seq_count, seq_len), 1)
    keep = positions < lens[:, None]
    keep_float = keep.astype(jnp.float32)
    lens_float = lens.astype(jnp.float32)[:, None]
    shape_heads = (seq_count, seq_len, HEADS, head_size)
    projected = product(inputs, weight_qkv)
    query = (projected[:, :width] + vectors[0]).astype(jnp.bfloat16)
    key_rows = projected[:, width : 2 * width].astype(jnp.bfloat16)
    value = (projected[:, 2 * width :] + vectors[1]).astype(jnp.bfloat16)
    query_heads = query.reshape(shape_heads)
    key_heads = key_rows.reshape(shape_heads)
    value_heads = value.reshape(shape_heads)
    scores = scores_of(query_heads, key_heads, keep)
    log_total = jax.nn.logsumexp(scores, axis=-1, keepdims=True)
    probs_low = jnp.exp(scores - log_total).astype(jnp.bfloat16)
    context = jnp.einsum(
        "shqk,skhe->sqhe", probs_low, value_heads, preferred_element_type=jnp.float32
    )
    context = context.reshape(rows, width).astype(jnp.bfloat16)
    attended = product(context, weight_attn) + vectors[2]
    first_norm, normed_one, inverse_one = norm_forward(
        inputs.astype(jnp.float32) + attended, scales[0], vectors[3]
    )
    first_low = first_norm.astype(jnp.bfloat16)
    hidden_pre = product(first_low, weight_in) + bias_in
    hidden = jax.nn.gelu(hidden_pre, approximate=False).astype(jnp.bfloat16)
    branch = product(hidden, weight_out) + vectors[4]
    output, normed_two, inverse_two = norm_forward(first_norm + branch, scales[1], vectors[5])
    pooled = (
        jnp.sum(output.reshape(seq_count, seq_len, width) * keep_float[:, :, None], axis=1)
        / lens_float
    )
    mine = pooled.astype(jnp.bfloat16)
    questions = from_behind(mine, "tower", 1)
    everyone, every_set = (
        lax.all_gather(mine, "batch", axis=0, tiled=True),
        lax.all_gather(datasets.astype(jnp.bfloat16), "batch", axis=0, tiled=True),
    )
    total_seqs = everyone.shape[0]
    columns = lax.broadcasted_iota(jnp.int32, (seq_count, total_seqs), 1)
    chosen = columns == positives[:, None]
    set_row = every_set.astype(jnp.float32)[None, :]
    query_set = jnp.sum(jnp.where(chosen, set_row, 0.0), axis=1, keepdims=True)
    allowed = set_row == query_set
    question_float = questions.astype(jnp.float32)
    everyone_float = everyone.astype(jnp.float32)
    logits = jnp.dot(question_float, everyone_float.T, precision=HIGH) * SCALE
    masked = jnp.where(allowed, logits, -1000000000.0)
    softmax_rows = jnp.exp(masked - jax.nn.logsumexp(masked, axis=1, keepdims=True))
    d_logits = (softmax_rows - chosen.astype(jnp.float32)) * SCALE
    d_questions = jnp.dot(d_logits, everyone_float, precision=HIGH).astype(jnp.bfloat16)
    passage_terms = jnp.dot(d_logits.T, question_float, precision=HIGH)
    d_passages = lax.psum_scatter(passage_terms, "batch", scatter_dimension=0, tiled=True)
    returned = from_behind(d_questions, "tower", -1)
    is_passage = lax.axis_index("tower") == 1
    d_pooled = jnp.where(is_passage, d_passages, returned.astype(jnp.float32))
    d_output = ((d_pooled / lens_float)[:, None, :] * keep_float[:, :, None]).reshape(rows, width)
    d_second, d_gain_two, d_shift_two = norm_backward(d_output, normed_two, inverse_two, scales[1])
    d_branch = d_second.astype(jnp.bfloat16)
    g_weight_out = transposed_left(hidden, d_branch)
    g_bias_out = jnp.sum(d_branch.astype(jnp.float32), axis=0)
    d_hidden = transposed_right(d_branch, weight_out)
    gelu_pull = jax.vjp(partial(jax.nn.gelu, approximate=False), hidden_pre)[1]
    d_pre = gelu_pull(d_hidden)[0].astype(jnp.bfloat16)
    g_weight_in = transposed_left(first_low, d_pre)
    g_bias_in = jnp.sum(d_pre.astype(jnp.float32), axis=0)
    d_first = d_second + transposed_right(d_pre, weight_in)
    d_sum_one, d_gain_one, d_shift_one = norm_backward(d_first, normed_one, inverse_one, scales[0])
    d_attended = d_sum_one.astype(jnp.bfloat16)
    g_weight_attn = transposed_left(context, d_attended)
    g_bias_attn = jnp.sum(d_attended.astype(jnp.float32), axis=0)
    d_context = transposed_right(d_attended, weight_attn).astype(jnp.bfloat16).reshape(shape_heads)
    again = scores_of(query_heads, key_heads, keep)
    probs = jnp.exp(again - log_total)
    d_value = jnp.einsum(
        "shqk,sqhe->skhe", probs.astype(jnp.bfloat16), d_context, preferred_element_type=jnp.float32
    )
    d_probs = jnp.einsum(
        "sqhe,skhe->shqk", d_context, value_heads, preferred_element_type=jnp.float32
    )
    d_scores = (probs * (d_probs - jnp.sum(d_probs * probs, axis=-1, keepdims=True))).astype(
        jnp.bfloat16
    )
    d_query = (
        jnp.einsum("shqk,skhe->sqhe", d_scores, key_heads, preferred_element_type=jnp.float32)
        * 0.125
    )
    d_key = (
        jnp.einsum("shqk,sqhe->skhe", d_scores, query_heads, preferred_element_type=jnp.float32)
        * 0.125
    )
    d_query_low = d_query.reshape(rows, width).astype(jnp.bfloat16)
    d_key_low = d_key.reshape(rows, width).astype(jnp.bfloat16)
    d_value_low = d_value.reshape(rows, width).astype(jnp.bfloat16)
    d_projected = jnp.concatenate([d_query_low, d_key_low, d_value_low], axis=1)
    g_weight_qkv = transposed_left(inputs, d_projected)
    g_bias_query = jnp.sum(d_query_low.astype(jnp.float32), axis=0)
    g_bias_value = jnp.sum(d_value_low.astype(jnp.float32), axis=0)
    d_inputs = d_sum_one + transposed_right(d_projected, weight_qkv)
    g_vectors = jnp.stack(
        [g_bias_query, g_bias_value, g_bias_attn, d_shift_one, g_bias_out, d_shift_two]
    )
    g_scales = jnp.stack([d_gain_one, d_gain_two])
    (
        summed_qkv,
        summed_attn,
        summed_in,
        summed_out,
        summed_bias_in,
        summed_vectors,
        summed_scales,
    ) = (
        lax.psum_scatter(g_weight_qkv, "batch", scatter_dimension=0, tiled=True),
        lax.psum_scatter(g_weight_attn, "batch", scatter_dimension=0, tiled=True),
        lax.psum_scatter(g_weight_in, "batch", scatter_dimension=0, tiled=True),
        lax.psum_scatter(g_weight_out, "batch", scatter_dimension=0, tiled=True),
        lax.psum_scatter(g_bias_in, "batch", scatter_dimension=0, tiled=True),
        lax.psum_scatter(g_vectors, "batch", scatter_dimension=1, tiled=True),
        lax.psum_scatter(g_scales, "batch", scatter_dimension=1, tiled=True),
    )
    return (
        pooled[None],
        d_inputs.reshape(1, seq_count, seq_len, width),
        summed_qkv[None],
        summed_attn[None],
        summed_in[None],
        summed_out[None],
        summed_bias_in[None],
        summed_vectors[None],
        summed_scales[None],
    )


def solution(mesh):
    in_specs = (
        P("tower", "batch", None, None),
        P("tower", "batch"),
        P("batch"),
        P("batch"),
        P("tower", None, None),
        P("tower", None, None),
        P("tower", None, None),
        P("tower", None, None),
        P("tower", None),
        P("tower", None, None),
        P("tower", None, None),
    )
    out_specs = (
        P("tower", "batch", None),
        P("tower", "batch", None, None),
        P("tower", "batch", None),
        P("tower", "batch", None),
        P("tower", "batch", None),
        P("tower", "batch", None),
        P("tower", "batch"),
        P("tower", None, "batch"),
        P("tower", None, "batch"),
    )
    return jax.shard_map(
        per_device, mesh=mesh, in_specs=in_specs, out_specs=out_specs, check_vma=False
    )
```

profile of v0, /device:TPU:0, one launch (start us, length us, event | category | flops | bytes accessed | tf_op | source)
XLA Modules:
  0.0 864.5 jit_solution(563446416470303097)
XLA Ops:
  12.7 5.2 fusion.17
  19.2 2.3 fusion.20
  21.5 2.8 copy.55
  24.3 3.8 reshape.244
  28.1 2.6 copy.56
  30.7 3.9 reshape.245
  34.6 2.6 copy.54
  37.2 3.9 reshape.243
  41.0 4.8 fusion.6
  46.6 4.9 exponential_reduce_fusion
  51.5 3.0 fusion.40
  60.7 35.4 %multiply_convert_fusion.1 = (bf16[1024,3072]{1,0:T(8,128)(2,1)S(1)}, f32[1024,3072]{1,0:T(8,128)}, f32[1024,3072]{1,0:T(8,128)}) fusion(f32[3072]{0:T(1024)S(1)} %bitcast.177, bf16[1,768,3072]{2,1,0:T(8,128)(2,1)S(1)} %bitcast.170, f32[1024,768]{1,0:T(8,128)S(1)} %get-tuple-element.69, f32[768]{0:T(1024)S(1)} %get-tuple-element.43, ...), kind=kOutput, calls=%fused_computation.6 | convolution fusion | flops 5043388416 | bytes 39348224 | tf_op jit(solution)/shard_map/dot_general | solution.py:23
  96.1 5.5 fusion.74
  104.0 5.4 collective-permute-start
  114.4 33.8 %all-reduce = bf16[64]{0:T(256)(128)(2,1)} all-reduce(bf16[64]{0:T(256)(128)(2,1)} %dynamic-update-slice), channel_id=1, replica_groups=mesh['tower'=2,'batch'=16] {'batch'}, use_global_device_ids=true, to_apply=%add | all-reduce | flops 64 | bytes 256
  150.8 19.1 %all-gather = bf16[16,4,768]{2,1,0:T(4,128)(2,1)} all-gather(bf16[1,4,768]{2,1,0:T(4,128)(2,1)} %fusion.95), channel_id=1, replica_groups=mesh['tower'=2,'batch'=16] {'batch'}, dimensions={0}, use_global_device_ids=true | all-gather | bytes 104448 | tf_op jit(solution)/shard_map/all_gather | solution.py:122
  180.5 2.6 collective-permute-done.1
  183.1 79.9 %all-reduce.5.cloned.1.call-done = f32[64,768]{1,0:T(8,128)} async-done(((f32[64,768]{1,0:T(8,128)}), f32[64,768]{1,0:T(8,128)}) %all-reduce.5.cloned.1.call-update) | async-done | bytes 196624
  264.0 2.0 multiply_reduce_fusion.1
  266.0 3.7 fusion.29
  269.7 3.4 convert_reduce_fusion.1
  273.1 18.9 %convert_reduce_fusion = (f32[3072]{0:T(1024)}, bf16[1024,3072]{1,0:T(8,128)(2,1)}) fusion(f32[1024,3072]{1,0:T(8,128)} %get-tuple-element.57, bf16[1024,768]{1,0:T(8,128)(2,1)} %get-tuple-element.53, bf16[1,3072,768]{2,1,0:T(8,128)(2,1)} %param.18, f32[1024,3072]{1,0:T(8,128)} %get-tuple-element.70, f32[3072]{0:T(1024)S(1)} %bitcast.178), kind=kOutput, calls=%fused_computation.2 | convolution fusion | flops 4885312512 | bytes 37773312 | tf_op jit(solution)/shard_map/dot_general | solution.py:33
  292.1 10.7 %multiply_reduce_fusion.2 = (f32[768]{0:T(1024)}, f32[1024]{0:T(1024)S(1)}, f32[1024]{0:T(1024)S(1)}, f32[768]{0:T(1024)}, f32[1024,768]{1,0:T(8,128)S(1)}) fusion(f32[1024,768]{1,0:T(8,128)S(1)} %copy-done.5, f32[1024]{0:T(1024)S(1)} %add_rsqrt_fusion.1, f32[1024]{0:T(1024)S(1)} %broadcast_multiply_fusion.4, f32[768]{0:T(1024)S(1)} %get-tuple-element.51, ...), kind=kOutput, calls=%fused_computation.54 | convolution fusion | flops 4839698432 | bytes 20472832 | tf_op jit(solution)/shard_map/dot_general | solution.py:33
  306.1 2.6 convolution_convert_fusion.2
  308.7 2.6 copy.62
  311.3 4.1 reshape.247
  315.4 9.9 %convert_reduce_fusion.3 = (f32[12,64]{1,0:T(8,128)}, bf16[4,12,64,256]{3,2,1,0:T(8,128)(2,1)}) fusion(f32[4,12,256,256]{2,3,1,0:T(8,128)} %copy-done.1, f32[4,12,256]{2,1,0:T(8,128)} %copy-done.14, pred[4,256]{1,0:T(4,128)(4,1)S(1)} %copy-done.19, bf16[4,256,12,64]{1,0,3,2:T(4,128)(2,1)} %reshape.247), kind=kOutput, calls=%fused_computation.57 | convolution fusion | flops 417594624 | bytes 15781888 | tf_op jit(solution)/shard_map/shqk,sqhe->skhe/dot_general | solution.py:161
  325.4 10.2 %multiply_reduce_fusion = (f32[4,12,256]{2,1,0:T(8,128)S(1)}, f32[4,12,256,256]{2,3,1,0:T(8,128)}) fusion(f32[4,12,256,256]{2,3,1,0:T(8,128)} %copy-done.1, f32[4,12,256]{2,1,0:T(8,128)S(1)} %copy-done.15, pred[4,256]{1,0:T(4,128)(4,1)S(1)} %copy-done.19, bf16[4,256,12,64]{1,0,3,2:T(4,128)(2,1)S(1)} %copy-done.9, bf16[4,256,12,64]{1,0,3,2:T(4,128)(2,1)S(1)} %copy-done.10), kind=kOutput, calls=%fused_computation.4 | convolution fusion | flops 418369536 | bytes 28410880 | tf_op jit(solution)/shard_map/sqhe,skhe->shqk/dot_general | solution.py:164
  335.6 8.0 multiply_convert_fusion
  343.7 3.1 fusion.41
  346.8 3.0 convert_reduce_fusion.4
  352.3 2.6 copy.67
  360.4 2.6 copy.73
  365.9 2.6 copy.70
  373.2 2.8 constant_dynamic-update-slice_fusion.1
  377.3 8.1 convolution_bitcast_fusion
  385.4 8.0 copy.80
  393.5 5.2 fusion.58
  398.8 9.9 %fusion.76 = f32[3072,768]{1,0:T(8,128)} fusion(bf16[1024,3072]{1,0:T(8,128)(2,1)} %copy-done.50, bf16[1024,768]{1,0:T(8,128)(2,1)} %get-tuple-element.53), kind=kOutput, calls=%fused_computation.146 | convolution fusion | flops 4831838208 | bytes 17301504 | tf_op jit(solution)/shard_map/dot_general | solution.py:27
  409.4 11.1 %fusion.67 = f32[768,3072]{1,0:T(8,128)} fusion(bf16[1024,3072]{1,0:T(8,128)(2,1)} %get-tuple-element.79, f32[1024,768]{1,0:T(8,128)} %copy-done.4, f32[768]{0:T(1024)S(1)} %copy-done.25, f32[768]{0:T(1024)S(1)} %get-tuple-element.51, f32[1024]{0:T(1024)S(1)} %add_rsqrt_fusion.1, f32[1024]{0:T(1024)S(1)} %broadcast_multiply_fusion.4), kind=kOutput, calls=%fused_computation.141 | convolution fusion | flops 4835770368 | bytes 18888704 | tf_op jit(solution)/shard_map/dot_general | solution.py:27
  421.8 58.5 %all-reduce.2 = f32[3072]{0:T(1024)S(1)} all-reduce(f32[3072]{0:T(1024)} %get-tuple-element.78), channel_id=7, replica_groups=mesh['tower'=2,'batch'=16] {'batch'}, use_global_device_ids=true, to_apply=%region_21.22.clone | all-reduce | flops 3072 | bytes 24576
  480.9 8.7 %fusion.36 = f32[1024,768]{1,0:T(8,128)} fusion(f32[1024,768]{1,0:T(8,128)} %copy-done.12, bf16[1024,2304]{0,1:T(8,128)(2,1)} %constant_dynamic-update-slice_fusion, bf16[1,768,2304]{2,1,0:T(8,128)(2,1)S(1)} %copy-done), kind=kOutput, calls=%fused_computation.75 | convolution fusion | flops 3624665088 | bytes 14548992 | tf_op jit(solution)/shard_map/dot_general | solution.py:33
  492.4 66.4 %reduce-scatter.19.cloned.1.call-done = f32[48,2304]{1,0:T(8,128)} async-done(((f32[768,2304]{1,0:T(8,128)}), f32[48,2304]{1,0:T(8,128)}) %reduce-scatter.19.cloned.1.call-update) | async-done | bytes 442384
  558.8 2.4 copy.81
  561.2 2.4 copy.74
  563.6 62.3 %reduce-scatter.13.cloned.1.call-done = f32[48,768]{1,0:T(8,128)} async-done(((f32[768,768]{1,0:T(8,128)}), f32[48,768]{1,0:T(8,128)}) %reduce-scatter.13.cloned.1.call-update) | async-done | bytes 147472 | tf_op jit(solution)/shard_map/reduce_scatter | solution.py:200
  625.9 114.9 %reduce-scatter.17.cloned.1.call-done = f32[192,768]{1,0:T(8,128)} async-done(((f32[3072,768]{1,0:T(8,128)}), f32[192,768]{1,0:T(8,128)}) %reduce-scatter.17.cloned.1.call-update) | async-done | bytes 589840 | tf_op jit(solution)/shard_map/reduce_scatter | solution.py:202
  740.8 116.4 %reduce-scatter.15.cloned.1.call-done = f32[48,3072]{1,0:T(8,128)} async-done(((f32[768,3072]{1,0:T(8,128)}), f32[48,3072]{1,0:T(8,128)}) %reduce-scatter.15.cloned.1.call-update) | async-done | bytes 589840 | tf_op jit(solution)/shard_map/reduce_scatter | solution.py:201
  (198 shorter events, 58.7 us)
Async XLA Ops:
  7.2 5.5 copy-start
  7.2 255.8 %all-reduce.5.cloned.1.call-start = ((), (), s32[]{:S(2)}) async-start(), calls=%async_computation.12 | async-start | bytes 393216
  11.3 40.2 %copy-start.18 = (pred[4,256]{1,0:T(4,128)(4,1)}, pred[4,256]{1,0:T(4,128)(4,1)S(1)}, u32[]{:S(2)}) copy-start(pred[4,256]{1,0:T(4,128)(4,1)S(1)} %get-tuple-element.65) | copy-start | bytes 3076
  12.7 83.4 %copy-start.24 = (f32[768]{0:T(1024)}, f32[768]{0:T(1024)S(1)}, u32[]{:S(2)}) copy-start(f32[768]{0:T(1024)S(1)} %get-tuple-element.43) | copy-start | bytes 9220
  45.9 5.6 copy-start.1
  46.6 4.9 copy-start.8
  51.5 3.1 copy-start.14
  56.2 2.8 slice-start.5
  56.3 3.0 slice-start.6
  56.3 39.7 %slice-start.3 = ((s8[4718592]{0:T(1024)(128)(4,1)}), s8[4194304]{0:T(1024)(128)(4,1)S(1)}, s32[]{:S(2)}) async-start(s8[4718592]{0:T(1024)(128)(4,1)} %bitcast.167), calls=%async_computation.16 | async-start | bytes 8388608
  58.0 38.0 %copy-start.4 = (f32[1024,768]{1,0:T(8,128)}, f32[1024,768]{1,0:T(8,128)S(1)}, u32[]{:S(2)}) copy-start(f32[1024,768]{1,0:T(8,128)S(1)} %get-tuple-element.69) | copy-start | bytes 9437188
  60.7 35.4 %copy-start.39 = (f32[768]{0:T(1024)S(1)}, f32[768]{0:T(1024)}, u32[]{:S(2)}) copy-start(f32[768]{0:T(1024)} %get-tuple-element.47) | copy-start | bytes 9220
  60.7 35.4 %slice-start.4 = ((s8[4718592]{0:T(1024)(128)(4,1)}), s8[524288]{0:T(1024)(128)(4,1)S(1)}, s32[]{:S(2)}) async-start(s8[4718592]{0:T(1024)(128)(4,1)} %bitcast.167), calls=%async_computation.17 | async-start | bytes 1048576
  96.0 5.5 copy-start.50
  101.6 8.5 copy-start.48
  102.2 7.9 copy-start.22
  103.3 6.1 copy-start.16
  104.0 67.4 %collective-permute-start = (bf16[4,768]{1,0:T(4,128)(2,1)}, bf16[4,768]{1,0:T(4,128)(2,1)}, u32[]{:S(2)}, u32[]{:S(2)}) collective-permute-start(bf16[4,768]{1,0:T(4,128)(2,1)} %divide_convert_fusion), channel_id=1, source_target_pairs={{0,16},{1,17},{2,18},{3,19},{4,20},{5,21},{6,22},{7,23},{8,24},{9,... | collective-permute-start | bytes 18440 | tf_op jit(solution)/shard_map/ppermute | solution.py:19
  175.5 314.1 %reduce-scatter.23.cloned.1.call-start = ((), (), s32[]{:S(2)}) async-start(), calls=%async_computation.11 | async-start | bytes 417792
  177.3 5.8 collective-permute-start.1
  263.0 6.7 copy-start.3
  263.0 6.7 copy-start.21
  263.0 6.7 copy-start.23
  263.0 6.7 copy-start.26
  269.7 3.4 copy-start.47
  273.1 19.0 %copy-start.5 = (f32[1024,768]{1,0:T(8,128)S(1)}, f32[1024,768]{1,0:T(8,128)}, u32[]{:S(2)}) copy-start(f32[1024,768]{1,0:T(8,128)} %copy-done.4) | copy-start | bytes 9437188
  302.7 3.3 copy-start.45
  308.7 6.7 copy-start.19
  315.4 10.0 %copy-start.9 = (bf16[4,256,12,64]{1,0,3,2:T(4,128)(2,1)S(1)}, bf16[4,256,12,64]{1,0,3,2:T(4,128)(2,1)}, u32[]{:S(2)}) copy-start(bf16[4,256,12,64]{1,0,3,2:T(4,128)(2,1)} %reshape.243) | copy-start | bytes 4718596
  315.4 10.0 %copy-start.10 = (bf16[4,256,12,64]{1,0,3,2:T(4,128)(2,1)S(1)}, bf16[4,256,12,64]{1,0,3,2:T(4,128)(2,1)}, u32[]{:S(2)}) copy-start(bf16[4,256,12,64]{1,0,3,2:T(4,128)(2,1)} %reshape.247) | copy-start | bytes 4718596
  315.4 10.0 %copy-start.15 = (f32[4,12,256]{2,1,0:T(8,128)S(1)}, f32[4,12,256]{2,1,0:T(8,128)}, u32[]{:S(2)}) copy-start(f32[4,12,256]{2,1,0:T(8,128)} %copy-done.14) | copy-start | bytes 147460
  315.4 20.2 %slice-start = ((s8[12582912]{0:T(1024)(128)(4,1)}), s8[4194304]{0:T(1024)(128)(4,1)S(1)}, s32[]{:S(2)}) async-start(s8[12582912]{0:T(1024)(128)(4,1)} %bitcast.142), calls=%async_computation.13 | async-start | bytes 8388608
  325.3 10.2 %slice-start.1 = ((s8[12582912]{0:T(1024)(128)(4,1)}), s8[4194304]{0:T(1024)(128)(4,1)S(1)}, s32[]{:S(2)}) async-start(s8[12582912]{0:T(1024)(128)(4,1)} %bitcast.142), calls=%async_computation.14 | async-start | bytes 8388608
  325.3 10.2 %slice-start.2 = ((s8[12582912]{0:T(1024)(128)(4,1)}), s8[4194304]{0:T(1024)(128)(4,1)S(1)}, s32[]{:S(2)}) async-start(s8[12582912]{0:T(1024)(128)(4,1)} %bitcast.142), calls=%async_computation.15 | async-start | bytes 8388608
  335.6 8.1 copy-start.6
  343.7 3.2 copy-start.7
  346.8 3.0 copy-start.29
  346.8 3.0 copy-start.38
  352.0 139.0 %reduce-scatter.21.cloned.1.call-start = ((), (), s32[]{:S(2)}) async-start(), calls=%async_computation.10 | async-start | bytes 417792
  355.0 2.9 copy-start.37
  355.0 3.4 copy-start.30
  365.9 4.1 copy-start.33
  373.1 185.7 %reduce-scatter.19.cloned.1.call-start = ((), (), s32[]{:S(2)}) async-start(), calls=%async_computation.9 | async-start | bytes 7520256
  373.1 2.9 copy-start.11
  373.1 4.2 copy-start.43
  393.5 232.4 %reduce-scatter.13.cloned.1.call-start = ((), (), s32[]{:S(2)}) async-start(), calls=%async_computation.6 | async-start | bytes 2506752 | tf_op jit(solution)/shard_map/reduce_scatter | solution.py:200
  398.7 342.1 %reduce-scatter.17.cloned.1.call-start = ((), (), s32[]{:S(2)}) async-start(), calls=%async_computation.8 | async-start | bytes 10027008 | tf_op jit(solution)/shard_map/reduce_scatter | solution.py:202
  408.7 448.5 %reduce-scatter.15.cloned.1.call-start = ((), (), s32[]{:S(2)}) async-start(), calls=%async_computation.7 | async-start | bytes 10027008 | tf_op jit(solution)/shard_map/reduce_scatter | solution.py:201
  (19 other events, 24.4 us)
Sparse Core Ops, SparseCore 0:
  175.6 87.3 all-reduce.4
  352.2 54.5 reduce-scatter.22
  411.2 54.5 reduce-scatter.20
  469.7 89.0 reduce-scatter.18
  563.5 62.4 reduce-scatter.12
  630.5 110.3 reduce-scatter.16
  746.1 111.0 reduce-scatter.14
where the time goes:
time: 869 us; the launch traced here: 865 us
  waiting for transfers between devices  443 us (51%)
  matrix products  162 us (19%)
  blocking collectives  111 us (13%)
  local copies, waits for them, and re-layouts  86.6 us (10%)
  other arithmetic  37.6 us (4%)
  between operations  17.3 us (2%)
    unnamed x11, waiting for transfers between devices  146 us
    reduce_scatter x1, waiting for transfers between devices, per_device(): lax.psum_scatter(g_weight_in, 'batch', scatter_dimension=0, tiled=True)  116 us
    reduce_scatter x1, waiting for transfers between devices, per_device(): lax.psum_scatter(g_weight_out, 'batch', scatter_dimension=0, tiled=True)  115 us
    unnamed x2, blocking collectives  92.3 us
    reduce_scatter x1, waiting for transfers between devices, per_device(): lax.psum_scatter(g_weight_attn, 'batch', scatter_dimension=0, tiled=True)  62.3 us
    dot_general x4, matrix products, product(): return jnp.dot(left, right, preferred_element_type=jnp.float32)  47.7 us
    dot_general x4, matrix products, transposed_right(): lax.dot_general(left, right, (((1,), (1,)), ((), ())), preferred_element_...  40.9 us
    unnamed x137, local copies, waits for them, and re-layouts  39.4 us
  transfers between devices with their start and end apart: 9, of which 6 were waited for; matrix products, arithmetic and copies ran while one was open for 11% of the time, Pallas kernels for 0%

commit v1 on v0

--- a/solution.py
+++ b/solution.py
@@ -3,20 +3,18 @@
 import jax
 import jax.numpy as jnp
 from jax import lax
+from jax.experimental import pallas as pl
+from jax.experimental.pallas import tpu as pltpu
 from jax.sharding import PartitionSpec as P
 
 HEADS = 12
-
-
 EPS = 1e-12
 SCALE = 4.0
 HIGH = lax.Precision.HIGHEST
-
-
-def from_behind(value, axis, steps):
-    count = lax.axis_size(axis)
-    leading, last = (max(0, -steps), min(count, count - steps))
-    return lax.ppermute(value, axis, [(source, source + steps) for source in range(leading, last)])
+MESH = pl.DeviceIdType.MESH
+NEG = -1000000000.0
+PIECES = 3
+CHUNK = 1536
 
 
 def product(left, right):
@@ -56,21 +54,354 @@
         jnp.einsum("sqhe,skhe->shqk", query_heads, key_heads, preferred_element_type=jnp.float32)
         * 0.125
     )
-    return jnp.where(keep[:, None, None, :], raw, -1000000000.0)
+    return jnp.where(keep[:, None, None, :], raw, NEG)
+
+
+def select(condition):
+    return jnp.where(condition, 1.0, 0.0)
+
+
+def loss_kernel(n, pooled_ref, extra_ref, out_ref, mine, everyone, send_sem, recv_sem):
+    tower, me = lax.axis_index("tower"), lax.axis_index("batch")
+    flat = tower * n + me
+    total = 2 * n
+
+    barrier = pltpu.get_barrier_semaphore()
+
+    @pl.loop(1, total)
+    def _(step):
+        other = lax.rem(flat + step, total)
+        pl.semaphore_signal(
+            barrier, inc=1, device_id=(other // n, lax.rem(other, n)), device_id_type=MESH
+        )
+
+    pooled = pooled_ref[...]
+    block = jnp.concatenate(
+        [pooled[:, 0:256], pooled[:, 256:512], pooled[:, 512:768], extra_ref[...]], axis=0
+    ).astype(jnp.bfloat16)
+    mine[...] = block
+    everyone[flat] = block
+    pl.semaphore_wait(barrier, total - 1)
+
+    def copy_to(step):
+        other = lax.rem(flat + step, total)
+        return pltpu.make_async_remote_copy(
+            src_ref=mine,
+            dst_ref=everyone.at[flat],
+            send_sem=send_sem.at[step],
+            recv_sem=recv_sem.at[step],
+            device_id=(other // n, lax.rem(other, n)),
+            device_id_type=MESH,
+        )
+
+    @pl.loop(1, total)
+    def _(step):
+        copy_to(step).start()
+
+    @pl.loop(1, total)
+    def _(step):
+        copy_to(step).wait()
+
+    seqs = 4 * n
+    packed = everyone[...]
+    questions = packed[:n].reshape(16 * n, 256)
+    passages = packed[n:].reshape(16 * n, 256)
+    rows = lax.broadcasted_iota(jnp.int32, (seqs, 16 * n), 0)
+    places = lax.broadcasted_iota(jnp.int32, (seqs, 16 * n), 1)
+    owner, lane = rows // 4, lax.rem(rows, 4)
+
+    def picked(values, row):
+        return product(select(places == owner * 16 + row).astype(jnp.bfloat16), values)
+
+    def whole(values):
+        parts = [
+            product(select(places == owner * 16 + 4 * part + lane).astype(jnp.bfloat16), values)
+            for part in range(3)
+        ]
+        return jnp.concatenate(parts, axis=1)
+
+    column_lane = lax.broadcasted_iota(jnp.int32, (seqs, 256), 1)
+    column_want = lax.rem(lax.broadcasted_iota(jnp.int32, (seqs, 256), 0), 4)
+
+    def column(row):
+        return jnp.sum(
+            jnp.where(column_lane == column_want, picked(passages, row), 0.0), axis=1, keepdims=True
+        )
+
+    question_float, passage_float = whole(questions), whole(passages)
+    question_low = question_float.astype(jnp.bfloat16)
+    passage_low = passage_float.astype(jnp.bfloat16)
+    positives, sets = column(12), column(13)
+    first = lax.broadcasted_iota(jnp.int32, (seqs, seqs), 0)
+    second = lax.broadcasted_iota(jnp.int32, (seqs, seqs), 1)
+    set_row = jnp.sum(jnp.where(first == second, sets, 0.0), axis=0, keepdims=True)
+    chosen = second == positives.astype(jnp.int32)
+    query_set = jnp.sum(jnp.where(chosen, set_row, 0.0), axis=1, keepdims=True)
+    logits = transposed_right(question_low, passage_low) * SCALE
+    masked = jnp.where(set_row == query_set, logits, NEG)
+    top = jnp.max(masked, axis=1, keepdims=True)
+    weights = jnp.exp(masked - top)
+    softmax = weights / jnp.sum(weights, axis=1, keepdims=True)
+    d_logits = (softmax - select(chosen)) * SCALE
+
+    mine_row = lax.broadcasted_iota(jnp.int32, (8, seqs), 0)
+    mine_column = lax.broadcasted_iota(jnp.int32, (8, seqs), 1)
+    own = select((mine_column == me * 4 + mine_row) & (mine_row < 4))
+
+    @pl.when(tower == 0)
+    def _():
+        terms = jnp.dot(own, d_logits, precision=HIGH, preferred_element_type=jnp.float32)
+        grad = jnp.dot(terms, passage_float, precision=HIGH, preferred_element_type=jnp.float32)
+        out_ref[...] = grad.astype(jnp.bfloat16).astype(jnp.float32)
+
+    @pl.when(tower == 1)
+    def _():
+        terms = lax.dot_general(
+            own, d_logits, (((1,), (1,)), ((), ())), precision=HIGH, preferred_element_type=jnp.float32
+        )
+        out_ref[...] = jnp.dot(terms, question_float, precision=HIGH, preferred_element_type=jnp.float32)
+
+
+def loss_gradient(pooled, positives, datasets, n):
+    extra = jnp.stack([positives.astype(jnp.float32), datasets.astype(jnp.float32)])
+    extra = jnp.pad(extra, ((0, 2), (0, 252)))
+    grad = pl.pallas_call(
+        partial(loss_kernel, n),
+        out_shape=jax.ShapeDtypeStruct((8, pooled.shape[1]), jnp.float32),
+        in_specs=[pl.BlockSpec(memory_space=pltpu.VMEM)] * 2,
+        out_specs=pl.BlockSpec(memory_space=pltpu.VMEM),
+        scratch_shapes=[
+            pltpu.VMEM((16, 256), jnp.bfloat16),
+            pltpu.VMEM((2 * n, 16, 256), jnp.bfloat16),
+            pltpu.SemaphoreType.DMA((2 * n,)),
+            pltpu.SemaphoreType.DMA((2 * n,)),
+        ],
+        compiler_params=pltpu.CompilerParams(collective_id=0, has_side_effects=True),
+        name="loss",
+    )(pooled, extra)
+    return grad[:4]
+
+
+def ring_place(chip, chips):
+    half, y = chip // 2, lax.rem(chip, 2)
+    return jnp.where(y == 0, half, chips - 1 - half)
+
+
+def ring_chip(place, chips):
+    return jnp.where(place < chips // 2, place * 2, (chips - 1 - place) * 2 + 1)
+
+
+def sum_kernel(
+    n, grads, small_ref, out_out, out_in, out_attn, out_qkv, out_small,
+    sibling_got, sending, ring_got, small_got,
+    pair_send, pair_recv, ring_send, ring_recv, small_send, small_recv,
+):
+    chips = n // 2
+    tower, me = lax.axis_index("tower"), lax.axis_index("batch")
+    chip, core = me // 2, lax.rem(me, 2)
+    place = ring_place(chip, chips)
+    sibling = (tower, me + 1 - 2 * core)
+    right = (tower, ring_chip(lax.rem(place + 1, chips), chips) * 2 + core)
+    left = (tower, ring_chip(lax.rem(place + chips - 1, chips), chips) * 2 + core)
+
+    barrier = pltpu.get_barrier_semaphore()
+
+    @pl.loop(1, n)
+    def _(step):
+        pl.semaphore_signal(
+            barrier, inc=1, device_id=(tower, lax.rem(me + step, n)), device_id_type=MESH
+        )
+
+    pl.semaphore_wait(barrier, n - 1)
+
+    def small_copy(step):
+        other = lax.rem(me + step, n)
+        return pltpu.make_async_remote_copy(
+            src_ref=small_ref.at[other], dst_ref=small_got.at[step],
+            send_sem=small_send.at[step], recv_sem=small_recv.at[step],
+            device_id=(tower, other), device_id_type=MESH,
+        )
+
+    def pair_copy(piece, step, way):
+        target = ring_chip(target_place(step, way), chips)
+        return pltpu.make_async_remote_copy(
+            src_ref=grads.at[piece, target, 1 - core, way],
+            dst_ref=sibling_got.at[piece, step, way],
+            send_sem=pair_send.at[piece, step, way], recv_sem=pair_recv.at[piece, step, way],
+            device_id=sibling, device_id_type=MESH,
+        )
+
+    def target_place(step, way):
+        return lax.rem(place + chips - 1 - step, chips) if way == 0 else lax.rem(place + 1 + step, chips)
+
+    def ring_copy(piece, step, way):
+        return pltpu.make_async_remote_copy(
+            src_ref=sending.at[piece, step, way], dst_ref=ring_got.at[piece, step, way],
+            send_sem=ring_send.at[piece, step, way], recv_sem=ring_recv.at[piece, step, way],
+            device_id=right if way == 0 else left, device_id_type=MESH,
+        )
+
+    @pl.loop(0, chips)
+    def _(step):
+        for piece in range(PIECES):
+            for way in range(2):
+                pair_copy(piece, step, way).start()
+
+    @pl.loop(1, n)
+    def _(step):
+        small_copy(step).start()
+
+    def local(piece, step, way):
+        pair_copy(piece, step, way).wait_recv()
+        target = ring_chip(target_place(step, way), chips)
+        return (
+            grads[piece, target, core, way].astype(jnp.float32)
+            + sibling_got[piece, step, way].astype(jnp.float32)
+        )
+
+    for piece in range(PIECES):
+        for way in range(2):
+            sending[piece, 0, way] = local(piece, 0, way).astype(jnp.bfloat16)
+            ring_copy(piece, 0, way).start()
+
+    @pl.loop(1, chips - 1)
+    def _(step):
+        for piece in range(PIECES):
+            for way in range(2):
+                base = local(piece, step, way)
+                ring_copy(piece, step - 1, way).wait_recv()
+                sending[piece, step, way] = (
+                    base + ring_got[piece, step - 1, way].astype(jnp.float32)
+                ).astype(jnp.bfloat16)
+                ring_copy(piece, step, way).start()
+
+    for piece in range(PIECES):
+        for way in range(2):
+            total = local(piece, chips - 1, way)
+            ring_copy(piece, chips - 2, way).wait_recv()
+            total = total + ring_got[piece, chips - 2, way].astype(jnp.float32)
+            if piece == 0:
+                for part in range(4):
+                    out_out[48 * part:48 * (part + 1), 384 * way:384 * (way + 1)] = total[
+                        :, 384 * part:384 * (part + 1)]
+            elif piece == 1:
+                out_in[:, CHUNK * way:CHUNK * (way + 1)] = total
+            else:
+                out_attn[:, 384 * way:384 * (way + 1)] = total[:, :384]
+                out_qkv[:, 1152 * way:1152 * (way + 1)] = total[:, 384:]
+
+    out_small[...] = small_ref[me]
+
+    @pl.loop(1, n)
+    def _(step):
+        small_copy(step).wait()
+        out_small[...] += small_got[step]
+
+    @pl.loop(0, chips)
+    def _(step):
+        for piece in range(PIECES):
+            for way in range(2):
+                pair_copy(piece, step, way).wait_send()
+
+    @pl.loop(0, chips - 1)
+    def _(step):
+        for piece in range(PIECES):
+            for way in range(2):
+                ring_copy(piece, step, way).wait_send()
+
+
+def summed_over_batch(packed, small, n):
+    chips = n // 2
+    block = (48, CHUNK)
+    f32 = jnp.float32
+    return pl.pallas_call(
+        partial(sum_kernel, n),
+        out_shape=[
+            jax.ShapeDtypeStruct((192, 768), f32),
+            jax.ShapeDtypeStruct((48, 3072), f32),
+            jax.ShapeDtypeStruct((48, 768), f32),
+            jax.ShapeDtypeStruct((48, 2304), f32),
+            jax.ShapeDtypeStruct((8, 128), f32),
+        ],
+        in_specs=[pl.BlockSpec(memory_space=pltpu.VMEM)] * 2,
+        out_specs=[pl.BlockSpec(memory_space=pltpu.VMEM)] * 5,
+        scratch_shapes=[
+            pltpu.VMEM((PIECES, chips, 2) + block, jnp.bfloat16),
+            pltpu.VMEM((PIECES, chips - 1, 2) + block, jnp.bfloat16),
+            pltpu.VMEM((PIECES, chips - 1, 2) + block, jnp.bfloat16),
+            pltpu.VMEM((n, 8, 128), f32),
+            pltpu.SemaphoreType.DMA((PIECES, chips, 2)),
+            pltpu.SemaphoreType.DMA((PIECES, chips, 2)),
+            pltpu.SemaphoreType.DMA((PIECES, chips - 1, 2)),
+            pltpu.SemaphoreType.DMA((PIECES, chips - 1, 2)),
+            pltpu.SemaphoreType.DMA((n,)),
+            pltpu.SemaphoreType.DMA((n,)),
+        ],
+        compiler_params=pltpu.CompilerParams(
+            collective_id=1, has_side_effects=True, vmem_limit_bytes=56 * 2**20
+        ),
+        name="gradient_sum",
+    )(packed, small)
+
+
+def packed_of(g_out, g_in, g_attn, g_qkv, n):
+    low = jnp.bfloat16
+    rows = 768 // n
+    piece_out = g_out.astype(low).reshape(n, 4, rows, 2, 384).transpose(0, 3, 2, 1, 4).reshape(n, 2, rows, CHUNK)
+    piece_in = g_in.astype(low).reshape(n, rows, 2, CHUNK).transpose(0, 2, 1, 3)
+    piece_rest = jnp.concatenate(
+        [g_attn.astype(low).reshape(n, rows, 2, 384), g_qkv.astype(low).reshape(n, rows, 2, 1152)], axis=3
+    ).transpose(0, 2, 1, 3)
+    return jnp.stack([piece_out, piece_in, piece_rest]).reshape(PIECES, n // 2, 2, 2, rows, CHUNK)
+
+
+def small_of(g_bias_in, g_vectors, g_scales, n):
+    parts = [
+        g_bias_in.reshape(n, -1),
+        g_vectors.reshape(6, n, -1).transpose(1, 0, 2).reshape(n, -1),
+        g_scales.reshape(2, n, -1).transpose(1, 0, 2).reshape(n, -1),
+    ]
+    small = jnp.concatenate(parts, axis=1)
+    return jnp.pad(small, ((0, 0), (0, 1024 - small.shape[1]))).reshape(n, 8, 128)
+
+
+def from_behind(value, axis, steps):
+    count = lax.axis_size(axis)
+    leading, last = (max(0, -steps), min(count, count - steps))
+    return lax.ppermute(value, axis, [(source, source + steps) for source in range(leading, last)])
+
+
+def loss_gradient_plain(pooled, positives, datasets):
+    seq_count = pooled.shape[0]
+    mine = pooled.astype(jnp.bfloat16)
+    questions = from_behind(mine, "tower", 1)
+    everyone, every_set = (
+        lax.all_gather(mine, "batch", axis=0, tiled=True),
+        lax.all_gather(datasets.astype(jnp.bfloat16), "batch", axis=0, tiled=True),
+    )
+    total_seqs = everyone.shape[0]
+    columns = lax.broadcasted_iota(jnp.int32, (seq_count, total_seqs), 1)
+    chosen = columns == positives[:, None]
+    set_row = every_set.astype(jnp.float32)[None, :]
+    query_set = jnp.sum(jnp.where(chosen, set_row, 0.0), axis=1, keepdims=True)
+    allowed = set_row == query_set
+    question_float = questions.astype(jnp.float32)
+    everyone_float = everyone.astype(jnp.float32)
+    logits = jnp.dot(question_float, everyone_float.T, precision=HIGH) * SCALE
+    masked = jnp.where(allowed, logits, NEG)
+    softmax_rows = jnp.exp(masked - jax.nn.logsumexp(masked, axis=1, keepdims=True))
+    d_logits = (softmax_rows - chosen.astype(jnp.float32)) * SCALE
+    d_questions = jnp.dot(d_logits, everyone_float, precision=HIGH).astype(jnp.bfloat16)
+    passage_terms = jnp.dot(d_logits.T, question_float, precision=HIGH)
+    d_passages = lax.psum_scatter(passage_terms, "batch", scatter_dimension=0, tiled=True)
+    returned = from_behind(d_questions, "tower", -1)
+    is_passage = lax.axis_index("tower") == 1
+    return jnp.where(is_passage, d_passages, returned.astype(jnp.float32))
 
 
 def per_device(
-    tokens,
-    lengths,
-    positives,
-    datasets,
-    w_qkv,
-    w_attn_out,
-    w_ffn_in,
-    w_ffn_out,
-    b_ffn_in,
-    biases,
-    gains,
+    n, direct,
+    tokens, lengths, positives, datasets, w_qkv, w_attn_out, w_ffn_in, w_ffn_out, b_ffn_in, biases, gains,
 ):
     seq_count, seq_len, width = (tokens.shape[1], tokens.shape[2], tokens.shape[3])
     head_size = width // HEADS
@@ -116,30 +447,10 @@
         jnp.sum(output.reshape(seq_count, seq_len, width) * keep_float[:, :, None], axis=1)
         / lens_float
     )
-    mine = pooled.astype(jnp.bfloat16)
-    questions = from_behind(mine, "tower", 1)
-    everyone, every_set = (
-        lax.all_gather(mine, "batch", axis=0, tiled=True),
-        lax.all_gather(datasets.astype(jnp.bfloat16), "batch", axis=0, tiled=True),
-    )
-    total_seqs = everyone.shape[0]
-    columns = lax.broadcasted_iota(jnp.int32, (seq_count, total_seqs), 1)
-    chosen = columns == positives[:, None]
-    set_row = every_set.astype(jnp.float32)[None, :]
-    query_set = jnp.sum(jnp.where(chosen, set_row, 0.0), axis=1, keepdims=True)
-    allowed = set_row == query_set
-    question_float = questions.astype(jnp.float32)
-    everyone_float = everyone.astype(jnp.float32)
-    logits = jnp.dot(question_float, everyone_float.T, precision=HIGH) * SCALE
-    masked = jnp.where(allowed, logits, -1000000000.0)
-    softmax_rows = jnp.exp(masked - jax.nn.logsumexp(masked, axis=1, keepdims=True))
-    d_logits = (softmax_rows - chosen.astype(jnp.float32)) * SCALE
-    d_questions = jnp.dot(d_logits, everyone_float, precision=HIGH).astype(jnp.bfloat16)
-    passage_terms = jnp.dot(d_logits.T, question_float, precision=HIGH)
-    d_passages = lax.psum_scatter(passage_terms, "batch", scatter_dimension=0, tiled=True)
-    returned = from_behind(d_questions, "tower", -1)
-    is_passage = lax.axis_index("tower") == 1
-    d_pooled = jnp.where(is_passage, d_passages, returned.astype(jnp.float32))
+    if direct:
+        d_pooled = loss_gradient(pooled, positives, datasets, n)
+    else:
+        d_pooled = loss_gradient_plain(pooled, positives, datasets)
     d_output = ((d_pooled / lens_float)[:, None, :] * keep_float[:, :, None]).reshape(rows, width)
     d_second, d_gain_two, d_shift_two = norm_backward(d_output, normed_two, inverse_two, scales[1])
     d_branch = d_second.astype(jnp.bfloat16)
@@ -187,23 +498,25 @@
         [g_bias_query, g_bias_value, g_bias_attn, d_shift_one, g_bias_out, d_shift_two]
     )
     g_scales = jnp.stack([d_gain_one, d_gain_two])
-    (
-        summed_qkv,
-        summed_attn,
-        summed_in,
-        summed_out,
-        summed_bias_in,
-        summed_vectors,
-        summed_scales,
-    ) = (
-        lax.psum_scatter(g_weight_qkv, "batch", scatter_dimension=0, tiled=True),
-        lax.psum_scatter(g_weight_attn, "batch", scatter_dimension=0, tiled=True),
-        lax.psum_scatter(g_weight_in, "batch", scatter_dimension=0, tiled=True),
-        lax.psum_scatter(g_weight_out, "batch", scatter_dimension=0, tiled=True),
-        lax.psum_scatter(g_bias_in, "batch", scatter_dimension=0, tiled=True),
-        lax.psum_scatter(g_vectors, "batch", scatter_dimension=1, tiled=True),
-        lax.psum_scatter(g_scales, "batch", scatter_dimension=1, tiled=True),
-    )
+    if direct:
+        packed = packed_of(g_weight_out, g_weight_in, g_weight_attn, g_weight_qkv, n)
+        small = small_of(g_bias_in, g_vectors, g_scales, n)
+        summed_out, summed_in, summed_attn, summed_qkv, small = summed_over_batch(packed, small, n)
+        small = small.reshape(1024)
+        part = width // n
+        summed_bias_in = small[: 4 * part]
+        summed_vectors = small[4 * part : 10 * part].reshape(6, part)
+        summed_scales = small[10 * part : 12 * part].reshape(2, part)
+    else:
+        def scatter(value, dimension):
+            return lax.psum_scatter(value, "batch", scatter_dimension=dimension, tiled=True)
+
+        summed_qkv, summed_attn, summed_in, summed_out = (
+            scatter(g_weight_qkv, 0), scatter(g_weight_attn, 0), scatter(g_weight_in, 0), scatter(g_weight_out, 0)
+        )
+        summed_bias_in, summed_vectors, summed_scales = (
+            scatter(g_bias_in, 0), scatter(g_vectors, 1), scatter(g_scales, 1)
+        )
     return (
         pooled[None],
         d_inputs.reshape(1, seq_count, seq_len, width),
@@ -218,6 +531,8 @@
 
 
 def solution(mesh):
+    n = mesh.shape["batch"]
+    direct = n == 16
     in_specs = (
         P("tower", "batch", None, None),
         P("tower", "batch"),
@@ -243,5 +558,5 @@
         P("tower", None, "batch"),
     )
     return jax.shard_map(
-        per_device, mesh=mesh, in_specs=in_specs, out_specs=out_specs, check_vma=False
-    )
+        partial(per_device, n, direct), mesh=mesh, in_specs=in_specs, out_specs=out_specs, check_vma=False
+    )

time: 869 us -> 445 us (0.51)
  waiting for transfers between devices: 443 us -> 0 us
  blocking collectives: 111 us -> 0 us
  Pallas kernels: 0 us -> 98.2 us
  local copies, waits for them, and re-layouts: 86.6 us -> 140 us
  matrix products: 162 us -> 143 us
  other arithmetic: 37.6 us -> 56.5 us
  between operations: 17.3 us -> 1.44 us
    reduce_scatter x3 -> x0, waiting for transfers between devices: 294 us -> none  [the longest x1 116 us: per_device(): lax.psum_scatter(g_weight_in, 'batch', scatter_dimension=0, tiled=True)]
    unnamed x11 -> x0, waiting for transfers between devices: 146 us -> none
    pallas_call x0 -> x2, Pallas kernels: none -> 98.2 us  [the longest x1 82.3 us: summed_over_batch(): pl.pallas_call(partial(sum_kernel, n), out_shape=[jax.ShapeDtypeStruct((1...]
    unnamed x2 -> x0, blocking collectives: 92.3 us -> none
    reshape x0 -> x9, local copies, waits for them, and re-layouts: none -> 49.1 us  [the longest x2 17.3 us: packed_of(): piece_in = g_in.astype(low).reshape(n, rows, 2, CHUNK).transpose(0, 2, 1, 3)]
    unnamed x137 -> x115, local copies, waits for them, and re-layouts: 39.4 us -> 20.1 us
    all_gather x1 -> x0, blocking collectives: 19.1 us -> none  [per_device(): lax.all_gather(mine, 'batch', axis=0, tiled=True)]
    another operation x1 -> x3, other arithmetic: 0.6 us -> 11.1 us  [the longest x1 10.5 us: packed_of(): jnp.stack([piece_out, piece_in, piece_rest])]
  transfers between devices with their start and end apart: 9 -> 0, of which waited for: 6 -> 0; matrix products, arithmetic and copies ran while one was open for 11% -> 0% of each run, Pallas kernels for 0% -> 0%
where the time goes in v1:
time: 445 us; the launch traced here: 439 us
  matrix products  143 us (32%)
  local copies, waits for them, and re-layouts  140 us (31%)
  Pallas kernels  98.2 us (22%)
  other arithmetic  56.5 us (13%)
    pallas_call x1, Pallas kernels, summed_over_batch(): pl.pallas_call(partial(sum_kernel, n), out_shape=[jax.ShapeDtypeStruct((1...  82.3 us
    dot_general x4, matrix products, product(): return jnp.dot(left, right, preferred_element_type=jnp.float32)  47.7 us
    dot_general x4, matrix products, transposed_right(): lax.dot_general(left, right, (((1,), (1,)), ((), ())), preferred_element_...  37.9 us
    dot_general x4, matrix products, transposed_left(): lax.dot_general(left, right, (((0,), (0,)), ((), ())), preferred_element_...  29.8 us
    unnamed x115, local copies, waits for them, and re-layouts  20.1 us
    reshape x2, local copies, waits for them, and re-layouts, packed_of(): piece_in = g_in.astype(low).reshape(n, rows, 2, CHUNK).transpose(0, 2, 1, 3)  17.3 us
    reshape x2, local copies, waits for them, and re-layouts, packed_of(): g_out.astype(low).reshape(n, 4, rows, 2, 384).transpose(0, 3, 2, 1, 4)  17 us
    pallas_call x1, Pallas kernels, loss_gradient(): pl.pallas_call(partial(loss_kernel, n), out_shape=jax.ShapeDtypeStruct((8...  15.9 us

profile of v1, /device:TPU:0, one launch (start us, length us, event | category | flops | bytes accessed | tf_op | source)
XLA Modules:
  0.0 439.0 jit_solution(7363843059871536877)
XLA Ops:
  4.9 5.2 %fusion.18 = f32[1024,2304]{1,0:T(8,128)S(1)} fusion(bf16[1024,768]{1,0:T(8,128)(2,1)} %bitcast.181, bf16[1,768,2304]{2,1,0:T(8,128)(2,1)S(1)} %copy-done), kind=kOutput, calls=%fused_computation.43 | convolution fusion | flops 3623878656 | bytes 14548992 | tf_op jit(solution)/shard_map/dot_general | solution.py:21
  10.2 2.8 fusion.21
  14.7 2.8 copy.36
  17.5 3.8 reshape.276
  21.4 3.2 slice.90
  24.6 2.6 copy.38
  27.2 3.9 reshape.278
  31.0 2.6 copy.37
  33.6 3.9 reshape.277
  37.5 4.8 %fusion.6 = (f32[4,12,256]{2,1,0:T(8,128)S(1)}, f32[4,12,256,256]{2,3,1,0:T(8,128)S(1)}) fusion(pred[4,256]{1,0:T(4,128)(4,1)S(1)} %get-tuple-element.46, bf16[4,256,12,64]{1,0,3,2:T(4,128)(2,1)} %reshape.278, bf16[4,256,12,64]{1,0,3,2:T(4,128)(2,1)} %reshape.277), kind=kOutput, calls=%fused_computation.24 | convolution fusion | flops 412078080 | bytes 15778816 | tf_op jit(solution)/shard_map/sqhe,skhe->shqk/dot_general | solution.py:54
  43.0 4.9 %exponential_reduce_fusion = f32[4,12,256]{2,1,0:T(8,128)S(1)} fusion(f32[4,12,256,256]{2,3,1,0:T(8,128)S(1)} %get-tuple-element.48, f32[4,12,256]{2,1,0:T(8,128)} %is-finite_select_fusion, pred[4,256]{1,0:T(4,128)(4,1)S(1)} %get-tuple-element.46), kind=kLoop, calls=%fused_computation.21 | loop fusion | flops 12570624 | bytes 12682240 | tf_op jit(solution)/shard_map/reduce_sum | solution.py:431
  48.0 3.0 fusion.41
  55.2 35.3 %multiply_convert_fusion.1 = (bf16[1024,3072]{1,0:T(8,128)(2,1)S(1)}, f32[1024,3072]{1,0:T(8,128)}, f32[1024,3072]{1,0:T(8,128)}) fusion(f32[3072]{0:T(1024)S(1)} %bitcast.184, bf16[1,768,3072]{2,1,0:T(8,128)(2,1)S(1)} %bitcast.180, f32[1024,768]{1,0:T(8,128)S(1)} %get-tuple-element.50, f32[768]{0:T(1024)S(1)} %copy-done.31, f32[768]{0:T(1024)S(1)} %copy-done.22, ...), kind=kOutput, calls=%fused_computation.7 | convolution fusion | flops 5043388416 | bytes 39348224 | tf_op jit(solution)/shard_map/dot_general | solution.py:21
  90.6 5.5 %fusion.70 = (f32[1024]{0:T(1024)S(1)}, f32[1024,768]{1,0:T(8,128)S(1)}) fusion(f32[768]{0:T(1024)S(1)} %copy-done.33, bf16[1024,3072]{1,0:T(8,128)(2,1)S(1)} %get-tuple-element.39, bf16[1,3072,768]{2,1,0:T(8,128)(2,1)S(1)} %bitcast.178, f32[768]{0:T(1024)S(1)} %copy-done.31, f32[768]{0:T(1024)S(1)} %copy-done.22, f32[1024]{0:T(1024)S(1)} %add_rsqrt_fusion.1, ...), kind=kOutput, calls=%fused_computation.146 | convolution fusion | flops 4837342208 | bytes 17323008 | tf_op jit(solution)/shard_map/dot_general | solution.py:21
  101.2 15.9 %loss.1 = f32[8,768]{1,0:T(8,128)} custom-call(f32[4,768]{1,0:T(4,128)} %broadcast_divide_fusion.pooled_ref, f32[4,256]{1,0:T(4,128)} %select_maximum_fusion.2.extra_ref), custom_call_target="tpu_custom_call" | custom-call | tf_op jit(solution)/shard_map/loss/pallas_call | solution.py:168
  118.1 4.1 fusion.30
  122.2 2.0 multiply_reduce_fusion.1
  124.2 4.2 convert_reduce_fusion.1
  128.4 19.0 %convert_reduce_fusion = (f32[3072]{0:T(1024)}, bf16[1024,3072]{1,0:T(8,128)(2,1)}) fusion(f32[1024,3072]{1,0:T(8,128)} %get-tuple-element.40, bf16[1024,768]{1,0:T(8,128)(2,1)} %get-tuple-element.36, bf16[1,3072,768]{2,1,0:T(8,128)(2,1)} %param.18, f32[1024,3072]{1,0:T(8,128)} %get-tuple-element.51, f32[3072]{0:T(1024)S(1)} %bitcast.185), kind=kOutput, calls=%fused_computation.3 | convolution fusion | flops 4885312512 | bytes 37773312 | tf_op jit(solution)/shard_map/dot_general | solution.py:31
  147.4 10.7 %multiply_reduce_fusion.2 = (f32[768]{0:T(1024)}, f32[1024]{0:T(1024)S(1)}, f32[1024]{0:T(1024)S(1)}, f32[768]{0:T(1024)}, f32[1024,768]{1,0:T(8,128)S(1)}) fusion(f32[1024,768]{1,0:T(8,128)S(1)} %copy-done.7, f32[1024]{0:T(1024)S(1)} %copy-done.26, f32[1024]{0:T(1024)S(1)} %broadcast_multiply_fusion.4, f32[768]{0:T(1024)S(1)} %copy-done.23, ...), kind=kOutput, calls=%fused_computation.60 | convolution fusion | flops 4839698432 | bytes 20472832 | tf_op jit(solution)/shard_map/dot_general | solution.py:31
  161.4 2.6 convolution_convert_fusion.5
  164.1 2.6 copy.44
  166.7 3.9 reshape.280
  170.5 11.4 %multiply_reduce_fusion = (f32[4,12,256]{2,1,0:T(8,128)S(1)}, f32[4,12,256,256]{2,3,1,0:T(8,128)S(1)}) fusion(f32[4,12,256,256]{2,3,1,0:T(8,128)} %copy-done.1, f32[4,12,256]{2,1,0:T(8,128)} %copy-done.16, pred[4,256]{1,0:T(4,128)(4,1)S(1)} %copy-done.20, bf16[4,256,12,64]{1,0,3,2:T(4,128)(2,1)} %reshape.276, bf16[4,256,12,64]{1,0,3,2:T(4,128)(2,1)} %reshape.280), kind=kOutput, calls=%fused_computation.5 | convolution fusion | flops 418369536 | bytes 28410880 | tf_op jit(solution)/shard_map/sqhe,skhe->shqk/dot_general | solution.py:475
  181.9 8.1 %multiply_convert_fusion = bf16[4,12,256,256]{2,3,1,0:T(8,128)(2,1)S(1)} fusion(f32[4,12,256,256]{2,3,1,0:T(8,128)S(1)} %get-tuple-element.56, f32[4,12,256,256]{2,3,1,0:T(8,128)} %copy-done.1, f32[4,12,256]{2,1,0:T(8,128)S(1)} %get-tuple-element.55, f32[4,12,256]{2,1,0:T(8,128)S(1)} %copy-done.17, pred[4,256]{1,0:T(4,128)(4,1)S(1)} %copy-done.20), kind=kLoop, calls=%fused_computation.4 | loop fusion | flops 18874368 | bytes 31556608 | tf_op jit(solution)/shard_map/convert_element_type | solution.py:478
  190.0 1.9 convert_reduce_fusion.4
  194.8 2.0 fusion.42
  200.6 4.0 convert_reduce_fusion.3
  208.2 5.6 %fusion.37 = f32[1024,768]{1,0:T(8,128)} fusion(f32[1024,768]{1,0:T(8,128)S(1)} %copy-done.13, bf16[1024,2304]{0,1:T(8,128)(2,1)S(1)} %constant_dynamic-update-slice_fusion, bf16[1,768,2304]{2,1,0:T(8,128)(2,1)S(1)} %copy-done), kind=kOutput, calls=%fused_computation.81 | convolution fusion | flops 3624665088 | bytes 14548992 | tf_op jit(solution)/shard_map/dot_general | solution.py:31
  213.9 5.3 %fusion.15 = bf16[768,2304]{0,1:T(8,128)(2,1)} fusion(bf16[1024,2304]{0,1:T(8,128)(2,1)S(1)} %constant_dynamic-update-slice_fusion, bf16[1024,768]{1,0:T(8,128)(2,1)S(1)} %bitcast.183), kind=kOutput, calls=%fused_computation.40 | convolution fusion | flops 3625648128 | bytes 9830400 | tf_op jit(solution)/shard_map/dot_general | solution.py:25
  219.1 5.8 %copy.58 = bf16[768,2304]{1,0:T(8,128)(2,1)} copy(bf16[768,2304]{0,1:T(8,128)(2,1)} %fusion.15) | data formatting | bytes 7077888 | tf_op jit(solution)/shard_map/convert_element_type | solution.py:353
  224.9 7.8 %reshape.285 = bf16[16,48,2,1152]{3,2,1,0:T(2,128)(2,1)} reshape(bf16[768,2304]{1,0:T(8,128)(2,1)} %copy.58) | data formatting | bytes 7077888 | tf_op jit(solution)/shard_map/reshape | solution.py:353
  232.8 4.8 %convolution_convert_fusion.6 = bf16[768,768]{1,0:T(8,128)(2,1)} fusion(bf16[1024,768]{0,1:T(8,128)(2,1)} %bitcast.161, f32[1024,768]{1,0:T(8,128)} %copy-done.12), kind=kOutput, calls=%fused_computation.86 | convolution fusion | flops 1209335808 | bytes 5898240 | tf_op jit(solution)/shard_map/dot_general | solution.py:25
  237.6 3.9 reshape.284
  241.5 9.7 %maximum_bitcast_fusion = bf16[16,2,48,1536]{3,1,2,0:T(2,128)(2,1)} fusion(bf16[16,48,2,1152]{3,2,1,0:T(2,128)(2,1)} %reshape.285, bf16[16,48,2,384]{3,2,1,0:T(2,128)(2,1)} %reshape.284), kind=kLoop, calls=%fused_computation.29 | loop fusion | flops 9437184 | bytes 9437184 | tf_op jit(solution)/shard_map/transpose | solution.py:354
  251.2 5.7 %copy.59 = bf16[16,2,48,1536]{3,2,1,0:T(8,128)(2,1)} copy(bf16[16,2,48,1536]{3,1,2,0:T(2,128)(2,1)} %maximum_bitcast_fusion) | data formatting | bytes 9437184 | tf_op jit(solution)/shard_map/transpose | solution.py:354
  256.9 9.8 %convolution_convert_fusion = bf16[768,3072]{1,0:T(8,128)(2,1)} fusion(bf16[1024,3072]{1,0:T(8,128)(2,1)} %get-tuple-element.62, f32[1024,768]{1,0:T(8,128)S(1)} %copy-done.8, f32[768]{0:T(1024)S(1)} %copy-done.32, f32[768]{0:T(1024)S(1)} %copy-done.23, f32[1024]{0:T(1024)S(1)} %copy-done.26, f32[1024]{0:T(1024)S(1)} %broadcast_multiply_fusion.4), kind=kOutput, calls=%fused_computation.26 | convolution fusion | flops 4838129664 | bytes 14170112 | tf_op jit(solution)/shard_map/dot_general | solution.py:25
  266.7 11.7 %reshape.283 = bf16[16,48,2,1536]{3,2,1,0:T(2,128)(2,1)} reshape(bf16[768,3072]{1,0:T(8,128)(2,1)} %convolution_convert_fusion) | data formatting | bytes 9437184 | tf_op jit(solution)/shard_map/reshape | solution.py:351
  278.4 5.6 %copy.57 = bf16[16,48,2,1536]{3,1,2,0:T(8,128)(2,1)} copy(bf16[16,48,2,1536]{3,2,1,0:T(2,128)(2,1)} %reshape.283) | data formatting | bytes 9437184 | tf_op jit(solution)/shard_map/reshape | solution.py:351
  284.0 9.9 %convolution_convert_fusion.1 = bf16[3072,768]{1,0:T(8,128)(2,1)} fusion(bf16[1024,3072]{1,0:T(8,128)(2,1)} %copy-done.43, bf16[1024,768]{1,0:T(8,128)(2,1)S(1)} %copy-done.15), kind=kOutput, calls=%fused_computation.27 | convolution fusion | flops 4834197504 | bytes 12582912 | tf_op jit(solution)/shard_map/dot_general | solution.py:25
  293.9 10.1 %reshape.282 = bf16[16,4,48,2,384]{4,3,2,1,0:T(2,128)(2,1)} reshape(bf16[3072,768]{1,0:T(8,128)(2,1)} %convolution_convert_fusion.1) | data formatting | bytes 9437184 | tf_op jit(solution)/shard_map/reshape | solution.py:350
  304.1 6.9 %copy.100 = bf16[16,4,48,2,384]{4,1,2,3,0:T(4,128)(2,1)} copy(bf16[16,4,48,2,384]{4,3,2,1,0:T(2,128)(2,1)} %reshape.282) | data formatting | bytes 9437184 | tf_op jit(solution)/shard_map/reshape | solution.py:350
  311.0 8.8 %stack.53 = bf16[1,8,2,2,48,1536]{5,4,3,2,1,0:T(8,128)(2,1)} reshape(bf16[16,2,48,4,384]{4,3,2,1,0:T(4,128)(2,1)} %bitcast.151) | data formatting | bytes 9437184 | tf_op jit(solution)/shard_map/stack | solution.py:355
  319.8 10.5 %pad_maximum_fusion.grads = bf16[3,8,2,2,48,1536]{5,4,3,2,1,0:T(8,128)(2,1)} fusion(bf16[1,8,2,2,48,1536]{5,4,3,2,1,0:T(8,128)(2,1)} %bitcast.149, bf16[1,8,2,2,48,1536]{5,4,3,2,1,0:T(8,128)(2,1)} %bitcast.150, bf16[1,8,2,2,48,1536]{5,4,3,2,1,0:T(8,128)(2,1)} %stack.53), kind=kLoop, calls=%fused_computation.1 | loop fusion | flops 14155776 | bytes 28311552 | tf_op jit(solution)/shard_map/stack | solution.py:355
  345.3 82.3 %gradient_sum.1 = (f32[192,768]{1,0:T(8,128)}, f32[48,3072]{1,0:T(8,128)}, f32[48,768]{1,0:T(8,128)}, f32[48,2304]{1,0:T(8,128)}, f32[8,128]{1,0:T(8,128)}) custom-call(bf16[3,8,2,2,48,1536]{5,4,3,2,1,0:T(8,128)(2,1)} %pad_maximum_fusion.grads, f32[16,8,128]{2,1,0:T(8,128)} %bitcast.166), custom_call_target="tpu_custom_call" | custom-call | tf_op jit(solution)/shard_map/gradient_sum/pallas_call | solution.py:317
  431.6 1.8 copy.107
  435.0 1.9 copy.109
  436.9 1.9 copy.110
  (163 shorter events, 51.1 us)
Async XLA Ops:
  0.6 4.3 copy-start
  2.1 45.8 %copy-start.19 = (pred[4,256]{1,0:T(4,128)(4,1)}, pred[4,256]{1,0:T(4,128)(4,1)S(1)}, u32[]{:S(2)}) copy-start(pred[4,256]{1,0:T(4,128)(4,1)S(1)} %get-tuple-element.46) | copy-start | bytes 3076
  10.2 4.6 %copy-start.11 = (f32[1024,2304]{1,0:T(8,128)}, f32[1024,2304]{1,0:T(8,128)S(1)}, u32[]{:S(2)}) copy-start(f32[1024,2304]{1,0:T(8,128)S(1)} %fusion.18) | copy-start | bytes 28311556
  42.3 5.6 %copy-start.1 = (f32[4,12,256,256]{2,3,1,0:T(8,128)}, f32[4,12,256,256]{2,3,1,0:T(8,128)S(1)}, u32[]{:S(2)}) copy-start(f32[4,12,256,256]{2,3,1,0:T(8,128)S(1)} %get-tuple-element.48) | copy-start | bytes 37748740
  43.0 4.9 %copy-start.9 = (bf16[4,256,12,64]{1,0,3,2:T(4,128)(2,1)S(1)}, bf16[4,256,12,64]{1,0,3,2:T(4,128)(2,1)}, u32[]{:S(2)}) copy-start(bf16[4,256,12,64]{1,0,3,2:T(4,128)(2,1)} %reshape.276) | copy-start | bytes 4718596
  48.0 3.1 copy-start.16
  51.0 1.7 copy-start.39
  52.3 2.9 slice-start.5
  52.7 1.8 copy-start.14
  52.8 2.4 copy-start.22
  52.8 2.4 copy-start.31
  52.8 2.4 slice-start.6
  52.8 2.4 copy-start.41
  52.8 37.7 %slice-start.3 = ((s8[4718592]{0:T(1024)(128)(4,1)}), s8[4194304]{0:T(1024)(128)(4,1)S(1)}, s32[]{:S(2)}) async-start(s8[4718592]{0:T(1024)(128)(4,1)} %bitcast.177), calls=%async_computation.3 | async-start | bytes 8388608
  54.5 36.0 %copy-start.6 = (f32[1024,768]{1,0:T(8,128)}, f32[1024,768]{1,0:T(8,128)S(1)}, u32[]{:S(2)}) copy-start(f32[1024,768]{1,0:T(8,128)S(1)} %get-tuple-element.50) | copy-start | bytes 9437188
  55.2 35.3 %copy-start.25 = (f32[1024]{0:T(1024)}, f32[1024]{0:T(1024)S(1)}, u32[]{:S(2)}) copy-start(f32[1024]{0:T(1024)S(1)} %add_rsqrt_fusion.1) | copy-start | bytes 12292
  55.2 35.3 %copy-start.33 = (f32[768]{0:T(1024)S(1)}, f32[768]{0:T(1024)}, u32[]{:S(2)}) copy-start(f32[768]{0:T(1024)} %get-tuple-element.30) | copy-start | bytes 9220
  55.2 35.3 %slice-start.4 = ((s8[4718592]{0:T(1024)(128)(4,1)}), s8[524288]{0:T(1024)(128)(4,1)S(1)}, s32[]{:S(2)}) async-start(s8[4718592]{0:T(1024)(128)(4,1)} %bitcast.177), calls=%async_computation.4 | async-start | bytes 1048576
  90.5 5.5 %copy-start.43 = (bf16[1024,3072]{1,0:T(8,128)(2,1)}, bf16[1024,3072]{1,0:T(8,128)(2,1)S(1)}, u32[]{:S(2)}) copy-start(bf16[1024,3072]{1,0:T(8,128)(2,1)S(1)} %get-tuple-element.39) | copy-start | bytes 18874372
  90.6 7.2 %copy-start.21 = (f32[4,256]{1,0:T(4,128)S(1)}, f32[4,256]{1,0:T(4,128)}, u32[]{:S(2)}) copy-start(f32[4,256]{1,0:T(4,128)} %get-tuple-element.45) | copy-start | bytes 12292
  90.6 7.2 %copy-start.27 = (f32[768]{0:T(1024)S(1)}, f32[768]{0:T(1024)}, u32[]{:S(2)}) copy-start(f32[768]{0:T(1024)} %get-tuple-element.25) | copy-start | bytes 9220
  96.1 2.5 copy-start.34
  96.1 3.2 copy-start.28
  96.1 4.5 %copy-start.35 = (s32[4]{0:T(128)S(1)}, s32[4]{0:T(128)}, u32[]{:S(2)}) copy-start(s32[4]{0:T(128)} %param.14) | copy-start | bytes 52
  96.1 4.5 %copy-start.36 = (s32[4]{0:T(128)S(1)}, s32[4]{0:T(128)}, u32[]{:S(2)}) copy-start(s32[4]{0:T(128)} %param.13) | copy-start | bytes 52
  98.6 2.0 copy-start.29
  117.2 7.1 %copy-start.3 = (f32[1024,768]{1,0:T(8,128)S(1)}, f32[1024,768]{1,0:T(8,128)}, u32[]{:S(2)}) copy-start(f32[1024,768]{1,0:T(8,128)} %copy-done.2) | copy-start | bytes 9437188
  124.2 4.2 copy-start.42
  128.4 19.0 %copy-start.7 = (f32[1024,768]{1,0:T(8,128)S(1)}, f32[1024,768]{1,0:T(8,128)}, u32[]{:S(2)}) copy-start(f32[1024,768]{1,0:T(8,128)} %copy-done.6) | copy-start | bytes 9437188
  128.4 19.0 %copy-start.23 = (f32[768]{0:T(1024)S(1)}, f32[768]{0:T(1024)}, u32[]{:S(2)}) copy-start(f32[768]{0:T(1024)} %get-tuple-element.34) | copy-start | bytes 9220
  128.4 19.0 %copy-start.26 = (f32[1024]{0:T(1024)S(1)}, f32[1024]{0:T(1024)}, u32[]{:S(2)}) copy-start(f32[1024]{0:T(1024)} %copy-done.25) | copy-start | bytes 12292
  158.1 3.3 copy-start.40
  164.1 6.5 %copy-start.20 = (pred[4,256]{1,0:T(4,128)(4,1)S(1)}, pred[4,256]{1,0:T(4,128)(4,1)}, u32[]{:S(2)}) copy-start(pred[4,256]{1,0:T(4,128)(4,1)} %copy-done.19) | copy-start | bytes 3076
  170.5 11.4 %copy-start.17 = (f32[4,12,256]{2,1,0:T(8,128)S(1)}, f32[4,12,256]{2,1,0:T(8,128)}, u32[]{:S(2)}) copy-start(f32[4,12,256]{2,1,0:T(8,128)} %copy-done.16) | copy-start | bytes 147460
  181.9 8.1 %copy-start.5 = (bf16[4,256,12,64]{1,0,3,2:T(4,128)(2,1)S(1)}, bf16[4,256,12,64]{1,0,3,2:T(4,128)(2,1)}, u32[]{:S(2)}) copy-start(bf16[4,256,12,64]{1,0,3,2:T(4,128)(2,1)} %reshape.278) | copy-start | bytes 4718596
  193.1 1.7 copy-start.4
  194.8 4.9 %slice-start = ((s8[12582912]{0:T(1024)(128)(4,1)}), s8[4194304]{0:T(1024)(128)(4,1)S(1)}, s32[]{:S(2)}) async-start(s8[12582912]{0:T(1024)(128)(4,1)} %bitcast.147), calls=%async_computation | async-start | bytes 8388608
  194.8 4.9 %slice-start.1 = ((s8[12582912]{0:T(1024)(128)(4,1)}), s8[4194304]{0:T(1024)(128)(4,1)S(1)}, s32[]{:S(2)}) async-start(s8[12582912]{0:T(1024)(128)(4,1)} %bitcast.147), calls=%async_computation.1 | async-start | bytes 8388608
  196.8 2.9 slice-start.2
  198.1 2.6 copy-start.10
  204.7 2.3 copy-start.18
  205.9 2.3 copy-start.13
  208.2 5.6 %copy-start.38 = (bf16[1,4,256,768]{3,2,1,0:T(8,128)(2,1)S(1)}, bf16[1,4,256,768]{3,2,1,0:T(8,128)(2,1)}, u32[]{:S(2)}) copy-start(bf16[1,4,256,768]{3,2,1,0:T(8,128)(2,1)} %param.11) | copy-start | bytes 4718596
  251.2 5.7 %copy-start.8 = (f32[1024,768]{1,0:T(8,128)S(1)}, f32[1024,768]{1,0:T(8,128)}, u32[]{:S(2)}) copy-start(f32[1024,768]{1,0:T(8,128)} %copy-done.6) | copy-start | bytes 9437188
  251.2 5.7 %copy-start.32 = (f32[768]{0:T(1024)S(1)}, f32[768]{0:T(1024)}, u32[]{:S(2)}) copy-start(f32[768]{0:T(1024)} %get-tuple-element.26) | copy-start | bytes 9220
  278.4 5.6 %copy-start.15 = (bf16[1024,768]{1,0:T(8,128)(2,1)S(1)}, bf16[1024,768]{1,0:T(8,128)(2,1)}, u32[]{:S(2)}) copy-start(bf16[1024,768]{1,0:T(8,128)(2,1)} %get-tuple-element.36) | copy-start | bytes 4718596
  319.7 10.5 %copy-start.24 = (f32[768]{0:T(1024)S(1)}, f32[768]{0:T(1024)}, u32[]{:S(2)}) copy-start(f32[768]{0:T(1024)} %get-tuple-element.21) | copy-start | bytes 9220
  319.8 11.2 %copy-start.30 = (f32[768]{0:T(1024)S(1)}, f32[768]{0:T(1024)}, u32[]{:S(2)}) copy-start(f32[768]{0:T(1024)} %get-tuple-element.19) | copy-start | bytes 9220
  (3 other events, 4.9 us)

commit v2 on v1

--- a/solution.py
+++ b/solution.py
@@ -13,8 +13,11 @@
 HIGH = lax.Precision.HIGHEST
 MESH = pl.DeviceIdType.MESH
 NEG = -1000000000.0
-PIECES = 3
+LOW = jnp.bfloat16
+F32 = jnp.float32
 CHUNK = 1536
+SUBS = 3
+MIB = 2**20
 
 
 def product(left, right):
@@ -179,7 +182,212 @@
         compiler_params=pltpu.CompilerParams(collective_id=0, has_side_effects=True),
         name="loss",
     )(pooled, extra)
-    return grad[:4]
+    return grad
+
+
+def gelu_parts(z):
+    t = 1.0 / (1.0 + jnp.abs(z) * (0.3275911 * 0.7071067811865476))
+    bell = jnp.exp(z * z * -0.5)
+    tail = t * bell * (
+        0.127414796 + t * (-0.142248368 + t * (0.7107068705 + t * (-0.7265760135 + t * 0.5307027145)))
+    )
+    below = jnp.where(z < 0.0, tail, 1.0 - tail)
+    return z * below, below + z * bell * 0.3989422804014327
+
+
+def normed(total):
+    mean = jnp.mean(total, axis=-1, keepdims=True)
+    centered = total - mean
+    inverse = lax.rsqrt(jnp.mean(centered * centered, axis=-1, keepdims=True) + EPS)
+    return centered * inverse, inverse
+
+
+def encoder_kernel(
+    lens, x_ref, wqkv_hbm, wattn_hbm, win_hbm, wout_hbm, bin_ref, vec_ref, gain_ref,
+    pooled_ref, query_ref, key_t_ref, value_ref, probs_ref, context_t_ref, low_t_ref, x_t_ref,
+    n1_ref, n2_ref, inv_ref, hidden_ref, slope_ref,
+    wqkv, wattn, win, wout, sems,
+):
+    step = pl.program_id(0)
+    loads = [
+        pltpu.make_async_copy(source.at[0], target, sems.at[place])
+        for place, (source, target) in enumerate(
+            [(wqkv_hbm, wqkv), (wattn_hbm, wattn), (win_hbm, win), (wout_hbm, wout)]
+        )
+    ]
+
+    @pl.when(step == 0)
+    def _():
+        for load in loads:
+            load.start()
+        loads[0].wait()
+
+    length = lens[step]
+    x = x_ref[...]
+    rows = x.shape[0]
+    query = (product(x, wqkv[:, :768]) + vec_ref[0, 0:1]).astype(LOW) * 0.125
+    key = product(x, wqkv[:, 768:1536]).astype(LOW)
+    value = (product(x, wqkv[:, 1536:]) + vec_ref[0, 1:2]).astype(LOW)
+    query_ref[...] = query
+    value_ref[...] = value
+    key_t_ref[...] = key.T
+    x_t_ref[...] = x.T
+    value_t = value.T
+    blocked = jnp.where(lax.broadcasted_iota(jnp.int32, (rows, 1), 0) < length, 0.0, NEG)
+    lane = lax.broadcasted_iota(jnp.int32, (rows, 128), 1)
+    for head in range(HEADS):
+        pair = slice(128 * (head // 2), 128 * (head // 2 + 1))
+        mine = (lane < 64) if head % 2 == 0 else (lane >= 64)
+        key_one = jnp.where(mine, key[:, pair], jnp.zeros((), LOW))
+        scores = transposed_right(key_one, query[:, pair]) + blocked
+        weights = jnp.exp(scores - jnp.max(scores, axis=0, keepdims=True))
+        probs = (weights * (1.0 / jnp.sum(weights, axis=0, keepdims=True))).astype(LOW)
+        probs_ref[0, head] = probs
+        context_t_ref[64 * head:64 * (head + 1), :] = product(
+            value_t[64 * head:64 * (head + 1)], probs
+        ).astype(LOW)
+
+    @pl.when(step == 0)
+    def _():
+        loads[1].wait()
+
+    attended = transposed_left(context_t_ref[...], wattn[...]) + vec_ref[0, 2:3]
+    n1, inv1 = normed(x.astype(F32) + attended)
+    first = n1 * gain_ref[0, 0:1] + vec_ref[0, 3:4]
+    first_low = first.astype(LOW)
+    low_t_ref[...] = first_low.T
+    n1_ref[...] = n1.astype(LOW)
+
+    @pl.when(step == 0)
+    def _():
+        loads[2].wait()
+        loads[3].wait()
+
+    total = first + vec_ref[0, 4:5]
+    for part in range(4):
+        columns = slice(768 * part, 768 * (part + 1))
+        hidden, slope = gelu_parts(product(first_low, win[:, columns]) + bin_ref[:, columns])
+        hidden = hidden.astype(LOW)
+        hidden_ref[:, columns] = hidden
+        slope_ref[:, columns] = slope.astype(LOW)
+        total = total + product(hidden, wout[columns, :])
+    n2, inv2 = normed(total)
+    n2_ref[...] = n2.astype(LOW)
+    inv_ref[...] = jnp.where(lane < 64, inv1, inv2)
+    output = n2 * gain_ref[0, 1:2] + vec_ref[0, 5:6]
+    keep = lax.broadcasted_iota(jnp.int32, (rows, 1), 0) < length
+    pooled_ref[0] = jnp.sum(jnp.where(keep, output, 0.0), axis=0, keepdims=True) / length.astype(F32)
+
+
+def encoder(lens, x, w_qkv, w_attn, w_in, w_out, b_in, vectors, gains):
+    seqs = lens.shape[0]
+    rows = x.shape[0]
+    per = rows // seqs
+
+    def by_rows(width):
+        return pl.BlockSpec((per, width), lambda s, *_: (s, 0))
+
+    def by_columns(height):
+        return pl.BlockSpec((height, per), lambda s, *_: (0, s))
+
+    def full(*shape):
+        return pl.BlockSpec(shape, lambda s, *_: (0,) * len(shape))
+
+    anywhere = pl.BlockSpec(memory_space=pl.ANY)
+    wide = lambda width, kind=LOW: jax.ShapeDtypeStruct((rows, width), kind)
+    tall = jax.ShapeDtypeStruct((768, rows), LOW)
+    return pl.pallas_call(
+        encoder_kernel,
+        grid_spec=pltpu.PrefetchScalarGridSpec(
+            num_scalar_prefetch=1,
+            grid=(seqs,),
+            in_specs=[by_rows(768)] + [anywhere] * 4 + [full(1, 3072), full(1, 6, 768), full(1, 2, 768)],
+            out_specs=[
+                pl.BlockSpec((1, 1, 768), lambda s, *_: (s, 0, 0)),
+                by_rows(768), by_columns(768), by_rows(768),
+                pl.BlockSpec((1, HEADS, per, per), lambda s, *_: (s, 0, 0, 0)),
+                by_columns(768), by_columns(768), by_columns(768),
+                by_rows(768), by_rows(768), by_rows(128), by_rows(3072), by_rows(3072),
+            ],
+            scratch_shapes=[
+                pltpu.VMEM((768, 2304), LOW), pltpu.VMEM((768, 768), LOW),
+                pltpu.VMEM((768, 3072), LOW), pltpu.VMEM((3072, 768), LOW),
+                pltpu.SemaphoreType.DMA((4,)),
+            ],
+        ),
+        out_shape=[
+            jax.ShapeDtypeStruct((seqs, 1, 768), F32),
+            wide(768), tall, wide(768),
+            jax.ShapeDtypeStruct((seqs, HEADS, per, per), LOW),
+            tall, tall, tall, wide(768), wide(768), wide(128, F32), wide(3072), wide(3072),
+        ],
+        compiler_params=pltpu.CompilerParams(vmem_limit_bytes=56 * MIB),
+        name="encoder",
+    )(lens, x, w_qkv, w_attn, w_in, w_out, b_in, vectors, gains)
+
+
+def second_norm_backward(grad_row, length, first_row, n2, inv2, gain):
+    scaled = grad_row * gain
+    mean = jnp.mean(scaled, axis=1, keepdims=True)
+    along = jnp.mean(scaled * n2, axis=1, keepdims=True)
+    keep = first_row + lax.broadcasted_iota(jnp.int32, (n2.shape[0], 1), 0) < length
+    return jnp.where(keep, inv2 * (scaled - mean - n2 * along), 0.0), keep
+
+
+def out_kernel(lens, dpool_ref, n2_ref, inv_ref, gain_ref, hidden_ref, packed_ref, small_ref, d_branch):
+    step = pl.program_id(0)
+
+    @pl.when(step == 0)
+    def _():
+        small_ref[...] = jnp.zeros_like(small_ref)
+        for seq in range(4):
+            rows = slice(256 * seq, 256 * (seq + 1))
+            length = lens[seq]
+            grad_row = dpool_ref[seq:seq + 1] / length.astype(F32)
+            n2 = n2_ref[rows].astype(F32)
+            d_second, keep = second_norm_backward(
+                grad_row, length, 0, n2, inv_ref[rows, 64:65], gain_ref[0, 1:2]
+            )
+            low = d_second.astype(LOW)
+            d_branch[rows] = low
+            small_ref[0:1] += jnp.sum(low.astype(F32), axis=0, keepdims=True)
+            small_ref[1:2] += dpool_ref[seq:seq + 1]
+            small_ref[2:3] += grad_row * jnp.sum(jnp.where(keep, n2, 0.0), axis=0, keepdims=True)
+
+    grad = transposed_left(hidden_ref[...], d_branch[...]).astype(LOW)
+    for core in range(2):
+        for way in range(2):
+            for part in range(4):
+                top = 192 * core + 48 * part
+                packed_ref[0, core, way, :, 384 * part:384 * (part + 1)] = grad[
+                    top:top + 48, 384 * way:384 * (way + 1)]
+
+
+def out_gradient(lens, dpool, n2, inv, gains, hidden, n):
+    chips = n // 2
+    rows = n2.shape[0]
+
+    def full(*shape):
+        return pl.BlockSpec(shape, lambda c, *_: (0,) * len(shape))
+
+    return pl.pallas_call(
+        out_kernel,
+        grid_spec=pltpu.PrefetchScalarGridSpec(
+            num_scalar_prefetch=1,
+            grid=(chips,),
+            in_specs=[
+                full(8, 768), full(rows, 768), full(rows, 128), full(1, 2, 768),
+                pl.BlockSpec((rows, 384), lambda c, *_: (0, c)),
+            ],
+            out_specs=[pl.BlockSpec((1, 2, 2, 48, CHUNK), lambda c, *_: (c, 0, 0, 0, 0)), full(8, 768)],
+            scratch_shapes=[pltpu.VMEM((rows, 768), LOW)],
+        ),
+        out_shape=[
+            jax.ShapeDtypeStruct((chips, 2, 2, 48, CHUNK), LOW), jax.ShapeDtypeStruct((8, 768), F32),
+        ],
+        compiler_params=pltpu.CompilerParams(vmem_limit_bytes=48 * MIB),
+        name="out_gradient",
+    )(lens, dpool, n2, inv, gains, hidden)
 
 
 def ring_place(chip, chips):
@@ -191,19 +399,398 @@
     return jnp.where(place < chips // 2, place * 2, (chips - 1 - place) * 2 + 1)
 
 
-def sum_kernel(
-    n, grads, small_ref, out_out, out_in, out_attn, out_qkv, out_small,
-    sibling_got, sending, ring_got, small_got,
-    pair_send, pair_recv, ring_send, ring_recv, small_send, small_recv,
+def ring_scratch(n):
+    chips = n // 2
+    block = (48, CHUNK)
+    return [
+        pltpu.VMEM((chips, 2) + block, LOW),
+        pltpu.VMEM((chips, 2) + block, LOW),
+        pltpu.VMEM((chips - 1, 2) + block, LOW),
+        pltpu.VMEM((chips - 1, 2) + block, LOW),
+        pltpu.SemaphoreType.DMA((chips, 2)),
+        pltpu.SemaphoreType.DMA((chips, 2)),
+        pltpu.SemaphoreType.DMA((chips, 2)),
+        pltpu.SemaphoreType.DMA((chips - 1, SUBS, 2)),
+        pltpu.SemaphoreType.DMA((chips - 1, SUBS, 2)),
+    ]
+
+
+class Ring:
+    def __init__(self, n, packed, scratch, finish):
+        self.n, self.chips, self.packed, self.finish = n, n // 2, packed, finish
+        (self.own, self.paired, self.sending, self.got, self.own_sem, self.pair_send, self.pair_recv,
+         self.ring_send, self.ring_recv) = scratch
+        self.tower, self.me = lax.axis_index("tower"), lax.axis_index("batch")
+        chips = self.chips
+        self.core = lax.rem(self.me, 2)
+        self.place = ring_place(self.me // 2, chips)
+        self.sibling = (self.tower, self.me + 1 - 2 * self.core)
+        self.next = [
+            (self.tower, ring_chip(lax.rem(self.place + 1, chips), chips) * 2 + self.core),
+            (self.tower, ring_chip(lax.rem(self.place + chips - 1, chips), chips) * 2 + self.core),
+        ]
+        self.turns = chips * SUBS
+
+    def target(self, step, way):
+        if way == 0:
+            return ring_chip(lax.rem(self.place + self.chips - 1 - step + self.chips, self.chips), self.chips)
+        return ring_chip(lax.rem(self.place + 1 + step, self.chips), self.chips)
+
+    def own_copy(self, step, way):
+        return pltpu.make_async_copy(
+            self.packed.at[self.target(step, way), self.core, way], self.own.at[step, way], self.own_sem.at[step, way]
+        )
+
+    def pair_copy(self, step, way):
+        return pltpu.make_async_remote_copy(
+            src_ref=self.packed.at[self.target(step, way), 1 - self.core, way],
+            dst_ref=self.paired.at[step, way],
+            send_sem=self.pair_send.at[step, way], recv_sem=self.pair_recv.at[step, way],
+            device_id=self.sibling, device_id_type=MESH,
+        )
+
+    def ring_copy(self, step, sub, way):
+        rows = pl.ds(pl.multiple_of(sub * 16, 16), 16)
+        return pltpu.make_async_remote_copy(
+            src_ref=self.sending.at[step, way, rows], dst_ref=self.got.at[step, way, rows],
+            send_sem=self.ring_send.at[step, sub, way], recv_sem=self.ring_recv.at[step, sub, way],
+            device_id=self.next[way], device_id_type=MESH,
+        )
+
+    def greet(self):
+        barrier = pltpu.get_barrier_semaphore()
+        for device in [self.sibling] + self.next:
+            pl.semaphore_signal(barrier, inc=1, device_id=device, device_id_type=MESH)
+
+    def greeted(self):
+        pl.semaphore_wait(pltpu.get_barrier_semaphore(), 3)
+
+    def load(self):
+        @pl.loop(0, self.chips)
+        def _(step):
+            for way in range(2):
+                self.own_copy(step, way).start()
+
+    def swap(self):
+        @pl.loop(0, self.chips)
+        def _(step):
+            for way in range(2):
+                self.pair_copy(step, way).start()
+
+    def turn(self, index):
+        step, sub = index // SUBS, lax.rem(index, SUBS)
+        rows = pl.ds(pl.multiple_of(sub * 16, 16), 16)
+        last = self.chips - 1
+
+        @pl.when(sub == 0)
+        def _():
+            for way in range(2):
+                self.own_copy(step, way).wait()
+                self.pair_copy(step, way).wait_recv()
+
+        def local(way):
+            return self.own[step, way, rows].astype(F32) + self.paired[step, way, rows].astype(F32)
+
+        @pl.when(step == 0)
+        def _():
+            for way in range(2):
+                self.sending[step, way, rows] = local(way).astype(LOW)
+                self.ring_copy(step, sub, way).start()
+
+        @pl.when((step > 0) & (step < last))
+        def _():
+            for way in range(2):
+                before = lax.max(step - 1, 0)
+                self.ring_copy(before, sub, way).wait_recv()
+                self.sending[step, way, rows] = (
+                    local(way) + self.got[before, way, rows].astype(F32)
+                ).astype(LOW)
+                self.ring_copy(step, sub, way).start()
+
+        @pl.when(step == last)
+        def _():
+            for way in range(2):
+                self.ring_copy(last - 1, sub, way).wait_recv()
+                self.finish(sub, way, local(way) + self.got[last - 1, way, rows].astype(F32))
+
+    def close(self):
+        @pl.loop(0, self.chips)
+        def _(step):
+            for way in range(2):
+                self.pair_copy(step, way).wait_send()
+
+        @pl.loop(0, self.chips - 1)
+        def _(step):
+            for sub in range(SUBS):
+                for way in range(2):
+                    self.ring_copy(step, sub, way).wait_send()
+
+
+def at(sub, base=0):
+    return pl.ds(pl.multiple_of(base + sub * 16, 16), 16)
+
+
+def ffn_kernel(
+    n, packed, lens, dpool_ref, win_hbm, wout_hbm, n1_hbm, n2_hbm, inv_hbm, slope_hbm, low_t_hbm, gain_ref,
+    summed_ref, packed_out, d_sum_out, small_ref, bias_in_ref,
+    *scratch,
 ):
-    chips = n // 2
+    ring_parts, (win, wout, n1, n2, inv, pre, low_t, d_sum, grads, sems, out_sems) = scratch[:9], scratch[9:]
+
+    def finish(sub, way, total):
+        for part in range(4):
+            summed_ref[at(sub, 48 * part), 384 * way:384 * (way + 1)] = total[:, 384 * part:384 * (part + 1)]
+
+    ring = Ring(n, packed, ring_parts, finish)
+    ring.greet()
+    weights = [
+        pltpu.make_async_copy(wout_hbm.at[0], wout, sems.at[0, 0]),
+        pltpu.make_async_copy(win_hbm.at[0], win, sems.at[0, 1]),
+    ]
+
+    def loads(seq):
+        rows = pl.ds(pl.multiple_of(seq * 256, 256), 256)
+        return [
+            pltpu.make_async_copy(source.at[rows], target.at[rows], sems.at[seq + 1, place])
+            for place, (source, target) in enumerate(
+                [(n2_hbm, n2), (inv_hbm, inv), (slope_hbm, pre), (n1_hbm, n1)]
+            )
+        ]
+
+    low_load = pltpu.make_async_copy(low_t_hbm, low_t, sems.at[0, 2])
+    weights[0].start()
+    for copy in loads(0):
+        copy.start()
+    weights[1].start()
+    ring.load()
+    ring.greeted()
+    ring.swap()
+    for seq in range(1, 4):
+        for copy in loads(seq):
+            copy.start()
+    low_load.start()
+
+    small_ref[...] = jnp.zeros_like(small_ref)
+    bias_in_ref[...] = jnp.zeros_like(bias_in_ref)
+    weights[0].wait()
+    weights[1].wait()
+
+    @pl.loop(0, 4)
+    def _(seq):
+        rows = pl.ds(pl.multiple_of(seq * 256, 256), 256)
+        for copy in loads(seq):
+            copy.wait()
+        length = lens[seq]
+        d_second, _ = second_norm_backward(
+            dpool_ref[pl.ds(seq, 1)] / length.astype(F32), length, 0, n2[rows].astype(F32), inv[rows, 64:65],
+            gain_ref[0, 1:2],
+        )
+        d_branch = d_second.astype(LOW)
+        d_first = d_second
+        for part in range(4):
+            ring.turn(seq * 4 + part)
+            columns = slice(768 * part, 768 * (part + 1))
+            d_pre = (
+                transposed_right(d_branch, wout[columns, :]) * pre[rows, columns].astype(F32)
+            ).astype(LOW)
+            pre[rows, columns] = d_pre
+            bias_in_ref[:, columns] += jnp.sum(d_pre.astype(F32), axis=0, keepdims=True)
+            d_first = d_first + transposed_right(d_pre, win[:, columns])
+        normal = n1[rows].astype(F32)
+        scaled = d_first * gain_ref[0, 0:1]
+        mean = jnp.mean(scaled, axis=1, keepdims=True)
+        along = jnp.mean(scaled * normal, axis=1, keepdims=True)
+        d_sum_one = inv[rows, 0:1] * (scaled - mean - normal * along)
+        d_sum[rows] = d_sum_one
+        pltpu.make_async_copy(d_sum.at[rows], d_sum_out.at[rows], out_sems.at[seq]).start()
+        small_ref[0:1] += jnp.sum(d_sum_one.astype(LOW).astype(F32), axis=0, keepdims=True)
+        small_ref[1:2] += jnp.sum(d_first, axis=0, keepdims=True)
+        small_ref[2:3] += jnp.sum(d_first * normal, axis=0, keepdims=True)
+
+    low_load.wait()
+
+    @pl.loop(0, 8)
+    def _(part):
+        ring.turn(16 + part)
+        columns = pl.ds(pl.multiple_of(part * 384, 384), 384)
+        grad = product(low_t[...], pre[:, columns]).astype(LOW)
+        place = pl.ds(pl.multiple_of(lax.rem(part, 4) * 384, 384), 384)
+        grads[:, :, part // 4, :, place] = grad.reshape(n // 2, 2, 48, 384)
+
+    done = pltpu.make_async_copy(grads, packed_out, out_sems.at[4])
+    done.start()
+    for seq in range(4):
+        rows = pl.ds(seq * 256, 256)
+        pltpu.make_async_copy(d_sum.at[rows], d_sum_out.at[rows], out_sems.at[seq]).wait()
+    done.wait()
+    ring.close()
+
+
+def ffn_backward(packed, lens, dpool, w_in, w_out, n1, n2, inv, slope, low_t, gains, n):
+    rows = n1.shape[0]
+    anywhere = pl.BlockSpec(memory_space=pl.ANY)
+    vmem = pl.BlockSpec(memory_space=pltpu.VMEM)
+    return pl.pallas_call(
+        partial(ffn_kernel, n),
+        in_specs=[anywhere, pl.BlockSpec(memory_space=pltpu.SMEM), vmem] + [anywhere] * 7 + [vmem],
+        out_specs=[vmem, anywhere, anywhere, vmem, vmem],
+        out_shape=[
+            jax.ShapeDtypeStruct((192, 768), F32), jax.ShapeDtypeStruct(packed.shape, LOW),
+            jax.ShapeDtypeStruct((rows, 768), F32), jax.ShapeDtypeStruct((8, 768), F32),
+            jax.ShapeDtypeStruct((1, 3072), F32),
+        ],
+        scratch_shapes=ring_scratch(n) + [
+            pltpu.VMEM((768, 3072), LOW), pltpu.VMEM((3072, 768), LOW),
+            pltpu.VMEM((rows, 768), LOW), pltpu.VMEM((rows, 768), LOW), pltpu.VMEM((rows, 128), F32),
+            pltpu.VMEM((rows, 3072), LOW), pltpu.VMEM((768, rows), LOW), pltpu.VMEM((rows, 768), F32),
+            pltpu.VMEM(packed.shape, LOW),
+            pltpu.SemaphoreType.DMA((5, 4)), pltpu.SemaphoreType.DMA((5,)),
+        ],
+        compiler_params=pltpu.CompilerParams(collective_id=1, has_side_effects=True, vmem_limit_bytes=56 * MIB),
+        name="ffn_backward",
+    )(packed, lens, dpool, w_in, w_out, n1, n2, inv, slope, low_t, gains)
+
+
+def attention_kernel(
+    n, packed, wattn_hbm, d_sum_hbm, query_hbm, key_t_hbm, value_hbm, probs_hbm, context_t_hbm, x_t_hbm,
+    summed_ref, packed_out, d_proj_out, small_ref,
+    *scratch,
+):
+    ring_parts, (wattn, d_sum, query, key_t, value, probs, context_t, x_t, d_low, d_proj, grads, sems, out_sems) = (
+        scratch[:9], scratch[9:]
+    )
+
+    def finish(sub, way, total):
+        summed_ref[at(sub), CHUNK * way:CHUNK * (way + 1)] = total
+
+    ring = Ring(n, packed, ring_parts, finish)
+    ring.greet()
+    wattn_load = pltpu.make_async_copy(wattn_hbm.at[0], wattn, sems.at[4, 0])
+    x_load = pltpu.make_async_copy(x_t_hbm, x_t, sems.at[4, 1])
+
+    def loads(seq):
+        rows = pl.ds(pl.multiple_of(seq * 256, 256), 256)
+        return [
+            pltpu.make_async_copy(source.at[rows], target.at[rows], sems.at[seq, place])
+            for place, (source, target) in enumerate([(d_sum_hbm, d_sum), (query_hbm, query), (value_hbm, value)])
+        ] + [
+            pltpu.make_async_copy(source.at[:, rows], target.at[:, rows], sems.at[seq, 3 + place])
+            for place, (source, target) in enumerate([(key_t_hbm, key_t), (context_t_hbm, context_t)])
+        ] + [pltpu.make_async_copy(probs_hbm.at[seq], probs.at[seq], sems.at[seq, 5])]
+
+    wattn_load.start()
+    for copy in loads(0):
+        copy.start()
+    ring.load()
+    ring.greeted()
+    ring.swap()
+    for seq in range(1, 4):
+        for copy in loads(seq):
+            copy.start()
+    x_load.start()
+    small_ref[...] = jnp.zeros_like(small_ref)
+    wattn_load.wait()
+    lane = lax.broadcasted_iota(jnp.int32, (256, 128), 1)
+    none = jnp.zeros((), LOW)
+
+    @pl.loop(0, 4)
+    def _(seq):
+        rows = pl.ds(pl.multiple_of(seq * 256, 256), 256)
+        for copy in loads(seq):
+            copy.wait()
+        d_attended = d_sum[rows].astype(LOW)
+        d_low[rows] = d_attended
+        d_context = transposed_right(d_attended, wattn[...]).astype(LOW)
+        d_context_t = transposed_right(wattn[...], d_attended).astype(LOW)
+        for pair in range(6):
+            if pair < 4:
+                ring.turn(seq * 4 + pair)
+            lanes = slice(128 * pair, 128 * (pair + 1))
+            key_pair, query_pair, value_pair = key_t[lanes, rows], query[rows, lanes], value[rows, lanes]
+            d_context_pair, d_context_t_pair = d_context[:, lanes], d_context_t[lanes]
+            weighed = d_context_t_pair.astype(F32) * context_t[lanes, rows].astype(F32)
+            d_queries, d_keys, d_values = [], [], []
+            for one in range(2):
+                half = slice(64 * one, 64 * (one + 1))
+                prob = probs[seq, 2 * pair + one]
+                value_one = jnp.where((lane < 64) if one == 0 else (lane >= 64), value_pair, none)
+                d_prob = product(value_one, d_context_t_pair)
+                row_sum = jnp.sum(weighed[half], axis=0, keepdims=True)
+                d_score = (prob.astype(F32) * (d_prob - row_sum)).astype(LOW)
+                d_values.append(product(prob, d_context_pair))
+                d_keys.append(product(d_score, query_pair))
+                d_queries.append(product(key_pair[half], d_score))
+            d_query = (jnp.concatenate(d_queries, axis=0).T * 0.125).astype(LOW)
+            d_key = jnp.where(lane < 64, d_keys[0], d_keys[1]).astype(LOW)
+            d_value = jnp.where(lane < 64, d_values[0], d_values[1]).astype(LOW)
+            d_proj[rows, 128 * pair:128 * (pair + 1)] = d_query
+            d_proj[rows, 768 + 128 * pair:768 + 128 * (pair + 1)] = d_key
+            d_proj[rows, 1536 + 128 * pair:1536 + 128 * (pair + 1)] = d_value
+            small_ref[0:1, lanes] += jnp.sum(d_query.astype(F32), axis=0, keepdims=True)
+            small_ref[1:2, lanes] += jnp.sum(d_value.astype(F32), axis=0, keepdims=True)
+        pltpu.make_async_copy(d_proj.at[rows], d_proj_out.at[rows], out_sems.at[seq]).start()
+
+    x_load.wait()
+    for way in range(2):
+        ring.turn(16 + way)
+        grad = product(context_t[...], d_low[:, 384 * way:384 * (way + 1)]).astype(LOW)
+        grads[:, :, way, :, 0:384] = grad.reshape(n // 2, 2, 48, 384)
+
+    @pl.loop(0, 6)
+    def _(part):
+        ring.turn(18 + part)
+        grad = product(x_t[...], d_proj[:, pl.ds(pl.multiple_of(part * 384, 384), 384)]).astype(LOW)
+        place = pl.ds(pl.multiple_of(384 + lax.rem(part, 3) * 384, 384), 384)
+        grads[:, :, part // 3, :, place] = grad.reshape(n // 2, 2, 48, 384)
+
+    done = pltpu.make_async_copy(grads, packed_out, out_sems.at[4])
+    done.start()
+    for seq in range(4):
+        rows = pl.ds(seq * 256, 256)
+        pltpu.make_async_copy(d_proj.at[rows], d_proj_out.at[rows], out_sems.at[seq]).wait()
+    done.wait()
+    ring.close()
+
+
+def attention_backward(packed, w_attn, d_sum, query, key_t, value, probs, context_t, x_t, n):
+    rows = query.shape[0]
+    anywhere = pl.BlockSpec(memory_space=pl.ANY)
+    vmem = pl.BlockSpec(memory_space=pltpu.VMEM)
+    wide, tall = pltpu.VMEM((rows, 768), LOW), pltpu.VMEM((768, rows), LOW)
+    return pl.pallas_call(
+        partial(attention_kernel, n),
+        in_specs=[anywhere] * 9,
+        out_specs=[vmem, anywhere, anywhere, vmem],
+        out_shape=[
+            jax.ShapeDtypeStruct((48, 3072), F32), jax.ShapeDtypeStruct(packed.shape, LOW),
+            jax.ShapeDtypeStruct((rows, 2304), LOW), jax.ShapeDtypeStruct((8, 768), F32),
+        ],
+        scratch_shapes=ring_scratch(n) + [
+            pltpu.VMEM((768, 768), LOW), pltpu.VMEM((rows, 768), F32), wide, tall, wide,
+            pltpu.VMEM(probs.shape, LOW), tall, tall, wide, pltpu.VMEM((rows, 2304), LOW),
+            pltpu.VMEM(packed.shape, LOW),
+            pltpu.SemaphoreType.DMA((5, 6)), pltpu.SemaphoreType.DMA((5,)),
+        ],
+        compiler_params=pltpu.CompilerParams(collective_id=2, has_side_effects=True, vmem_limit_bytes=58 * MIB),
+        name="attention_backward",
+    )(packed, w_attn, d_sum, query, key_t, value, probs, context_t, x_t)
+
+
+def tokens_kernel(
+    n, packed, wqkv_hbm, d_sum_hbm, d_proj_hbm, out_small_ref, ffn_small_ref, bias_in_ref, attn_small_ref,
+    attn_ref, qkv_ref, summed_small_ref, grad_out,
+    *scratch,
+):
+    ring_parts, (wqkv, d_sum, d_proj, small, small_got, sems, out_sems, small_send, small_recv) = (
+        scratch[:9], scratch[9:]
+    )
     tower, me = lax.axis_index("tower"), lax.axis_index("batch")
-    chip, core = me // 2, lax.rem(me, 2)
-    place = ring_place(chip, chips)
-    sibling = (tower, me + 1 - 2 * core)
-    right = (tower, ring_chip(lax.rem(place + 1, chips), chips) * 2 + core)
-    left = (tower, ring_chip(lax.rem(place + chips - 1, chips), chips) * 2 + core)
-
+
+    def finish(sub, way, total):
+        attn_ref[at(sub), 384 * way:384 * (way + 1)] = total[:, :384]
+        qkv_ref[at(sub), 1152 * way:1152 * (way + 1)] = total[:, 384:]
+
+    ring = Ring(n, packed, ring_parts, finish)
     barrier = pltpu.get_barrier_semaphore()
 
     @pl.loop(1, n)
@@ -212,157 +799,137 @@
             barrier, inc=1, device_id=(tower, lax.rem(me + step, n)), device_id_type=MESH
         )
 
+    wqkv_load = pltpu.make_async_copy(wqkv_hbm.at[0], wqkv, sems.at[4, 0])
+
+    def loads(seq):
+        rows = pl.ds(pl.multiple_of(seq * 256, 256), 256)
+        return [
+            pltpu.make_async_copy(source.at[rows], target.at[rows], sems.at[seq, place])
+            for place, (source, target) in enumerate([(d_sum_hbm, d_sum), (d_proj_hbm, d_proj)])
+        ]
+
+    ring.load()
+    wqkv_load.start()
+    for seq in range(4):
+        for copy in loads(seq):
+            copy.start()
+    rows_of = [
+        attn_small_ref[0:1], attn_small_ref[1:2], ffn_small_ref[0:1], ffn_small_ref[1:2],
+        out_small_ref[0:1], out_small_ref[1:2], ffn_small_ref[2:3], out_small_ref[2:3],
+    ]
+    bundle = jnp.concatenate(rows_of, axis=0)
+    bias_in = bias_in_ref[...]
+    small[...] = jnp.zeros_like(small)
+    for device in range(n):
+        small[device, 0:8, 0:48] = bundle[:, 48 * device:48 * (device + 1)]
+        for part in range(4):
+            start = 192 * device + 48 * part
+            small[device, 8 + part:9 + part, 0:48] = bias_in[:, start:start + 48]
     pl.semaphore_wait(barrier, n - 1)
+    ring.swap()
 
     def small_copy(step):
         other = lax.rem(me + step, n)
         return pltpu.make_async_remote_copy(
-            src_ref=small_ref.at[other], dst_ref=small_got.at[step],
+            src_ref=small.at[other], dst_ref=small_got.at[step],
             send_sem=small_send.at[step], recv_sem=small_recv.at[step],
             device_id=(tower, other), device_id_type=MESH,
         )
 
-    def pair_copy(piece, step, way):
-        target = ring_chip(target_place(step, way), chips)
-        return pltpu.make_async_remote_copy(
-            src_ref=grads.at[piece, target, 1 - core, way],
-            dst_ref=sibling_got.at[piece, step, way],
-            send_sem=pair_send.at[piece, step, way], recv_sem=pair_recv.at[piece, step, way],
-            device_id=sibling, device_id_type=MESH,
-        )
-
-    def target_place(step, way):
-        return lax.rem(place + chips - 1 - step, chips) if way == 0 else lax.rem(place + 1 + step, chips)
-
-    def ring_copy(piece, step, way):
-        return pltpu.make_async_remote_copy(
-            src_ref=sending.at[piece, step, way], dst_ref=ring_got.at[piece, step, way],
-            send_sem=ring_send.at[piece, step, way], recv_sem=ring_recv.at[piece, step, way],
-            device_id=right if way == 0 else left, device_id_type=MESH,
-        )
-
-    @pl.loop(0, chips)
-    def _(step):
-        for piece in range(PIECES):
-            for way in range(2):
-                pair_copy(piece, step, way).start()
+    for turn in range(SUBS):
+        ring.turn(turn)
 
     @pl.loop(1, n)
     def _(step):
         small_copy(step).start()
 
-    def local(piece, step, way):
-        pair_copy(piece, step, way).wait_recv()
-        target = ring_chip(target_place(step, way), chips)
-        return (
-            grads[piece, target, core, way].astype(jnp.float32)
-            + sibling_got[piece, step, way].astype(jnp.float32)
-        )
-
-    for piece in range(PIECES):
-        for way in range(2):
-            sending[piece, 0, way] = local(piece, 0, way).astype(jnp.bfloat16)
-            ring_copy(piece, 0, way).start()
-
-    @pl.loop(1, chips - 1)
-    def _(step):
-        for piece in range(PIECES):
-            for way in range(2):
-                base = local(piece, step, way)
-                ring_copy(piece, step - 1, way).wait_recv()
-                sending[piece, step, way] = (
-                    base + ring_got[piece, step - 1, way].astype(jnp.float32)
-                ).astype(jnp.bfloat16)
-                ring_copy(piece, step, way).start()
-
-    for piece in range(PIECES):
-        for way in range(2):
-            total = local(piece, chips - 1, way)
-            ring_copy(piece, chips - 2, way).wait_recv()
-            total = total + ring_got[piece, chips - 2, way].astype(jnp.float32)
-            if piece == 0:
-                for part in range(4):
-                    out_out[48 * part:48 * (part + 1), 384 * way:384 * (way + 1)] = total[
-                        :, 384 * part:384 * (part + 1)]
-            elif piece == 1:
-                out_in[:, CHUNK * way:CHUNK * (way + 1)] = total
-            else:
-                out_attn[:, 384 * way:384 * (way + 1)] = total[:, :384]
-                out_qkv[:, 1152 * way:1152 * (way + 1)] = total[:, 384:]
-
-    out_small[...] = small_ref[me]
+    wqkv_load.wait()
+
+    @pl.loop(0, 4)
+    def _(seq):
+        rows = pl.ds(pl.multiple_of(seq * 256, 256), 256)
+        for copy in loads(seq):
+            copy.wait()
+        for part in range(3):
+            ring.turn(SUBS + seq * 3 + part)
+            columns = slice(256 * part, 256 * (part + 1))
+            d_sum[rows, columns] += transposed_right(d_proj[rows], wqkv[columns, :])
+        pltpu.make_async_copy(d_sum.at[rows], grad_out.at[rows], out_sems.at[seq]).start()
+
+    summed_small_ref[...] = small[me]
 
     @pl.loop(1, n)
     def _(step):
         small_copy(step).wait()
-        out_small[...] += small_got[step]
-
-    @pl.loop(0, chips)
-    def _(step):
-        for piece in range(PIECES):
-            for way in range(2):
-                pair_copy(piece, step, way).wait_send()
-
-    @pl.loop(0, chips - 1)
-    def _(step):
-        for piece in range(PIECES):
-            for way in range(2):
-                ring_copy(piece, step, way).wait_send()
-
-
-def summed_over_batch(packed, small, n):
-    chips = n // 2
-    block = (48, CHUNK)
-    f32 = jnp.float32
+        summed_small_ref[...] += small_got[step]
+
+    @pl.loop(SUBS + 12, ring.turns)
+    def _(turn):
+        ring.turn(turn)
+
+    for seq in range(4):
+        rows = pl.ds(seq * 256, 256)
+        pltpu.make_async_copy(d_sum.at[rows], grad_out.at[rows], out_sems.at[seq]).wait()
+    ring.close()
+
+
+def tokens_gradient(packed, w_qkv, d_sum, d_proj, out_small, ffn_small, bias_in, attn_small, n):
+    rows = d_sum.shape[0]
+    anywhere = pl.BlockSpec(memory_space=pl.ANY)
+    vmem = pl.BlockSpec(memory_space=pltpu.VMEM)
     return pl.pallas_call(
-        partial(sum_kernel, n),
+        partial(tokens_kernel, n),
+        in_specs=[anywhere] * 4 + [vmem] * 4,
+        out_specs=[vmem, vmem, vmem, anywhere],
         out_shape=[
-            jax.ShapeDtypeStruct((192, 768), f32),
-            jax.ShapeDtypeStruct((48, 3072), f32),
-            jax.ShapeDtypeStruct((48, 768), f32),
-            jax.ShapeDtypeStruct((48, 2304), f32),
-            jax.ShapeDtypeStruct((8, 128), f32),
+            jax.ShapeDtypeStruct((48, 768), F32), jax.ShapeDtypeStruct((48, 2304), F32),
+            jax.ShapeDtypeStruct((16, 128), F32), jax.ShapeDtypeStruct((rows, 768), F32),
         ],
-        in_specs=[pl.BlockSpec(memory_space=pltpu.VMEM)] * 2,
-        out_specs=[pl.BlockSpec(memory_space=pltpu.VMEM)] * 5,
-        scratch_shapes=[
-            pltpu.VMEM((PIECES, chips, 2) + block, jnp.bfloat16),
-            pltpu.VMEM((PIECES, chips - 1, 2) + block, jnp.bfloat16),
-            pltpu.VMEM((PIECES, chips - 1, 2) + block, jnp.bfloat16),
-            pltpu.VMEM((n, 8, 128), f32),
-            pltpu.SemaphoreType.DMA((PIECES, chips, 2)),
-            pltpu.SemaphoreType.DMA((PIECES, chips, 2)),
-            pltpu.SemaphoreType.DMA((PIECES, chips - 1, 2)),
-            pltpu.SemaphoreType.DMA((PIECES, chips - 1, 2)),
-            pltpu.SemaphoreType.DMA((n,)),
-            pltpu.SemaphoreType.DMA((n,)),
+        scratch_shapes=ring_scratch(n) + [
+            pltpu.VMEM((768, 2304), LOW), pltpu.VMEM((rows, 768), F32), pltpu.VMEM((rows, 2304), LOW),
+            pltpu.VMEM((n, 16, 128), F32), pltpu.VMEM((n, 16, 128), F32),
+            pltpu.SemaphoreType.DMA((5, 2)), pltpu.SemaphoreType.DMA((4,)),
+            pltpu.SemaphoreType.DMA((n,)), pltpu.SemaphoreType.DMA((n,)),
         ],
-        compiler_params=pltpu.CompilerParams(
-            collective_id=1, has_side_effects=True, vmem_limit_bytes=56 * 2**20
-        ),
-        name="gradient_sum",
-    )(packed, small)
-
-
-def packed_of(g_out, g_in, g_attn, g_qkv, n):
-    low = jnp.bfloat16
-    rows = 768 // n
-    piece_out = g_out.astype(low).reshape(n, 4, rows, 2, 384).transpose(0, 3, 2, 1, 4).reshape(n, 2, rows, CHUNK)
-    piece_in = g_in.astype(low).reshape(n, rows, 2, CHUNK).transpose(0, 2, 1, 3)
-    piece_rest = jnp.concatenate(
-        [g_attn.astype(low).reshape(n, rows, 2, 384), g_qkv.astype(low).reshape(n, rows, 2, 1152)], axis=3
-    ).transpose(0, 2, 1, 3)
-    return jnp.stack([piece_out, piece_in, piece_rest]).reshape(PIECES, n // 2, 2, 2, rows, CHUNK)
-
-
-def small_of(g_bias_in, g_vectors, g_scales, n):
-    parts = [
-        g_bias_in.reshape(n, -1),
-        g_vectors.reshape(6, n, -1).transpose(1, 0, 2).reshape(n, -1),
-        g_scales.reshape(2, n, -1).transpose(1, 0, 2).reshape(n, -1),
-    ]
-    small = jnp.concatenate(parts, axis=1)
-    return jnp.pad(small, ((0, 0), (0, 1024 - small.shape[1]))).reshape(n, 8, 128)
+        compiler_params=pltpu.CompilerParams(collective_id=3, has_side_effects=True, vmem_limit_bytes=48 * MIB),
+        name="tokens_gradient",
+    )(packed, w_qkv, d_sum, d_proj, out_small, ffn_small, bias_in, attn_small)
+
+
+def per_device(
+    n,
+    tokens, lengths, positives, datasets, w_qkv, w_attn_out, w_ffn_in, w_ffn_out, b_ffn_in, biases, gains,
+):
+    seq_count, seq_len, width = (tokens.shape[1], tokens.shape[2], tokens.shape[3])
+    lens = lengths[0]
+    inputs = tokens[0].reshape(seq_count * seq_len, width)
+    (pooled, query, key_t, value, probs, context_t, low_t, x_t, n1, n2, inv, hidden, slope) = encoder(
+        lens, inputs, w_qkv, w_attn_out, w_ffn_in, w_ffn_out, b_ffn_in, biases, gains
+    )
+    pooled = pooled.reshape(seq_count, width)
+    d_pooled = loss_gradient(pooled, positives, datasets, n)
+    packed_out, out_small = out_gradient(lens, d_pooled, n2, inv, gains, hidden, n)
+    summed_out, packed_in, d_sum, ffn_small, bias_in = ffn_backward(
+        packed_out, lens, d_pooled, w_ffn_in, w_ffn_out, n1, n2, inv, slope, low_t, gains, n
+    )
+    summed_in, packed_rest, d_proj, attn_small = attention_backward(
+        packed_in, w_attn_out, d_sum, query, key_t, value, probs, context_t, x_t, n
+    )
+    summed_attn, summed_qkv, small, grad_tokens = tokens_gradient(
+        packed_rest, w_qkv, d_sum, d_proj, out_small, ffn_small, bias_in, attn_small, n
+    )
+    part = width // n
+    return (
+        pooled[None],
+        grad_tokens.reshape(1, seq_count, seq_len, width),
+        summed_qkv[None],
+        summed_attn[None],
+        summed_in[None],
+        summed_out[None],
+        small[8:12, :part].reshape(1, 4 * part),
+        small[None, 0:6, :part],
+        small[None, 6:8, :part],
+    )
 
 
 def from_behind(value, axis, steps):
@@ -399,8 +966,8 @@
     return jnp.where(is_passage, d_passages, returned.astype(jnp.float32))
 
 
-def per_device(
-    n, direct,
+def per_device_plain(
+
     tokens, lengths, positives, datasets, w_qkv, w_attn_out, w_ffn_in, w_ffn_out, b_ffn_in, biases, gains,
 ):
     seq_count, seq_len, width = (tokens.shape[1], tokens.shape[2], tokens.shape[3])
@@ -447,10 +1014,7 @@
         jnp.sum(output.reshape(seq_count, seq_len, width) * keep_float[:, :, None], axis=1)
         / lens_float
     )
-    if direct:
-        d_pooled = loss_gradient(pooled, positives, datasets, n)
-    else:
-        d_pooled = loss_gradient_plain(pooled, positives, datasets)
+    d_pooled = loss_gradient_plain(pooled, positives, datasets)
     d_output = ((d_pooled / lens_float)[:, None, :] * keep_float[:, :, None]).reshape(rows, width)
     d_second, d_gain_two, d_shift_two = norm_backward(d_output, normed_two, inverse_two, scales[1])
     d_branch = d_second.astype(jnp.bfloat16)
@@ -498,25 +1062,16 @@
         [g_bias_query, g_bias_value, g_bias_attn, d_shift_one, g_bias_out, d_shift_two]
     )
     g_scales = jnp.stack([d_gain_one, d_gain_two])
-    if direct:
-        packed = packed_of(g_weight_out, g_weight_in, g_weight_attn, g_weight_qkv, n)
-        small = small_of(g_bias_in, g_vectors, g_scales, n)
-        summed_out, summed_in, summed_attn, summed_qkv, small = summed_over_batch(packed, small, n)
-        small = small.reshape(1024)
-        part = width // n
-        summed_bias_in = small[: 4 * part]
-        summed_vectors = small[4 * part : 10 * part].reshape(6, part)
-        summed_scales = small[10 * part : 12 * part].reshape(2, part)
-    else:
-        def scatter(value, dimension):
-            return lax.psum_scatter(value, "batch", scatter_dimension=dimension, tiled=True)
-
-        summed_qkv, summed_attn, summed_in, summed_out = (
-            scatter(g_weight_qkv, 0), scatter(g_weight_attn, 0), scatter(g_weight_in, 0), scatter(g_weight_out, 0)
-        )
-        summed_bias_in, summed_vectors, summed_scales = (
-            scatter(g_bias_in, 0), scatter(g_vectors, 1), scatter(g_scales, 1)
-        )
+
+    def scatter(value, dimension):
+        return lax.psum_scatter(value, "batch", scatter_dimension=dimension, tiled=True)
+
+    summed_qkv, summed_attn, summed_in, summed_out = (
+        scatter(g_weight_qkv, 0), scatter(g_weight_attn, 0), scatter(g_weight_in, 0), scatter(g_weight_out, 0)
+    )
+    summed_bias_in, summed_vectors, summed_scales = (
+        scatter(g_bias_in, 0), scatter(g_vectors, 1), scatter(g_scales, 1)
+    )
     return (
         pooled[None],
         d_inputs.reshape(1, seq_count, seq_len, width),
@@ -558,5 +1113,5 @@
         P("tower", None, "batch"),
     )
     return jax.shard_map(
-        partial(per_device, n, direct), mesh=mesh, in_specs=in_specs, out_specs=out_specs, check_vma=False
-    )
+        partial(per_device, n) if direct else per_device_plain, mesh=mesh, in_specs=in_specs, out_specs=out_specs, check_vma=False
+    )

time: 445 us -> 209 us (0.47); the launches traced: 439 us -> 208 us
  matrix products: 143 us -> 0 us
  local copies, waits for them, and re-layouts: 140 us -> 15.2 us
  Pallas kernels: 98.2 us -> 191 us
  other arithmetic: 56.5 us -> 1.28 us
    dot_general x18 -> x0, matrix products: 143 us -> none  [the longest x4 47.7 us: product(): return jnp.dot(left, right, preferred_element_type=jnp.float32)]
    pallas_call x1 -> x5, Pallas kernels: 82.3 us -> 175 us  [the longest x1 48.1 us: encoder(): pl.pallas_call(encoder_kernel, grid_spec=pltpu.PrefetchScalarGridSpec(num...]
    reshape x13 -> x1, local copies, waits for them, and re-layouts: 64.5 us -> 0.64 us  [per_device(): small[8:12, :part].reshape(1, 4 * part)]
    another operation x12 -> x0, local copies, waits for them, and re-layouts: 19.9 us -> none  [the longest x1 8.76 us: packed_of(): jnp.stack([piece_out, piece_in, piece_rest])]
    reduce_sum x8 -> x0, other arithmetic: 18.7 us -> none  [the longest x2 6.06 us: norm_backward(): return (d_total, jnp.sum(grad * normed, axis=0), jnp.sum(grad, axis=0))]
    convert_element_type x8 -> x0, local copies, waits for them, and re-layouts: 18.7 us -> none  [the longest x1 5.81 us: packed_of(): g_qkv.astype(low).reshape(n, rows, 2, 1152)]
    slice x7 -> x1, local copies, waits for them, and re-layouts: 11.4 us -> 0.01 us  [per_device(): small[8:12, :part].reshape(1, 4 * part)]
    convert_element_type x3 -> x0, other arithmetic: 10.8 us -> none  [the longest x1 8.06 us: per_device(): (probs * (d_probs - jnp.sum(d_probs * probs, axis=-1, keepdims=True))).as...]
where the time goes in v2:
time: 209 us; the launch traced here: 208 us
  Pallas kernels  191 us (91%)
  local copies, waits for them, and re-layouts  15.2 us (7%)
    pallas_call x1, Pallas kernels, encoder(): pl.pallas_call(encoder_kernel, grid_spec=pltpu.PrefetchScalarGridSpec(num...  48.1 us
    pallas_call x1, Pallas kernels, ffn_backward(): pl.pallas_call(partial(ffn_kernel, n), in_specs=[anywhere, pl.BlockSpec(m...  40.2 us
    pallas_call x1, Pallas kernels, attention_backward(): pl.pallas_call(partial(attention_kernel, n), in_specs=[anywhere] * 9, out...  39.7 us
    pallas_call x1, Pallas kernels, tokens_gradient(): pl.pallas_call(partial(tokens_kernel, n), in_specs=[anywhere] * 4 + [vmem...  34.1 us
    pallas_call x1, Pallas kernels, loss_gradient(): pl.pallas_call(partial(loss_kernel, n), out_shape=jax.ShapeDtypeStruct((8...  16 us
    unnamed x33, local copies, waits for them, and re-layouts  13.9 us
    pallas_call x1, Pallas kernels, out_gradient(): pl.pallas_call(out_kernel, grid_spec=pltpu.PrefetchScalarGridSpec(num_sca...  12.4 us

profile of v2, /device:TPU:0, one launch (start us, length us, event | category | flops | bytes accessed | tf_op | source)
XLA Modules:
  0.0 207.8 jit_solution(14585905548422562836)
XLA Ops:
  0.6 0.7 convert_bitcast_fusion
  1.3 0.6 select_maximum_fusion.extra_ref
  1.9 1.3 copy.20.vec_ref
  3.3 0.0 copy-start.5
  3.3 0.0 copy-start.9
  3.3 48.1 %encoder.1 = (f32[4,1,768]{2,1,0:T(1,128)}, bf16[1024,768]{1,0:T(8,128)(2,1)}, bf16[768,1024]{1,0:T(8,128)(2,1)}, bf16[1024,768]{1,0:T(8,128)(2,1)}, bf16[4,12,2...) custom-call(s32[4]{0:T(128)} %bitcast.22, ...), custom_call_target="tpu_custom_call" | custom-call | tf_op jit(solution)/shard_map/encoder/pallas_call | solution.py:299
  51.4 1.3 copy.21
  52.7 1.3 copy.25
  54.0 16.0 %loss.1.dpool_ref = f32[8,768]{1,0:T(8,128)} custom-call(f32[4,768]{1,0:T(4,128)} %bitcast.29, f32[4,256]{1,0:T(4,128)} %select_maximum_fusion.extra_ref), custom_call_target="tpu_custom_call" | custom-call | tf_op jit(solution)/shard_map/loss/pallas_call | solution.py:171
  70.0 0.0 copy-done.5
  70.0 0.0 copy-done.9
  70.0 0.0 copy-start
  70.0 1.4 copy-done
  71.4 0.0 copy-start.1
  71.4 1.0 copy-done.1
  72.5 0.0 copy-start.4
  72.5 0.7 copy-done.4
  73.2 12.4 %out_gradient.1 = (bf16[8,2,2,48,1536]{4,3,2,1,0:T(8,128)(2,1)}, f32[8,768]{1,0:T(8,128)S(1)}) custom-call(s32[4]{0:T(128)S(1)} %bitcast.24, f32[8,768]{1,0:T(8,128)S(1)} %copy-done.4, bf16[1024,768]{1,0:T(8,128)(2,1)S(1)} %copy-done, f32[1024,128]{1,0:T(8,128)S(1)} %copy-done.1, f32[1,2,768]{2,1,0:T(2,128)S(1)} %copy-done.5, ...), custom_call_target="tpu_custom_call" | custom-call | tf_op jit(solution)/shard_map/out_gradient/pallas_call | solution.py:373
  85.6 40.2 %ffn_backward.1 = (f32[192,768]{1,0:T(8,128)}, bf16[8,2,2,48,1536]{4,3,2,1,0:T(8,128)(2,1)}, f32[1024,768]{1,0:T(8,128)}, f32[8,768]{1,0:T(8,128)}, f32[1,3072]{1,0:T(1,128)}) custom-call(bf16[8,2,2,48,1536]{4,3,2,1,0:T(8,128)(2,1)} %get-tuple-element.41.packed, s32[4]{0:T(128)} %bitcast.23, f32[8,768]{1,0:T(8,128)} %loss.1.dpool_ref, ...), custom_call_target="tpu_custom_call" | custom-call | tf_op jit(solution)/shard_map/ffn_backward/pallas_call | solution.py:633
  125.9 0.0 copy-start.6
  125.9 0.0 copy-start.8
  125.9 39.7 %attention_backward.1 = (f32[48,3072]{1,0:T(8,128)}, bf16[8,2,2,48,1536]{4,3,2,1,0:T(8,128)(2,1)}, bf16[1024,2304]{1,0:T(8,128)(2,1)}, f32[8,768]{1,0:T(8,128)}) custom-call(bf16[8,2,2,48,1536]{4,3,2,1,0:T(8,128)(2,1)} %get-tuple-element.45.packed, bf16[1,768,768]{2,1,0:T(8,128)(2,1)} %wattn_hbm.3, f32[1024,768]{1,0:T(8,128)} %get-tuple-element.46.d_sum_hbm, ...), custom_call_target="tpu_custom_call" | custom-call | tf_op jit(solution)/shard_map/attention_backward/pallas_call | solution.py:760
  165.6 0.0 copy-done.6
  165.6 0.0 copy-done.8
  165.6 0.0 copy-start.7
  165.6 0.7 copy-done.7
  166.4 34.1 %tokens_gradient.1 = (f32[48,768]{1,0:T(8,128)S(1)}, f32[48,2304]{1,0:T(8,128)S(1)}, f32[16,128]{1,0:T(8,128)S(1)}, f32[1024,768]{1,0:T(8,128)S(1)}) custom-call(bf16[8,2,2,48,1536]{4,3,2,1,0:T(8,128)(2,1)} %get-tuple-element.53.packed, bf16[1,768,2304]{2,1,0:T(8,128)(2,1)} %wqkv_hbm.3, f32[1024,768]{1,0:T(8,128)} %get-tuple-element.46.d_sum_hbm, ...), custom_call_target="tpu_custom_call" | custom-call | tf_op jit(solution)/shard_map/tokens_gradient/pallas_call | solution.py:880
  200.5 0.0 copy-start.2
  200.5 0.8 copy-done.2
  201.2 0.6 slice_bitcast_fusion.1
  201.8 0.6 copy.22
  202.4 0.6 reshape.29
  203.0 0.0 copy-start.3
  203.0 0.0 copy-start.11
  203.0 0.0 copy-start.10
  203.0 1.7 copy.31
  204.7 0.0 copy-done.3
  204.7 0.8 copy.32
  205.5 0.7 copy.33
  206.1 0.0 copy-done.11
  206.1 0.8 copy.34
  206.9 0.0 copy-done.10
  206.9 0.8 copy.35
  (2 shorter events, 0.0 us)
Async XLA Ops:
  3.3 66.7 %copy-start.5 = (f32[1,2,768]{2,1,0:T(2,128)S(1)}, f32[1,2,768]{2,1,0:T(2,128)}, u32[]{:S(2)}) copy-start(f32[1,2,768]{2,1,0:T(2,128)} %gain_ref.5) | copy-start | bytes 18436
  3.3 66.7 %copy-start.9 = (s32[1,4]{1,0:T(1,128)S(1)}, s32[1,4]{1,0:T(1,128)}, u32[]{:S(2)}) copy-start(s32[1,4]{1,0:T(1,128)} %param.12) | copy-start | bytes 52
  70.0 1.4 copy-start
  71.4 1.0 copy-start.1
  72.5 0.7 copy-start.4
  125.9 39.7 %copy-start.6 = (f32[8,768]{1,0:T(8,128)S(1)}, f32[8,768]{1,0:T(8,128)}, u32[]{:S(2)}) copy-start(f32[8,768]{1,0:T(8,128)} %get-tuple-element.56.ffn_small_ref) | copy-start | bytes 73732
  125.9 39.7 %copy-start.8 = (f32[1,3072]{1,0:T(1,128)S(1)}, f32[1,3072]{1,0:T(1,128)}, u32[]{:S(2)}) copy-start(f32[1,3072]{1,0:T(1,128)} %get-tuple-element.57.bias_in_ref) | copy-start | bytes 36868
  165.6 0.7 copy-start.7
  200.5 0.8 copy-start.2
  203.0 1.7 copy-start.3
  203.0 3.1 %copy-start.11 = (f32[48,3072]{1,0:T(8,128)S(1)}, f32[48,3072]{1,0:T(8,128)}, u32[]{:S(2)}) copy-start(f32[48,3072]{1,0:T(8,128)} %get-tuple-element.62) | copy-start | bytes 1769476
  203.0 3.9 %copy-start.10 = (f32[192,768]{1,0:T(8,128)S(1)}, f32[192,768]{1,0:T(8,128)}, u32[]{:S(2)}) copy-start(f32[192,768]{1,0:T(8,128)} %get-tuple-element.63) | copy-start | bytes 1769476

commit v3 on v0

--- a/solution.py
+++ b/solution.py
@@ -3,20 +3,20 @@
 import jax
 import jax.numpy as jnp
 from jax import lax
+from jax.experimental import pallas as pl
+from jax.experimental.pallas import tpu as pltpu
 from jax.sharding import PartitionSpec as P
 
 HEADS = 12
-
-
 EPS = 1e-12
 SCALE = 4.0
 HIGH = lax.Precision.HIGHEST
-
-
-def from_behind(value, axis, steps):
-    count = lax.axis_size(axis)
-    leading, last = (max(0, -steps), min(count, count - steps))
-    return lax.ppermute(value, axis, [(source, source + steps) for source in range(leading, last)])
+MESH = pl.DeviceIdType.MESH
+NEG = -1000000000.0
+LOW = jnp.bfloat16
+F32 = jnp.float32
+CHUNKS = 12
+MIB = 2**20
 
 
 def product(left, right):
@@ -56,21 +56,792 @@
         jnp.einsum("sqhe,skhe->shqk", query_heads, key_heads, preferred_element_type=jnp.float32)
         * 0.125
     )
-    return jnp.where(keep[:, None, None, :], raw, -1000000000.0)
+    return jnp.where(keep[:, None, None, :], raw, NEG)
+
+
+def gelu_parts(z):
+    t = 1.0 / (1.0 + jnp.abs(z) * (0.3275911 * 0.7071067811865476))
+    bell = jnp.exp(z * z * -0.5)
+    tail = t * bell * (
+        0.127414796 + t * (-0.142248368 + t * (0.7107068705 + t * (-0.7265760135 + t * 0.5307027145)))
+    )
+    below = jnp.where(z < 0.0, tail, 1.0 - tail)
+    return z * below, below + z * bell * 0.3989422804014327
+
+
+def normed(total):
+    mean = jnp.mean(total, axis=-1, keepdims=True)
+    centered = total - mean
+    inverse = lax.rsqrt(jnp.mean(centered * centered, axis=-1, keepdims=True) + EPS)
+    return centered * inverse, inverse
+
+
+def encoder_kernel(
+    lens, x_ref, wqkv_hbm, wattn_hbm, win_hbm, wout_hbm, bin_ref, vec_ref, gain_ref,
+    pooled_ref, hidden_ref, slope_ref, n1_ref, n2_ref, inv_ref, low_t_ref, query_ref, key_t_ref, value_ref, probs_ref,
+    context_t_ref, x_t_ref,
+    wqkv, wattn, win, wout, sems,
+):
+    step = pl.program_id(0)
+    loads = [
+        pltpu.make_async_copy(source.at[0], target, sems.at[place])
+        for place, (source, target) in enumerate(
+            [(wqkv_hbm, wqkv), (wattn_hbm, wattn), (win_hbm, win), (wout_hbm, wout)]
+        )
+    ]
+
+    @pl.when(step == 0)
+    def _():
+        for load in loads:
+            load.start()
+        loads[0].wait()
+
+    length = lens[step]
+    x = x_ref[...]
+    rows = x.shape[0]
+    query = (product(x, wqkv[:, :768]) + vec_ref[0]).astype(LOW) * 0.125
+    key = product(x, wqkv[:, 768:1536]).astype(LOW)
+    value = (product(x, wqkv[:, 1536:]) + vec_ref[1]).astype(LOW)
+    query_ref[...] = query
+    value_ref[...] = value
+    key_t_ref[...] = key.T
+    x_t_ref[...] = x.T
+    value_t = value.T
+    blocked = jnp.where(lax.broadcasted_iota(jnp.int32, (rows, 1), 0) < length, 0.0, NEG)
+    lane = lax.broadcasted_iota(jnp.int32, (rows, 128), 1)
+
+    def scores_of_head(head):
+        pair = slice(128 * (head // 2), 128 * (head // 2 + 1))
+        mine = (lane < 64) if head % 2 == 0 else (lane >= 64)
+        key_one = jnp.where(mine, key[:, pair], jnp.zeros((), LOW))
+        return transposed_right(key_one, query[:, pair]) + blocked
+
+    def context_of_head(head, probs):
+        context_t_ref[64 * head:64 * (head + 1), :] = product(
+            value_t[64 * head:64 * (head + 1)], probs
+        ).astype(LOW)
+
+    ahead, behind = [scores_of_head(head) for head in range(4)], []
+    for head in range(HEADS):
+        if head + 4 < HEADS:
+            ahead.append(scores_of_head(head + 4))
+        scores = ahead.pop(0)
+        weights = jnp.exp(scores - jnp.max(scores, axis=0, keepdims=True))
+        probs = (weights * (1.0 / jnp.sum(weights, axis=0, keepdims=True))).astype(LOW)
+        probs_ref[:, 256 * head:256 * (head + 1)] = probs
+        behind.append((head, probs))
+        if len(behind) > 2:
+            context_of_head(*behind.pop(0))
+    for item in behind:
+        context_of_head(*item)
+
+    @pl.when(step == 0)
+    def _():
+        loads[1].wait()
+
+    attended = transposed_left(context_t_ref[...], wattn[...]) + vec_ref[2]
+    n1, inv1 = normed(x.astype(F32) + attended)
+    first = n1 * gain_ref[0, 0:1] + vec_ref[3]
+    first_low = first.astype(LOW)
+    low_t_ref[...] = first_low.T
+    n1_ref[...] = n1.astype(LOW)
+
+    @pl.when(step == 0)
+    def _():
+        loads[2].wait()
+        loads[3].wait()
+
+    total = first + vec_ref[4]
+    blocks = [slice(768 * part, 768 * (part + 1)) for part in range(4)]
+    ahead, late = product(first_low, win[:, blocks[0]]), None
+    for part in range(4):
+        before = ahead
+        if part + 1 < 4:
+            ahead = product(first_low, win[:, blocks[part + 1]])
+        hidden, slope = gelu_parts(before + bin_ref[:, blocks[part]])
+        hidden = hidden.astype(LOW)
+        hidden_ref[:, blocks[part]] = hidden
+        slope_ref[:, blocks[part]] = slope.astype(LOW)
+        if late is not None:
+            total = total + product(late, wout[blocks[part - 1], :])
+        late = hidden
+    total = total + product(late, wout[blocks[3], :])
+    n2, inv2 = normed(total)
+    n2_ref[...] = n2.astype(LOW)
+    inv_ref[...] = jnp.where(lane < 64, inv1, inv2)
+    output = n2 * gain_ref[0, 1:2] + vec_ref[5]
+    keep = lax.broadcasted_iota(jnp.int32, (rows, 1), 0) < length
+    pooled_ref[pl.ds(step, 1)] = jnp.sum(jnp.where(keep, output, 0.0), axis=0, keepdims=True) / length.astype(F32)
+
+
+def encoder(lens, x, w_qkv, w_attn, w_in, w_out, b_in, vectors, gains):
+    seqs = lens.shape[0]
+    rows = x.shape[0]
+    per = rows // seqs
+
+    def by_rows(width):
+        return pl.BlockSpec((per, width), lambda s, *_: (s, 0))
+
+    def by_columns(height):
+        return pl.BlockSpec((height, per), lambda s, *_: (0, s))
+
+    def full(*shape):
+        return pl.BlockSpec(shape, lambda s, *_: (0,) * len(shape))
+
+    anywhere = pl.BlockSpec(memory_space=pl.ANY)
+    def wide(width, kind=LOW):
+        return by_rows(width), jax.ShapeDtypeStruct((rows, width), kind)
+
+    tall = by_columns(768), jax.ShapeDtypeStruct((768, rows), LOW)
+    kept = [
+        wide(3072), wide(3072), wide(768), wide(768), wide(128, F32), tall,
+        wide(768), tall, wide(768), wide(3072), tall, tall,
+    ]
+    return pl.pallas_call(
+        encoder_kernel,
+        grid_spec=pltpu.PrefetchScalarGridSpec(
+            num_scalar_prefetch=1,
+            grid=(seqs,),
+            in_specs=[by_rows(768)] + [anywhere] * 4 + [full(1, 3072), full(6, 1, 768), full(1, 2, 768)],
+            out_specs=[full(seqs, 768)] + [spec for spec, _ in kept],
+            scratch_shapes=[
+                pltpu.VMEM((768, 2304), LOW), pltpu.VMEM((768, 768), LOW),
+                pltpu.VMEM((768, 3072), LOW), pltpu.VMEM((3072, 768), LOW),
+                pltpu.SemaphoreType.DMA((4,)),
+            ],
+        ),
+        out_shape=[jax.ShapeDtypeStruct((seqs, 768), F32)] + [shape for _, shape in kept],
+        compiler_params=pltpu.CompilerParams(vmem_limit_bytes=56 * MIB),
+        name="encoder",
+    )(lens, x, w_qkv, w_attn, w_in, w_out, b_in, vectors, gains)
+
+
+def second_norm_backward(grad_row, length, first_row, n2, inv2, gain):
+    scaled = grad_row * gain
+    mean = jnp.mean(scaled, axis=1, keepdims=True)
+    along = jnp.mean(scaled * n2, axis=1, keepdims=True)
+    keep = first_row + lax.broadcasted_iota(jnp.int32, (n2.shape[0], 1), 0) < length
+    return jnp.where(keep, inv2 * (scaled - mean - n2 * along), 0.0), keep
+
+
+def select(condition):
+    return jnp.where(condition, 1.0, 0.0)
+
+
+def aligned(start, size, multiple):
+    return pl.ds(pl.multiple_of(start, multiple), size)
+
+
+class Sums:
+    def __init__(self, n, scratch):
+        (self.grads, self.paired, self.crossed, self.rows_got, self.got, self.pair_send, self.pair_recv,
+         self.cross_send, self.cross_recv, self.z_send, self.z_recv) = scratch
+        self.tower, self.me = lax.axis_index("tower"), lax.axis_index("batch")
+        self.depth = n // 4
+        self.z, self.y, self.core = self.me // 4, lax.rem(self.me // 2, 2), lax.rem(self.me, 2)
+
+    def z_at(self, offset):
+        return lax.rem(self.z + offset, self.depth)
+
+    def device(self, z, y, core):
+        return (self.tower, z * 4 + y * 2 + core)
+
+    def pair_copy(self, chunk):
+        return pltpu.make_async_remote_copy(
+            src_ref=self.grads.at[chunk, :, 1 - self.core], dst_ref=self.paired.at[chunk],
+            send_sem=self.pair_send.at[chunk], recv_sem=self.pair_recv.at[chunk],
+            device_id=self.device(self.z, self.y, 1 - self.core), device_id_type=MESH,
+        )
+
+    def cross_copy(self, chunk):
+        return pltpu.make_async_remote_copy(
+            src_ref=self.grads.at[chunk, 1 - self.y, self.core], dst_ref=self.crossed.at[chunk],
+            send_sem=self.cross_send.at[chunk], recv_sem=self.cross_recv.at[chunk],
+            device_id=self.device(self.z, 1 - self.y, self.core), device_id_type=MESH,
+        )
+
+    def rows_copy(self, chunk):
+        return pltpu.make_async_remote_copy(
+            src_ref=self.grads.at[chunk, self.y, self.core], dst_ref=self.rows_got.at[chunk],
+            send_sem=self.z_send.at[chunk, 0], recv_sem=self.z_recv.at[chunk, 0],
+            device_id=self.device(self.z_at(chunk + 1), self.y, self.core), device_id_type=MESH,
+        )
+
+    def z_copy(self, chunk, offset):
+        return pltpu.make_async_remote_copy(
+            src_ref=self.grads.at[chunk, self.y, self.core, self.z_at(offset)],
+            dst_ref=self.got.at[chunk - 4, offset - 1],
+            send_sem=self.z_send.at[chunk, offset - 1], recv_sem=self.z_recv.at[chunk, offset - 1],
+            device_id=self.device(self.z_at(offset), self.y, self.core), device_id_type=MESH,
+        )
+
+    def pair(self, chunk):
+        self.pair_copy(chunk).start()
+
+    def cross(self, chunk):
+        self.pair_copy(chunk).wait_recv()
+        place = (chunk, 1 - self.y, self.core)
+        self.grads[place] = (self.grads[place].astype(F32) + self.paired[chunk, 1 - self.y].astype(F32)).astype(LOW)
+        self.cross_copy(chunk).start()
+
+    def spread(self, chunk, by_rows=False, last=False):
+        self.cross_copy(chunk).wait_recv()
+        place = (chunk, self.y, self.core)
+        self.grads[place] = (
+            self.grads[place].astype(F32) + self.paired[chunk, self.y].astype(F32) + self.crossed[chunk].astype(F32)
+        ).astype(LOW)
+        if by_rows:
+            if not last:
+                self.rows_copy(chunk).start()
+        else:
+            for offset in range(1, self.depth):
+                self.z_copy(chunk, offset).start()
+
+    def rows_total(self, part):
+        total = self.grads[3, self.y, self.core, part].astype(F32)
+        for chunk in range(3):
+            total = total + self.rows_got[chunk, part].astype(F32)
+        return total
+
+    def total(self, chunk):
+        total = self.grads[chunk, self.y, self.core, self.z].astype(F32)
+        for offset in range(1, self.depth):
+            self.z_copy(chunk, offset).wait_recv()
+            total = total + self.got[chunk - 4, offset - 1].astype(F32)
+        return total
+
+    def close(self):
+        @pl.loop(0, CHUNKS)
+        def _(chunk):
+            self.pair_copy(chunk).wait_send()
+            self.cross_copy(chunk).wait_send()
+
+        for chunk in range(3):
+            self.rows_copy(chunk).wait_send()
+
+        @pl.loop(4, CHUNKS)
+        def _(chunk):
+            for offset in range(1, self.depth):
+                self.z_copy(chunk, offset).wait_send()
+
+
+def d_pooled_of(n, tower, me, everyone):
+    seqs = 4 * n
+    packed = everyone[...]
+    questions = packed[:n].reshape(16 * n, 256)
+    passages = packed[n:].reshape(16 * n, 256)
+    rows = lax.broadcasted_iota(jnp.int32, (seqs, 16 * n), 0)
+    places = lax.broadcasted_iota(jnp.int32, (seqs, 16 * n), 1)
+    owner, lane = rows // 4, lax.rem(rows, 4)
+
+    def picked(values, row):
+        return product(select(places == owner * 16 + row).astype(LOW), values)
+
+    def whole(values):
+        parts = [product(select(places == owner * 16 + 4 * part + lane).astype(LOW), values) for part in range(3)]
+        return jnp.concatenate(parts, axis=1)
+
+    column_lane = lax.broadcasted_iota(jnp.int32, (seqs, 256), 1)
+    column_want = lax.rem(lax.broadcasted_iota(jnp.int32, (seqs, 256), 0), 4)
+
+    def column(row):
+        return jnp.sum(
+            jnp.where(column_lane == column_want, picked(passages, row), 0.0), axis=1, keepdims=True
+        )
+
+    question_float, passage_float = whole(questions), whole(passages)
+    positives, sets = column(12), column(13)
+    first = lax.broadcasted_iota(jnp.int32, (seqs, seqs), 0)
+    second = lax.broadcasted_iota(jnp.int32, (seqs, seqs), 1)
+    set_row = jnp.sum(jnp.where(first == second, sets, 0.0), axis=0, keepdims=True)
+    chosen = second.astype(F32) == positives
+    query_set = jnp.sum(jnp.where(chosen, set_row, 0.0), axis=1, keepdims=True)
+    logits = transposed_right(question_float.astype(LOW), passage_float.astype(LOW)) * SCALE
+    masked = jnp.where(set_row == query_set, logits, NEG)
+    weights = jnp.exp(masked - jnp.max(masked, axis=1, keepdims=True))
+    softmax = weights / jnp.sum(weights, axis=1, keepdims=True)
+    d_logits = (softmax - select(chosen)) * SCALE
+    mine_row = lax.broadcasted_iota(jnp.int32, (8, seqs), 0)
+    mine_column = lax.broadcasted_iota(jnp.int32, (8, seqs), 1)
+    own = select((mine_column == me * 4 + mine_row) & (mine_row < 4))
+    by_question = jnp.dot(own, d_logits, precision=HIGH, preferred_element_type=F32)
+    by_passage = lax.dot_general(
+        own, d_logits, (((1,), (1,)), ((), ())), precision=HIGH, preferred_element_type=F32
+    )
+    is_passage = tower == 1
+    terms = jnp.where(is_passage, by_passage, by_question)
+    others = jnp.where(is_passage, question_float, passage_float)
+    grad = jnp.dot(terms, others, precision=HIGH, preferred_element_type=F32)
+    return jnp.where(is_passage, grad, grad.astype(LOW).astype(F32))
+
+
+def backward_kernel(
+    n, lens, positives, datasets, pooled_ref, gain_ref, wqkv_hbm, wattn_hbm, win_hbm, wout_hbm,
+    hidden_hbm, slope_hbm, n1_hbm, n2_hbm, inv_hbm, low_t_hbm, query_hbm, key_t_hbm, value_hbm, probs_hbm,
+    context_t_hbm, x_t_hbm,
+    out_ref, in_ref, attn_ref, qkv_ref, summed_small_ref, tokens_out,
+    grads, paired, crossed, rows_got, got, pair_send, pair_recv, cross_send, cross_recv, z_send, z_recv,
+    first_weights, second_weights, wide, tall, rows_a, rows_b, rows_c, key_t, context_t, inv, stage,
+    rows_small, bias_in, small, small_got, mine, everyone, d_pooled,
+    sems, stage_sems, small_send, small_recv, pool_send, pool_recv,
+):
+    tower, me = lax.axis_index("tower"), lax.axis_index("batch")
+    flat = tower * n + me
+    everybody = 2 * n
+    sums = Sums(
+        n, (grads, paired, crossed, rows_got, got, pair_send, pair_recv, cross_send, cross_recv, z_send, z_recv)
+    )
+    barrier = pltpu.get_barrier_semaphore()
+
+    def other_device(step):
+        other = lax.rem(flat + step, everybody)
+        return other // n, lax.rem(other, n)
+
+    @pl.loop(1, everybody)
+    def _(step):
+        pl.semaphore_signal(barrier, inc=1, device_id=other_device(step), device_id_type=MESH)
+
+    def load(place, source, target):
+        return pltpu.make_async_copy(source, target, sems.at[place])
+
+    def seq_rows(seq):
+        return aligned(seq * 256, 256, 256)
+
+    def block(part):
+        return slice(768 * part, 768 * (part + 1))
+
+    n2_load, inv_load = load(0, n2_hbm, rows_a), load(1, inv_hbm, inv)
+    hidden_loads = [
+        load(2 + part, hidden_hbm.at[:, aligned(sums.z_at(part + 1) * 768, 768, 128)], wide.at[:, block(part)])
+        for part in range(4)
+    ]
+    slope_loads = [load(10 + part, slope_hbm.at[:, block(part)], wide.at[:, block(part)]) for part in range(4)]
+    out_load = load(14, wout_hbm.at[0], first_weights)
+    in_loads = [load(15 + part, win_hbm.at[0, :, block(part)], second_weights.at[block(part)]) for part in range(4)]
+    n1_load, low_load = load(19, n1_hbm, rows_b), load(20, low_t_hbm, tall)
+    key_load, context_load = load(21, key_t_hbm, key_t), load(22, context_t_hbm, context_t)
+    attn_load = load(23, wattn_hbm.at[0], first_weights.at[block(0)])
+    qkv_loads = [
+        load(24 + part, wqkv_hbm.at[0, :, block(part)], first_weights.at[block(part + 1)]) for part in range(3)
+    ]
+    query_load, value_load, x_load = load(27, query_hbm, rows_a), load(28, value_hbm, rows_b), load(29, x_t_hbm, tall)
+
+    def probs_load(seq):
+        return load(30 + seq, probs_hbm.at[seq_rows(seq)], wide.at[seq_rows(seq)])
+
+    for copy in [n2_load, inv_load] + hidden_loads + [out_load] + in_loads + [n1_load, low_load, key_load, context_load]:
+        copy.start()
+
+    row = lax.broadcasted_iota(jnp.int32, (4, 256), 0)
+    lane = lax.broadcasted_iota(jnp.int32, (4, 256), 1)
+    extra = jnp.zeros((4, 256), F32)
+    for seq in range(4):
+        for place, numbers in enumerate((positives, datasets)):
+            extra = jnp.where((row == place) & (lane == seq), numbers[seq].astype(F32), extra)
+    pooled = pooled_ref[...]
+    pooled_block = jnp.concatenate(
+        [pooled[:, 0:256], pooled[:, 256:512], pooled[:, 512:768], extra], axis=0
+    ).astype(LOW)
+    mine[...] = pooled_block
+    everyone[flat] = pooled_block
+    rows_small[...] = jnp.zeros_like(rows_small)
+    bias_in[...] = jnp.zeros_like(bias_in)
+    pl.semaphore_wait(barrier, everybody - 1)
+
+    def pool_copy(step):
+        return pltpu.make_async_remote_copy(
+            src_ref=mine, dst_ref=everyone.at[flat], send_sem=pool_send.at[step], recv_sem=pool_recv.at[step],
+            device_id=other_device(step), device_id_type=MESH,
+        )
+
+    @pl.loop(1, everybody)
+    def _(step):
+        pool_copy(step).start()
+
+    @pl.loop(1, everybody)
+    def _(step):
+        pool_copy(step).wait_recv()
+
+    d_pooled[...] = d_pooled_of(n, tower, me, everyone)
+
+    n2_load.wait()
+    inv_load.wait()
+
+    def second_backward(seq):
+        length = lens[seq]
+        grad_row = d_pooled[pl.ds(seq, 1)] / length.astype(F32)
+        normal = rows_a[seq_rows(seq)].astype(F32)
+        d_second, keep = second_norm_backward(
+            grad_row, length, 0, normal, inv[seq_rows(seq), 64:65], gain_ref[0, 1:2]
+        )
+        return d_second, keep, normal, grad_row
+
+    @pl.loop(0, 4)
+    def _(seq):
+        d_second, keep, normal, grad_row = second_backward(seq)
+        low = d_second.astype(LOW)
+        rows_c[seq_rows(seq)] = low
+        rows_small[4:5] += jnp.sum(low.astype(F32), axis=0, keepdims=True)
+        rows_small[5:6] += d_pooled[pl.ds(seq, 1)]
+        rows_small[7:8] += grad_row * jnp.sum(jnp.where(keep, normal, 0.0), axis=0, keepdims=True)
+
+    for part in range(4):
+        hidden_loads[part].wait()
+        for y in range(2):
+            columns = slice(768 * part + 384 * y, 768 * part + 384 * (y + 1))
+            grads[part, y] = transposed_left(wide[:, columns], rows_c[...]).astype(LOW).reshape(2, 4, 48, 768)
+        slope_loads[part].start()
+        sums.pair(part)
+        if part in (1, 2):
+            sums.cross(part - 1)
+
+    @pl.loop(1, everybody)
+    def _(step):
+        pool_copy(step).wait_send()
+
+    for copy in [out_load] + in_loads + [n1_load] + slope_loads:
+        copy.wait()
+
+    def stage_copy(seq, kind):
+        slot, rows = stage.at[lax.rem(seq, 2)], tokens_out.at[seq_rows(seq)]
+        source, target = (rows, slot) if kind == 1 else (slot, rows)
+        return pltpu.make_async_copy(source, target, stage_sems.at[kind, seq])
+
+    @pl.loop(0, 4)
+    def _(seq):
+        @pl.when(seq >= 1)
+        def _():
+            sums.spread(lax.max(seq - 1, 0), by_rows=True)
+
+        @pl.when((seq >= 1) & (seq <= 2))
+        def _():
+            sums.cross(lax.min(seq + 1, 3))
+
+        rows = seq_rows(seq)
+        d_second = second_backward(seq)[0]
+        d_branch = rows_c[rows]
+        d_first = d_second
+        for part in range(4):
+            d_pre = (
+                transposed_right(d_branch, first_weights[block(part), :]) * wide[rows, block(part)].astype(F32)
+            ).astype(LOW)
+            wide[rows, block(part)] = d_pre
+            bias_in[:, block(part)] += jnp.sum(d_pre.astype(F32), axis=0, keepdims=True)
+            d_first = d_first + transposed_right(d_pre, second_weights[block(part), :])
+        normal = rows_b[rows].astype(F32)
+        scaled = d_first * gain_ref[0, 0:1]
+        mean = jnp.mean(scaled, axis=1, keepdims=True)
+        along = jnp.mean(scaled * normal, axis=1, keepdims=True)
+        d_sum_one = inv[rows, 0:1] * (scaled - mean - normal * along)
+
+        @pl.when(seq >= 2)
+        def _():
+            stage_copy(lax.max(seq - 2, 0), 0).wait()
+
+        stage[lax.rem(seq, 2)] = d_sum_one
+        stage_copy(seq, 0).start()
+        d_attended = d_sum_one.astype(LOW)
+        rows_c[rows] = d_attended
+        rows_small[2:3] += jnp.sum(d_attended.astype(F32), axis=0, keepdims=True)
+        rows_small[3:4] += jnp.sum(d_first, axis=0, keepdims=True)
+        rows_small[6:7] += jnp.sum(d_first * normal, axis=0, keepdims=True)
+
+    for copy in [attn_load] + qkv_loads + [query_load, value_load]:
+        copy.start()
+    low_load.wait()
+
+    def store(chunk, rows_ref, columns):
+        for half in range(2):
+            grad = product(rows_ref[384 * half:384 * (half + 1)], columns).astype(LOW)
+            for z in range(2):
+                grads[chunk, :, :, 2 * half + z] = grad[192 * z:192 * (z + 1)].reshape(2, 2, 48, 768)
+        sums.pair(chunk)
+
+    for part in range(4):
+        store(4 + part, tall, wide[:, block(part)])
+        if part == 1:
+            sums.spread(3, by_rows=True, last=True)
+        if part in (1, 2):
+            sums.cross(3 + part)
+    for seq in range(4):
+        probs_load(seq).start()
+    x_load.start()
+
+    context_load.wait()
+    store(8, context_t, rows_c[...])
+    for copy in [attn_load] + qkv_loads + [query_load, value_load, key_load]:
+        copy.wait()
+    lane = lax.broadcasted_iota(jnp.int32, (256, 128), 1)
+    none = jnp.zeros((), LOW)
+
+    @pl.loop(0, 4)
+    def _(seq):
+        rows = seq_rows(seq)
+
+        @pl.when(seq >= 1)
+        def _():
+            sums.spread(3 + lax.max(seq, 1))
+            sums.cross(5 + lax.max(seq, 1))
+
+        probs_load(seq).wait()
+        d_attended = rows_c[rows]
+        weight = first_weights[block(0), :]
+        d_context = transposed_right(d_attended, weight).astype(LOW)
+        d_context_t = transposed_right(weight, d_attended).astype(LOW)
+        for pair in range(6):
+            lanes = slice(128 * pair, 128 * (pair + 1))
+            key_pair, query_pair, value_pair = key_t[lanes, rows], rows_a[rows, lanes], rows_b[rows, lanes]
+            d_context_pair, d_context_t_pair = d_context[:, lanes], d_context_t[lanes]
+            weighed = d_context_t_pair.astype(F32) * context_t[lanes, rows].astype(F32)
+            d_queries, d_keys, d_values = [], [], []
+            for one in range(2):
+                half = slice(64 * one, 64 * (one + 1))
+                head = 2 * pair + one
+                prob = wide[rows, 256 * head:256 * (head + 1)]
+                value_one = jnp.where((lane < 64) if one == 0 else (lane >= 64), value_pair, none)
+                d_prob = product(value_one, d_context_t_pair)
+                row_sum = jnp.sum(weighed[half], axis=0, keepdims=True)
+                d_score = (prob.astype(F32) * (d_prob - row_sum)).astype(LOW)
+                d_values.append(product(prob, d_context_pair))
+                d_keys.append(product(d_score, query_pair))
+                d_queries.append(product(key_pair[half], d_score))
+            d_query = (jnp.concatenate(d_queries, axis=0).T * 0.125).astype(LOW)
+            d_key = jnp.where(lane < 64, d_keys[0], d_keys[1]).astype(LOW)
+            d_value = jnp.where(lane < 64, d_values[0], d_values[1]).astype(LOW)
+            for part, value in enumerate((d_query, d_key, d_value)):
+                second_weights[aligned(1024 * part + seq * 256, 256, 256), lanes] = value
+            rows_small[0:1, lanes] += jnp.sum(d_query.astype(F32), axis=0, keepdims=True)
+            rows_small[1:2, lanes] += jnp.sum(d_value.astype(F32), axis=0, keepdims=True)
+
+    for seq in (2, 3):
+        stage_copy(seq, 0).wait()
+    for seq in (0, 1):
+        stage_copy(seq, 1).start()
+    x_load.wait()
+    sums.spread(7)
+    for part in range(3):
+        store(9 + part, tall, second_weights[1024 * part:1024 * (part + 1), :])
+        if part == 1:
+            sums.cross(9)
+
+    bundle, bias_row = rows_small[...], bias_in[...]
+    small[...] = jnp.zeros_like(small)
+    for device in range(n):
+        small[device, 0:8, 0:48] = bundle[:, 48 * device:48 * (device + 1)]
+        for part in range(4):
+            start = 192 * device + 48 * part
+            small[device, 8 + part:9 + part, 0:48] = bias_row[:, start:start + 48]
+
+    def small_copy(step):
+        other = lax.rem(me + step, n)
+        return pltpu.make_async_remote_copy(
+            src_ref=small.at[other], dst_ref=small_got.at[step],
+            send_sem=small_send.at[step], recv_sem=small_recv.at[step],
+            device_id=(tower, other), device_id_type=MESH,
+        )
+
+    sums.spread(8)
+    sums.cross(10)
+
+    @pl.loop(1, n)
+    def _(step):
+        small_copy(step).start()
+
+    def tokens(seq):
+        stage_copy(seq, 1).wait()
+        slot = seq % 2
+        total = stage[slot]
+        for part in range(3):
+            total = total + transposed_right(
+                second_weights[1024 * part + seq * 256:1024 * part + seq * 256 + 256, :],
+                first_weights[block(part + 1), :],
+            )
+        stage[slot] = total
+        stage_copy(seq, 2).start()
+
+    tokens(0)
+    tokens(1)
+    sums.spread(9)
+    sums.cross(11)
+    for seq in (2, 3):
+        stage_copy(seq - 2, 2).wait()
+        stage_copy(seq, 1).start()
+    tokens(2)
+    tokens(3)
+    summed_small_ref[...] = small[me]
+
+    @pl.loop(1, n)
+    def _(step):
+        small_copy(step).wait()
+        summed_small_ref[...] += small_got[step]
+
+    for chunk in range(3):
+        sums.rows_copy(chunk).wait_recv()
+    for part in range(4):
+        out_ref[48 * part:48 * (part + 1)] = sums.rows_total(part)
+    for chunk in range(4, 8):
+        in_ref[:, block(chunk - 4)] = sums.total(chunk)
+    sums.spread(10)
+    attn_ref[...] = sums.total(8)
+    qkv_ref[:, block(0)] = sums.total(9)
+    sums.spread(11)
+    qkv_ref[:, block(1)] = sums.total(10)
+    qkv_ref[:, block(2)] = sums.total(11)
+    for seq in (2, 3):
+        stage_copy(seq, 2).wait()
+    sums.close()
+
+
+def backward(lens, positives, datasets, pooled, gains, weights, activations, n):
+    rows = activations[0].shape[0]
+    anywhere = pl.BlockSpec(memory_space=pl.ANY)
+    vmem = pl.BlockSpec(memory_space=pltpu.VMEM)
+    scalars = pl.BlockSpec(memory_space=pltpu.SMEM)
+    tile = (48, 768)
+    dma = pltpu.SemaphoreType.DMA
+    return pl.pallas_call(
+        partial(backward_kernel, n),
+        in_specs=[scalars] * 3 + [vmem] * 2 + [anywhere] * (4 + len(activations)),
+        out_specs=[vmem] * 5 + [anywhere],
+        out_shape=[
+            jax.ShapeDtypeStruct(shape, F32)
+            for shape in ((192, 768), (48, 3072), (48, 768), (48, 2304), (16, 128), (rows, 768))
+        ],
+        scratch_shapes=[
+            pltpu.VMEM((CHUNKS, 2, 2, 4) + tile, LOW), pltpu.VMEM((CHUNKS, 2, 4) + tile, LOW),
+            pltpu.VMEM((CHUNKS, 4) + tile, LOW), pltpu.VMEM((3, 4) + tile, LOW), pltpu.VMEM((CHUNKS - 4, 3) + tile, LOW),
+            dma((CHUNKS,)), dma((CHUNKS,)), dma((CHUNKS,)), dma((CHUNKS,)), dma((CHUNKS, 3)), dma((CHUNKS, 3)),
+            pltpu.VMEM((3072, 768), LOW), pltpu.VMEM((3072, 768), LOW), pltpu.VMEM((rows, 3072), LOW),
+            pltpu.VMEM((768, rows), LOW), pltpu.VMEM((rows, 768), LOW), pltpu.VMEM((rows, 768), LOW),
+            pltpu.VMEM((rows, 768), LOW), pltpu.VMEM((768, rows), LOW), pltpu.VMEM((768, rows), LOW),
+            pltpu.VMEM((rows, 128), F32), pltpu.VMEM((2, 256, 768), F32),
+            pltpu.VMEM((8, 768), F32), pltpu.VMEM((1, 3072), F32),
+            pltpu.VMEM((n, 16, 128), F32), pltpu.VMEM((n, 16, 128), F32),
+            pltpu.VMEM((16, 256), LOW), pltpu.VMEM((2 * n, 16, 256), LOW), pltpu.VMEM((8, 768), F32),
+            dma((34,)), dma((3, 4)), dma((n,)), dma((n,)), dma((2 * n,)), dma((2 * n,)),
+        ],
+        compiler_params=pltpu.CompilerParams(collective_id=1, has_side_effects=True, vmem_limit_bytes=60 * MIB),
+        name="backward",
+    )(lens, positives, datasets, pooled, gains, *weights, *activations)
+
+
+def deliver_kernel(
+    out_hbm, in_hbm, attn_hbm, qkv_hbm, small_hbm, tokens_hbm,
+    out_to, in_to, attn_to, qkv_to, bias_in_to, vectors_to, gains_to, tokens_to,
+    out_held, in_held, attn_held, qkv_held, small_held, held, sems,
+):
+    parts, rows = held.shape[0], held.shape[1]
+    ways = [
+        (tokens_hbm.at[pl.ds(rows * part, rows)], held.at[part], tokens_to.at[pl.ds(rows * part, rows)])
+        for part in range(parts)
+    ] + [
+        (out_hbm, out_held, out_to), (in_hbm, in_held, in_to), (attn_hbm, attn_held, attn_to),
+        (qkv_hbm, qkv_held, qkv_to),
+    ]
+    fetches = [
+        pltpu.make_async_copy(source, middle, sems.at[0, place]) for place, (source, middle, _) in enumerate(ways)
+    ]
+    sends = [
+        pltpu.make_async_copy(middle, target, sems.at[1, place]) for place, (_, middle, target) in enumerate(ways)
+    ]
+    small_fetch = pltpu.make_async_copy(small_hbm, small_held, sems.at[0, len(ways)])
+    small_fetch.start()
+    for fetch in fetches:
+        fetch.start()
+    for fetch, send in zip(fetches, sends):
+        fetch.wait()
+        send.start()
+    small_fetch.wait()
+    small = small_held[...]
+    for row in range(6):
+        vectors_to[row] = small[row:row + 1, :48]
+    gains_to[...] = small[6:8, :48]
+    bias_in_to[...] = jnp.concatenate([small[8 + part:9 + part, :48] for part in range(4)], axis=1)
+    for send in sends:
+        send.wait()
+
+
+def deliver(*arrays):
+    *sums, small, tokens = arrays
+    anywhere = pl.BlockSpec(memory_space=pl.ANY)
+    vmem = pl.BlockSpec(memory_space=pltpu.VMEM)
+    shapes = [array.shape for array in sums] + [(1, 192), (6, 1, 48), (2, 48), tokens.shape]
+    rows, width = tokens.shape
+    parts = 4
+    return pl.pallas_call(
+        deliver_kernel,
+        in_specs=[anywhere] * 6,
+        out_specs=[anywhere] * 4 + [vmem] * 3 + [anywhere],
+        out_shape=[jax.ShapeDtypeStruct(shape, F32) for shape in shapes],
+        scratch_shapes=[pltpu.VMEM(array.shape, F32) for array in sums]
+        + [pltpu.VMEM(small.shape, F32), pltpu.VMEM((parts, rows // parts, width), F32)]
+        + [pltpu.SemaphoreType.DMA((2, parts + 5))],
+        compiler_params=pltpu.CompilerParams(vmem_limit_bytes=60 * MIB),
+        name="deliver",
+    )(*arrays)
 
 
 def per_device(
-    tokens,
-    lengths,
-    positives,
-    datasets,
-    w_qkv,
-    w_attn_out,
-    w_ffn_in,
-    w_ffn_out,
-    b_ffn_in,
-    biases,
-    gains,
+    n,
+    tokens, lengths, positives, datasets, w_qkv, w_attn_out, w_ffn_in, w_ffn_out, b_ffn_in, biases, gains,
+):
+    seq_count, seq_len, width = (tokens.shape[1], tokens.shape[2], tokens.shape[3])
+    lens = lengths[0]
+    inputs = tokens[0].reshape(seq_count * seq_len, width)
+    weights = (w_qkv, w_attn_out, w_ffn_in, w_ffn_out)
+    pooled, *activations = encoder(lens, inputs, *weights, b_ffn_in, biases.transpose(1, 0, 2), gains)
+    *sums, grad_tokens = backward(lens, positives, datasets, pooled, gains, weights, activations, n)
+    summed_out, summed_in, summed_attn, summed_qkv, bias_in, vectors, scales, grad_tokens = deliver(*sums, grad_tokens)
+    return (
+        pooled[None],
+        grad_tokens.reshape(1, seq_count, seq_len, width),
+        summed_qkv[None],
+        summed_attn[None],
+        summed_in[None],
+        summed_out[None],
+        bias_in,
+        vectors.transpose(1, 0, 2),
+        scales[None],
+    )
+
+
+def from_behind(value, axis, steps):
+    count = lax.axis_size(axis)
+    leading, last = (max(0, -steps), min(count, count - steps))
+    return lax.ppermute(value, axis, [(source, source + steps) for source in range(leading, last)])
+
+
+def loss_gradient_plain(pooled, positives, datasets):
+    seq_count = pooled.shape[0]
+    mine = pooled.astype(jnp.bfloat16)
+    questions = from_behind(mine, "tower", 1)
+    everyone, every_set = (
+        lax.all_gather(mine, "batch", axis=0, tiled=True),
+        lax.all_gather(datasets.astype(jnp.bfloat16), "batch", axis=0, tiled=True),
+    )
+    total_seqs = everyone.shape[0]
+    columns = lax.broadcasted_iota(jnp.int32, (seq_count, total_seqs), 1)
+    chosen = columns == positives[:, None]
+    set_row = every_set.astype(jnp.float32)[None, :]
+    query_set = jnp.sum(jnp.where(chosen, set_row, 0.0), axis=1, keepdims=True)
+    allowed = set_row == query_set
+    question_float = questions.astype(jnp.float32)
+    everyone_float = everyone.astype(jnp.float32)
+    logits = jnp.dot(question_float, everyone_float.T, precision=HIGH) * SCALE
+    masked = jnp.where(allowed, logits, NEG)
+    softmax_rows = jnp.exp(masked - jax.nn.logsumexp(masked, axis=1, keepdims=True))
+    d_logits = (softmax_rows - chosen.astype(jnp.float32)) * SCALE
+    d_questions = jnp.dot(d_logits, everyone_float, precision=HIGH).astype(jnp.bfloat16)
+    passage_terms = jnp.dot(d_logits.T, question_float, precision=HIGH)
+    d_passages = lax.psum_scatter(passage_terms, "batch", scatter_dimension=0, tiled=True)
+    returned = from_behind(d_questions, "tower", -1)
+    is_passage = lax.axis_index("tower") == 1
+    return jnp.where(is_passage, d_passages, returned.astype(jnp.float32))
+
+
+def per_device_plain(
+
+    tokens, lengths, positives, datasets, w_qkv, w_attn_out, w_ffn_in, w_ffn_out, b_ffn_in, biases, gains,
 ):
     seq_count, seq_len, width = (tokens.shape[1], tokens.shape[2], tokens.shape[3])
     head_size = width // HEADS
@@ -116,30 +887,7 @@
         jnp.sum(output.reshape(seq_count, seq_len, width) * keep_float[:, :, None], axis=1)
         / lens_float
     )
-    mine = pooled.astype(jnp.bfloat16)
-    questions = from_behind(mine, "tower", 1)
-    everyone, every_set = (
-        lax.all_gather(mine, "batch", axis=0, tiled=True),
-        lax.all_gather(datasets.astype(jnp.bfloat16), "batch", axis=0, tiled=True),
-    )
-    total_seqs = everyone.shape[0]
-    columns = lax.broadcasted_iota(jnp.int32, (seq_count, total_seqs), 1)
-    chosen = columns == positives[:, None]
-    set_row = every_set.astype(jnp.float32)[None, :]
-    query_set = jnp.sum(jnp.where(chosen, set_row, 0.0), axis=1, keepdims=True)
-    allowed = set_row == query_set
-    question_float = questions.astype(jnp.float32)
-    everyone_float = everyone.astype(jnp.float32)
-    logits = jnp.dot(question_float, everyone_float.T, precision=HIGH) * SCALE
-    masked = jnp.where(allowed, logits, -1000000000.0)
-    softmax_rows = jnp.exp(masked - jax.nn.logsumexp(masked, axis=1, keepdims=True))
-    d_logits = (softmax_rows - chosen.astype(jnp.float32)) * SCALE
-    d_questions = jnp.dot(d_logits, everyone_float, precision=HIGH).astype(jnp.bfloat16)
-    passage_terms = jnp.dot(d_logits.T, question_float, precision=HIGH)
-    d_passages = lax.psum_scatter(passage_terms, "batch", scatter_dimension=0, tiled=True)
-    returned = from_behind(d_questions, "tower", -1)
-    is_passage = lax.axis_index("tower") == 1
-    d_pooled = jnp.where(is_passage, d_passages, returned.astype(jnp.float32))
+    d_pooled = loss_gradient_plain(pooled, positives, datasets)
     d_output = ((d_pooled / lens_float)[:, None, :] * keep_float[:, :, None]).reshape(rows, width)
     d_second, d_gain_two, d_shift_two = norm_backward(d_output, normed_two, inverse_two, scales[1])
     d_branch = d_second.astype(jnp.bfloat16)
@@ -187,22 +935,15 @@
         [g_bias_query, g_bias_value, g_bias_attn, d_shift_one, g_bias_out, d_shift_two]
     )
     g_scales = jnp.stack([d_gain_one, d_gain_two])
-    (
-        summed_qkv,
-        summed_attn,
-        summed_in,
-        summed_out,
-        summed_bias_in,
-        summed_vectors,
-        summed_scales,
-    ) = (
-        lax.psum_scatter(g_weight_qkv, "batch", scatter_dimension=0, tiled=True),
-        lax.psum_scatter(g_weight_attn, "batch", scatter_dimension=0, tiled=True),
-        lax.psum_scatter(g_weight_in, "batch", scatter_dimension=0, tiled=True),
-        lax.psum_scatter(g_weight_out, "batch", scatter_dimension=0, tiled=True),
-        lax.psum_scatter(g_bias_in, "batch", scatter_dimension=0, tiled=True),
-        lax.psum_scatter(g_vectors, "batch", scatter_dimension=1, tiled=True),
-        lax.psum_scatter(g_scales, "batch", scatter_dimension=1, tiled=True),
+
+    def scatter(value, dimension):
+        return lax.psum_scatter(value, "batch", scatter_dimension=dimension, tiled=True)
+
+    summed_qkv, summed_attn, summed_in, summed_out = (
+        scatter(g_weight_qkv, 0), scatter(g_weight_attn, 0), scatter(g_weight_in, 0), scatter(g_weight_out, 0)
+    )
+    summed_bias_in, summed_vectors, summed_scales = (
+        scatter(g_bias_in, 0), scatter(g_vectors, 1), scatter(g_scales, 1)
     )
     return (
         pooled[None],
@@ -218,6 +959,8 @@
 
 
 def solution(mesh):
+    n = mesh.shape["batch"]
+    direct = n == 16
     in_specs = (
         P("tower", "batch", None, None),
         P("tower", "batch"),
@@ -243,5 +986,5 @@
         P("tower", None, "batch"),
     )
     return jax.shard_map(
-        per_device, mesh=mesh, in_specs=in_specs, out_specs=out_specs, check_vma=False
-    )
+        partial(per_device, n) if direct else per_device_plain, mesh=mesh, in_specs=in_specs, out_specs=out_specs, check_vma=False
+    )

time: 869 us -> 159 us (0.18)
  waiting for transfers between devices: 443 us -> 0 us
  matrix products: 162 us -> 0 us
  Pallas kernels: 0 us -> 158 us
  blocking collectives: 111 us -> 0 us
  local copies, waits for them, and re-layouts: 86.6 us -> 0 us
  other arithmetic: 37.6 us -> 0 us
  between operations: 17.3 us -> 0.86 us
    reduce_scatter x3 -> x0, waiting for transfers between devices: 294 us -> none  [the longest x1 116 us: per_device(): lax.psum_scatter(g_weight_in, 'batch', scatter_dimension=0, tiled=True)]
    dot_general x21 -> x0, matrix products: 162 us -> none  [the longest x4 47.7 us: product(): return jnp.dot(left, right, preferred_element_type=jnp.float32)]
    pallas_call x0 -> x3, Pallas kernels: none -> 158 us  [the longest x1 116 us: backward(): pl.pallas_call(partial(backward_kernel, n), in_specs=[scalars] * 3 + [vme...]
    unnamed x11 -> x0, waiting for transfers between devices: 146 us -> none
    unnamed x2 -> x0, blocking collectives: 92.3 us -> none
    unnamed x137 -> x0, local copies, waits for them, and re-layouts: 39.4 us -> none
    reduce_sum x10 -> x0, other arithmetic: 19.1 us -> none  [the longest x2 5.69 us: norm_backward(): return (d_total, jnp.sum(grad * normed, axis=0), jnp.sum(grad, axis=0))]
    all_gather x1 -> x0, blocking collectives: 19.1 us -> none  [per_device(): lax.all_gather(mine, 'batch', axis=0, tiled=True)]
  transfers between devices with their start and end apart: 9 -> 0, of which waited for: 6 -> 0; matrix products, arithmetic and copies ran while one was open for 11% -> 0% of each run, Pallas kernels for 0% -> 0%
where the time goes in v3:
time: 159 us
  Pallas kernels  158 us (99%)
    pallas_call x1, Pallas kernels, backward(): pl.pallas_call(partial(backward_kernel, n), in_specs=[scalars] * 3 + [vme...  116 us
    pallas_call x1, Pallas kernels, encoder(): pl.pallas_call(encoder_kernel, grid_spec=pltpu.PrefetchScalarGridSpec(num...  36.8 us
    pallas_call x1, Pallas kernels, deliver(): pl.pallas_call(deliver_kernel, in_specs=[anywhere] * 6, out_specs=[anywhe...  4.7 us

profile of v3, /device:TPU:0, one launch (start us, length us, event | category | flops | bytes accessed | tf_op | source)
XLA Modules:
  0.0 158.8 jit_solution(9531921286753339243)
XLA Ops:
  0.6 36.8 %encoder.1 = (f32[4,768]{1,0:T(4,128)}, bf16[1024,3072]{1,0:T(8,128)(2,1)}, bf16[1024,3072]{1,0:T(8,128)(2,1)}, bf16[1024,768]{1,0:T(8,128)(2,1)}, bf16[1024,768...) custom-call(s32[4]{0:T(128)} %bitcast.14, ...), custom_call_target="tpu_custom_call" | custom-call | tf_op jit(solution)/shard_map/encoder/pallas_call | solution.py:200
  37.4 116.4 %backward.1 = (f32[192,768]{1,0:T(8,128)}, f32[48,3072]{1,0:T(8,128)}, f32[48,768]{1,0:T(8,128)}, f32[48,2304]{1,0:T(8,128)}, f32[16,128]{1,0:T(8,128)}, /*index=5*/f32[1024,768]{1,0:T(8,128)}) custom-call(s32[4]{0:T(128)} %bitcast.15, s32[4]{0:T(128)} %positives.1, s32[4]{0:T(128)} %datasets.1, f32[4,768]{1,0:T(4,128)} %get-tuple-element.36.pooled_ref, ...), custom_call_target="tpu_custom_call" | custom-call | tf_op jit(solution)/shard_map/backward/pallas_call | solution.py:702
  153.9 4.7 %deliver.1 = (f32[192,768]{1,0:T(8,128)}, f32[48,3072]{1,0:T(8,128)}, f32[48,768]{1,0:T(8,128)}, f32[48,2304]{1,0:T(8,128)}, f32[1,192]{1,0:T(1,128)}, /*index=5...) custom-call(f32[192,768]{1,0:T(8,128)} %get-tuple-element.49.out_hbm, f32[48,3072]{1,0:T(8,128)} %get-tuple-element.50.in_hbm, ...), custom_call_target="tpu_custom_call" | custom-call | tf_op jit(solution)/shard_map/deliver/pallas_call | solution.py:771

commit v4 on v3

--- a/solution.py
+++ b/solution.py
@@ -328,11 +328,12 @@
 def d_pooled_of(n, tower, me, everyone):
     seqs = 4 * n
     packed = everyone[...]
-    questions = packed[:n].reshape(16 * n, 256)
-    passages = packed[n:].reshape(16 * n, 256)
+    questions, passages = (
+        jnp.concatenate([packed[core, side].reshape(8 * n, 256) for core in range(2)], axis=0) for side in range(2)
+    )
     rows = lax.broadcasted_iota(jnp.int32, (seqs, 16 * n), 0)
     places = lax.broadcasted_iota(jnp.int32, (seqs, 16 * n), 1)
-    owner, lane = rows // 4, lax.rem(rows, 4)
+    owner, lane = lax.rem(rows // 4, 2) * (n // 2) + rows // 8, lax.rem(rows, 4)
 
     def picked(values, row):
         return product(select(places == owner * 16 + row).astype(LOW), values)
@@ -386,20 +387,24 @@
     sems, stage_sems, small_send, small_recv, pool_send, pool_recv,
 ):
     tower, me = lax.axis_index("tower"), lax.axis_index("batch")
-    flat = tower * n + me
-    everybody = 2 * n
+    chips = n // 2
+    chip, core = me // 2, lax.rem(me, 2)
     sums = Sums(
         n, (grads, paired, crossed, rows_got, got, pair_send, pair_recv, cross_send, cross_recv, z_send, z_recv)
     )
     barrier = pltpu.get_barrier_semaphore()
 
-    def other_device(step):
-        other = lax.rem(flat + step, everybody)
-        return other // n, lax.rem(other, n)
-
-    @pl.loop(1, everybody)
+    @pl.loop(1, n)
     def _(step):
-        pl.semaphore_signal(barrier, inc=1, device_id=other_device(step), device_id_type=MESH)
+        pl.semaphore_signal(
+            barrier, inc=1, device_id=(tower, lax.rem(me + step, n)), device_id_type=MESH
+        )
+
+    @pl.loop(0, chips)
+    def _(other):
+        pl.semaphore_signal(
+            barrier, inc=1, device_id=(1 - tower, 2 * other + core), device_id_type=MESH
+        )
 
     def load(place, source, target):
         return pltpu.make_async_copy(source, target, sems.at[place])
@@ -443,25 +448,49 @@
         [pooled[:, 0:256], pooled[:, 256:512], pooled[:, 512:768], extra], axis=0
     ).astype(LOW)
     mine[...] = pooled_block
-    everyone[flat] = pooled_block
+
+    @pl.when(tower == 0)
+    def _():
+        everyone[core, 0] = jnp.zeros((chips, 16, 256), LOW)
+
+    everyone[core, tower, chip] = pooled_block
     rows_small[...] = jnp.zeros_like(rows_small)
     bias_in[...] = jnp.zeros_like(bias_in)
-    pl.semaphore_wait(barrier, everybody - 1)
-
-    def pool_copy(step):
+    pl.semaphore_wait(barrier, n - 1 + chips)
+
+    def pool_copy(side, step, slot):
         return pltpu.make_async_remote_copy(
-            src_ref=mine, dst_ref=everyone.at[flat], send_sem=pool_send.at[step], recv_sem=pool_recv.at[step],
-            device_id=other_device(step), device_id_type=MESH,
+            src_ref=mine, dst_ref=everyone.at[core, tower, chip],
+            send_sem=pool_send.at[slot], recv_sem=pool_recv.at[slot],
+            device_id=(side, 2 * lax.rem(chip + step, chips) + core), device_id_type=MESH,
         )
 
-    @pl.loop(1, everybody)
+    pool_forward = pltpu.make_async_remote_copy(
+        src_ref=everyone.at[core], dst_ref=everyone.at[core],
+        send_sem=pool_send.at[n], recv_sem=pool_recv.at[n],
+        device_id=(tower, me + 1 - 2 * core), device_id_type=MESH,
+    )
+
+    @pl.loop(0, chips)
     def _(step):
-        pool_copy(step).start()
-
-    @pl.loop(1, everybody)
+        pool_copy(1 - tower, step, chips + step).start()
+
+    @pl.when(tower == 1)
+    def _():
+        @pl.loop(1, chips)
+        def _(step):
+            pool_copy(1, step, step).start()
+
+        @pl.loop(1, chips)
+        def _(step):
+            pool_copy(1, step, step).wait_recv()
+
+    @pl.loop(0, chips)
     def _(step):
-        pool_copy(step).wait_recv()
-
+        pool_copy(1 - tower, step, chips + step).wait_recv()
+
+    pool_forward.start()
+    pool_forward.wait_recv()
     d_pooled[...] = d_pooled_of(n, tower, me, everyone)
 
     n2_load.wait()
@@ -495,9 +524,17 @@
         if part in (1, 2):
             sums.cross(part - 1)
 
-    @pl.loop(1, everybody)
+    @pl.loop(0, chips)
     def _(step):
-        pool_copy(step).wait_send()
+        pool_copy(1 - tower, step, chips + step).wait_send()
+
+    @pl.when(tower == 1)
+    def _():
+        @pl.loop(1, chips)
+        def _(step):
+            pool_copy(1, step, step).wait_send()
+
+    pool_forward.wait_send()
 
     for copy in [out_load] + in_loads + [n1_load] + slope_loads:
         copy.wait()
@@ -521,13 +558,18 @@
         d_second = second_backward(seq)[0]
         d_branch = rows_c[rows]
         d_first = d_second
+        ahead, late = transposed_right(d_branch, first_weights[block(0), :]), None
         for part in range(4):
-            d_pre = (
-                transposed_right(d_branch, first_weights[block(part), :]) * wide[rows, block(part)].astype(F32)
-            ).astype(LOW)
+            d_hidden = ahead
+            if part < 3:
+                ahead = transposed_right(d_branch, first_weights[block(part + 1), :])
+            d_pre = (d_hidden * wide[rows, block(part)].astype(F32)).astype(LOW)
             wide[rows, block(part)] = d_pre
             bias_in[:, block(part)] += jnp.sum(d_pre.astype(F32), axis=0, keepdims=True)
-            d_first = d_first + transposed_right(d_pre, second_weights[block(part), :])
+            if late is not None:
+                d_first = d_first + transposed_right(late, second_weights[block(part - 1), :])
+            late = d_pre
+        d_first = d_first + transposed_right(late, second_weights[block(3), :])
         normal = rows_b[rows].astype(F32)
         scaled = d_first * gain_ref[0, 0:1]
         mean = jnp.mean(scaled, axis=1, keepdims=True)
@@ -588,23 +630,22 @@
         weight = first_weights[block(0), :]
         d_context = transposed_right(d_attended, weight).astype(LOW)
         d_context_t = transposed_right(weight, d_attended).astype(LOW)
-        for pair in range(6):
+
+        def d_probs_of(pair):
             lanes = slice(128 * pair, 128 * (pair + 1))
-            key_pair, query_pair, value_pair = key_t[lanes, rows], rows_a[rows, lanes], rows_b[rows, lanes]
-            d_context_pair, d_context_t_pair = d_context[:, lanes], d_context_t[lanes]
-            weighed = d_context_t_pair.astype(F32) * context_t[lanes, rows].astype(F32)
-            d_queries, d_keys, d_values = [], [], []
-            for one in range(2):
-                half = slice(64 * one, 64 * (one + 1))
-                head = 2 * pair + one
-                prob = wide[rows, 256 * head:256 * (head + 1)]
-                value_one = jnp.where((lane < 64) if one == 0 else (lane >= 64), value_pair, none)
-                d_prob = product(value_one, d_context_t_pair)
-                row_sum = jnp.sum(weighed[half], axis=0, keepdims=True)
-                d_score = (prob.astype(F32) * (d_prob - row_sum)).astype(LOW)
-                d_values.append(product(prob, d_context_pair))
-                d_keys.append(product(d_score, query_pair))
-                d_queries.append(product(key_pair[half], d_score))
+            value_pair = rows_b[rows, lanes]
+            return [
+                product(jnp.where(mask, value_pair, none), d_context_t[lanes]) for mask in (lane < 64, lane >= 64)
+            ]
+
+        ahead, late = d_probs_of(0), None
+
+        def d_projected_of(pair, probs, d_scores):
+            lanes = slice(128 * pair, 128 * (pair + 1))
+            key_pair, query_pair, d_context_pair = key_t[lanes, rows], rows_a[rows, lanes], d_context[:, lanes]
+            d_values = [product(prob, d_context_pair) for prob in probs]
+            d_keys = [product(d_score, query_pair) for d_score in d_scores]
+            d_queries = [product(key_pair[64 * one:64 * (one + 1)], d_scores[one]) for one in range(2)]
             d_query = (jnp.concatenate(d_queries, axis=0).T * 0.125).astype(LOW)
             d_key = jnp.where(lane < 64, d_keys[0], d_keys[1]).astype(LOW)
             d_value = jnp.where(lane < 64, d_values[0], d_values[1]).astype(LOW)
@@ -612,6 +653,24 @@
                 second_weights[aligned(1024 * part + seq * 256, 256, 256), lanes] = value
             rows_small[0:1, lanes] += jnp.sum(d_query.astype(F32), axis=0, keepdims=True)
             rows_small[1:2, lanes] += jnp.sum(d_value.astype(F32), axis=0, keepdims=True)
+
+        for pair in range(6):
+            d_probs = ahead
+            if pair < 5:
+                ahead = d_probs_of(pair + 1)
+            lanes = slice(128 * pair, 128 * (pair + 1))
+            weighed = d_context_t[lanes].astype(F32) * context_t[lanes, rows].astype(F32)
+            probs, d_scores = [], []
+            for one in range(2):
+                head = 2 * pair + one
+                row_sum = jnp.sum(weighed[64 * one:64 * (one + 1)], axis=0, keepdims=True)
+                prob = wide[rows, 256 * head:256 * (head + 1)]
+                probs.append(prob)
+                d_scores.append((prob.astype(F32) * (d_probs[one] - row_sum)).astype(LOW))
+            if late is not None:
+                d_projected_of(*late)
+            late = pair, probs, d_scores
+        d_projected_of(*late)
 
     for seq in (2, 3):
         stage_copy(seq, 0).wait()
@@ -717,7 +776,7 @@
             pltpu.VMEM((rows, 128), F32), pltpu.VMEM((2, 256, 768), F32),
             pltpu.VMEM((8, 768), F32), pltpu.VMEM((1, 3072), F32),
             pltpu.VMEM((n, 16, 128), F32), pltpu.VMEM((n, 16, 128), F32),
-            pltpu.VMEM((16, 256), LOW), pltpu.VMEM((2 * n, 16, 256), LOW), pltpu.VMEM((8, 768), F32),
+            pltpu.VMEM((16, 256), LOW), pltpu.VMEM((2, 2, n // 2, 16, 256), LOW), pltpu.VMEM((8, 768), F32),
             dma((34,)), dma((3, 4)), dma((n,)), dma((n,)), dma((2 * n,)), dma((2 * n,)),
         ],
         compiler_params=pltpu.CompilerParams(collective_id=1, has_side_effects=True, vmem_limit_bytes=60 * MIB),

time: 159 us -> 156 us (0.981)
  Pallas kernels: 158 us -> 155 us
    pallas_call x1, Pallas kernels: 116 us -> 113 us  [backward(): pl.pallas_call(partial(backward_kernel, n), in_specs=[scalars] * 3 + [vme...]
where the time goes in v4:
time: 156 us
  Pallas kernels  155 us (99%)
    pallas_call x1, Pallas kernels, backward(): pl.pallas_call(partial(backward_kernel, n), in_specs=[scalars] * 3 + [vme...  113 us
    pallas_call x1, Pallas kernels, encoder(): pl.pallas_call(encoder_kernel, grid_spec=pltpu.PrefetchScalarGridSpec(num...  36.8 us
    pallas_call x1, Pallas kernels, deliver(): pl.pallas_call(deliver_kernel, in_specs=[anywhere] * 6, out_specs=[anywhe...  4.7 us

profile of v4, /device:TPU:0, one launch (start us, length us, event | category | flops | bytes accessed | tf_op | source)
XLA Modules:
  0.0 155.7 jit_solution(10671567250231750865)
XLA Ops:
  0.6 36.8 %encoder.1 = (f32[4,768]{1,0:T(4,128)}, bf16[1024,3072]{1,0:T(8,128)(2,1)}, bf16[1024,3072]{1,0:T(8,128)(2,1)}, bf16[1024,768]{1,0:T(8,128)(2,1)}, bf16[1024,768...) custom-call(s32[4]{0:T(128)} %bitcast.14, ...), custom_call_target="tpu_custom_call" | custom-call | tf_op jit(solution)/shard_map/encoder/pallas_call | solution.py:200
  37.4 113.4 %backward.1 = (f32[192,768]{1,0:T(8,128)}, f32[48,3072]{1,0:T(8,128)}, f32[48,768]{1,0:T(8,128)}, f32[48,2304]{1,0:T(8,128)}, f32[16,128]{1,0:T(8,128)}, /*index=5*/f32[1024,768]{1,0:T(8,128)}) custom-call(s32[4]{0:T(128)} %bitcast.15, s32[4]{0:T(128)} %positives.1, s32[4]{0:T(128)} %datasets.1, f32[4,768]{1,0:T(4,128)} %get-tuple-element.36.pooled_ref, ...), custom_call_target="tpu_custom_call" | custom-call | tf_op jit(solution)/shard_map/backward/pallas_call | solution.py:761
  150.8 4.7 %deliver.1 = (f32[192,768]{1,0:T(8,128)}, f32[48,3072]{1,0:T(8,128)}, f32[48,768]{1,0:T(8,128)}, f32[48,2304]{1,0:T(8,128)}, f32[1,192]{1,0:T(1,128)}, /*index=5...) custom-call(f32[192,768]{1,0:T(8,128)} %get-tuple-element.49.out_hbm, f32[48,3072]{1,0:T(8,128)} %get-tuple-element.50.in_hbm, ...), custom_call_target="tpu_custom_call" | custom-call | tf_op jit(solution)/shard_map/deliver/pallas_call | solution.py:830

commit v5 on v4

--- a/solution.py
+++ b/solution.py
@@ -234,11 +234,14 @@
 
 class Sums:
     def __init__(self, n, scratch):
-        (self.grads, self.paired, self.crossed, self.rows_got, self.got, self.pair_send, self.pair_recv,
+        (self.grads, self.paired, self.crossed, self.rows_got, self.relayed, self.got, self.z_first, self.pair_send, self.pair_recv,
          self.cross_send, self.cross_recv, self.z_send, self.z_recv) = scratch
         self.tower, self.me = lax.axis_index("tower"), lax.axis_index("batch")
         self.depth = n // 4
         self.z, self.y, self.core = self.me // 4, lax.rem(self.me // 2, 2), lax.rem(self.me, 2)
+        self.inner = (self.z == 1) | (self.z == 2)
+        self.beside = jnp.where(self.z < 2, 1 - self.z, 5 - self.z)
+        self.first = jnp.where(self.z < 2, 1, 0)
 
     def z_at(self, offset):
         return lax.rem(self.z + offset, self.depth)
@@ -267,35 +270,122 @@
             device_id=self.device(self.z_at(chunk + 1), self.y, self.core), device_id_type=MESH,
         )
 
-    def z_copy(self, chunk, offset):
+    def z_copy(self, chunk, part, target, slot):
         return pltpu.make_async_remote_copy(
-            src_ref=self.grads.at[chunk, self.y, self.core, self.z_at(offset)],
-            dst_ref=self.got.at[chunk - 4, offset - 1],
+            src_ref=self.grads.at[chunk, self.y, self.core, part], dst_ref=self.got.at[chunk - 4, slot],
+            send_sem=self.z_send.at[chunk, slot], recv_sem=self.z_recv.at[chunk, slot],
+            device_id=self.device(target, self.y, self.core), device_id_type=MESH,
+        )
+
+    def relay_copy(self, chunk):
+        return pltpu.make_async_remote_copy(
+            src_ref=self.grads.at[chunk, self.y, self.core, pl.ds(self.first, 3)], dst_ref=self.relayed.at[chunk - 4],
+            send_sem=self.z_send.at[chunk, 2], recv_sem=self.z_recv.at[chunk, 2],
+            device_id=self.device(self.beside, self.y, self.core), device_id_type=MESH,
+        )
+
+    def near_copy(self, chunk):
+        return pltpu.make_async_remote_copy(
+            src_ref=self.grads.at[chunk, self.y, self.core, self.beside], dst_ref=self.got.at[chunk - 4, 0],
+            send_sem=self.z_send.at[chunk, 2], recv_sem=self.z_recv.at[chunk, 0],
+            device_id=self.device(self.beside, self.y, self.core), device_id_type=MESH,
+        )
+
+    def mate_copy(self, chunk):
+        return self.z_copy(chunk, 3 - self.z, 3 - self.z, 0)
+
+    def far_copy(self, chunk):
+        far = 3 - self.beside
+        return self.z_copy(chunk, far, far, 1)
+
+    def straight_copy(self, chunk, offset):
+        return self.z_copy(chunk, self.z_at(offset), self.z_at(offset), offset - 1)
+
+    def z_first_copy(self, chunk, offset):
+        return pltpu.make_async_remote_copy(
+            src_ref=self.grads.at[chunk, :, self.core, self.z_at(offset)], dst_ref=self.z_first.at[offset - 1],
             send_sem=self.z_send.at[chunk, offset - 1], recv_sem=self.z_recv.at[chunk, offset - 1],
             device_id=self.device(self.z_at(offset), self.y, self.core), device_id_type=MESH,
         )
 
+    def y_last_copy(self, chunk):
+        return pltpu.make_async_remote_copy(
+            src_ref=self.grads.at[chunk, 1 - self.y, self.core, self.z], dst_ref=self.crossed.at[chunk, 0],
+            send_sem=self.cross_send.at[chunk], recv_sem=self.cross_recv.at[chunk],
+            device_id=self.device(self.z, 1 - self.y, self.core), device_id_type=MESH,
+        )
+
+    def z_first_spread(self, chunk):
+        self.pair_copy(chunk).wait_recv()
+        for y in range(2):
+            for z in range(self.depth):
+                place = (chunk, y, self.core, z)
+                self.grads[place] = (self.grads[place].astype(F32) + self.paired[chunk, y, z].astype(F32)).astype(LOW)
+        for offset in range(1, self.depth):
+            self.z_first_copy(chunk, offset).start()
+
+    def z_first_sum(self, chunk, y):
+        total = self.grads[chunk, y, self.core, self.z].astype(F32)
+        for slot in range(self.depth - 1):
+            total = total + self.z_first[slot, y].astype(F32)
+        return total
+
+    def z_first_cross(self, chunk):
+        for offset in range(1, self.depth):
+            self.z_first_copy(chunk, offset).wait_recv()
+        self.grads[chunk, 1 - self.y, self.core, self.z] = self.z_first_sum(chunk, 1 - self.y).astype(LOW)
+        self.y_last_copy(chunk).start()
+
+    def z_first_total(self, chunk):
+        self.y_last_copy(chunk).wait_recv()
+        return self.z_first_sum(chunk, self.y) + self.crossed[chunk, 0].astype(F32)
+
     def pair(self, chunk):
         self.pair_copy(chunk).start()
 
     def cross(self, chunk):
         self.pair_copy(chunk).wait_recv()
-        place = (chunk, 1 - self.y, self.core)
-        self.grads[place] = (self.grads[place].astype(F32) + self.paired[chunk, 1 - self.y].astype(F32)).astype(LOW)
+        for part in range(4):
+            place = (chunk, 1 - self.y, self.core, part)
+            self.grads[place] = (
+                self.grads[place].astype(F32) + self.paired[chunk, 1 - self.y, part].astype(F32)
+            ).astype(LOW)
         self.cross_copy(chunk).start()
 
-    def spread(self, chunk, by_rows=False, last=False):
+    def spread(self, chunk, by_rows=False, last=False, straight=False):
         self.cross_copy(chunk).wait_recv()
-        place = (chunk, self.y, self.core)
-        self.grads[place] = (
-            self.grads[place].astype(F32) + self.paired[chunk, self.y].astype(F32) + self.crossed[chunk].astype(F32)
-        ).astype(LOW)
+        for part in range(4):
+            place = (chunk, self.y, self.core, part)
+            self.grads[place] = (
+                self.grads[place].astype(F32) + self.paired[chunk, self.y, part].astype(F32)
+                + self.crossed[chunk, part].astype(F32)
+            ).astype(LOW)
         if by_rows:
             if not last:
                 self.rows_copy(chunk).start()
+        elif straight:
+            for offset in range(1, self.depth):
+                self.straight_copy(chunk, offset).start()
         else:
-            for offset in range(1, self.depth):
-                self.z_copy(chunk, offset).start()
+            @pl.when(self.inner)
+            def _():
+                self.near_copy(chunk).start()
+
+            @pl.when(jnp.logical_not(self.inner))
+            def _():
+                self.relay_copy(chunk).start()
+
+    def relay(self, chunk):
+        @pl.when(self.inner)
+        def _():
+            self.relay_copy(chunk).wait_recv()
+            for part in range(3):
+                place = (chunk, self.y, self.core, self.first + part)
+                self.grads[place] = (
+                    self.grads[place].astype(F32) + self.relayed[chunk - 4, part].astype(F32)
+                ).astype(LOW)
+            self.mate_copy(chunk).start()
+            self.far_copy(chunk).start()
 
     def rows_total(self, part):
         total = self.grads[3, self.y, self.core, part].astype(F32)
@@ -304,25 +394,46 @@
         return total
 
     def total(self, chunk):
+        self.mate_copy(chunk).wait_recv()
+
+        @pl.when(jnp.logical_not(self.inner))
+        def _():
+            self.far_copy(chunk).wait_recv()
+
+        total = self.grads[chunk, self.y, self.core, self.z].astype(F32) + self.got[chunk - 4, 0].astype(F32)
+        return total + jnp.where(self.inner, 0.0, self.got[chunk - 4, 1].astype(F32))
+
+    def straight_total(self, chunk):
         total = self.grads[chunk, self.y, self.core, self.z].astype(F32)
         for offset in range(1, self.depth):
-            self.z_copy(chunk, offset).wait_recv()
+            self.straight_copy(chunk, offset).wait_recv()
             total = total + self.got[chunk - 4, offset - 1].astype(F32)
         return total
 
     def close(self):
-        @pl.loop(0, CHUNKS)
-        def _(chunk):
+        for chunk in range(CHUNKS):
             self.pair_copy(chunk).wait_send()
-            self.cross_copy(chunk).wait_send()
+            (self.y_last_copy(chunk) if chunk == 8 else self.cross_copy(chunk)).wait_send()
+
+        for offset in range(1, self.depth):
+            self.z_first_copy(8, offset).wait_send()
+            for chunk in range(9, CHUNKS):
+                self.straight_copy(chunk, offset).wait_send()
 
         for chunk in range(3):
             self.rows_copy(chunk).wait_send()
 
-        @pl.loop(4, CHUNKS)
+        @pl.loop(4, 8)
         def _(chunk):
-            for offset in range(1, self.depth):
-                self.z_copy(chunk, offset).wait_send()
+            @pl.when(self.inner)
+            def _():
+                self.near_copy(chunk).wait_send()
+                self.mate_copy(chunk).wait_send()
+                self.far_copy(chunk).wait_send()
+
+            @pl.when(jnp.logical_not(self.inner))
+            def _():
+                self.relay_copy(chunk).wait_send()
 
 
 def d_pooled_of(n, tower, me, everyone):
@@ -381,7 +492,7 @@
     hidden_hbm, slope_hbm, n1_hbm, n2_hbm, inv_hbm, low_t_hbm, query_hbm, key_t_hbm, value_hbm, probs_hbm,
     context_t_hbm, x_t_hbm,
     out_ref, in_ref, attn_ref, qkv_ref, summed_small_ref, tokens_out,
-    grads, paired, crossed, rows_got, got, pair_send, pair_recv, cross_send, cross_recv, z_send, z_recv,
+    grads, paired, crossed, rows_got, relayed, got, z_first, pair_send, pair_recv, cross_send, cross_recv, z_send, z_recv,
     first_weights, second_weights, wide, tall, rows_a, rows_b, rows_c, key_t, context_t, inv, stage,
     rows_small, bias_in, small, small_got, mine, everyone, d_pooled,
     sems, stage_sems, small_send, small_recv, pool_send, pool_recv,
@@ -390,7 +501,7 @@
     chips = n // 2
     chip, core = me // 2, lax.rem(me, 2)
     sums = Sums(
-        n, (grads, paired, crossed, rows_got, got, pair_send, pair_recv, cross_send, cross_recv, z_send, z_recv)
+        n, (grads, paired, crossed, rows_got, relayed, got, z_first, pair_send, pair_recv, cross_send, cross_recv, z_send, z_recv)
     )
     barrier = pltpu.get_barrier_semaphore()
 
@@ -521,7 +632,7 @@
             grads[part, y] = transposed_left(wide[:, columns], rows_c[...]).astype(LOW).reshape(2, 4, 48, 768)
         slope_loads[part].start()
         sums.pair(part)
-        if part in (1, 2):
+        if part > 0:
             sums.cross(part - 1)
 
     @pl.loop(0, chips)
@@ -546,13 +657,13 @@
 
     @pl.loop(0, 4)
     def _(seq):
-        @pl.when(seq >= 1)
+        @pl.when(seq >= 2)
         def _():
-            sums.spread(lax.max(seq - 1, 0), by_rows=True)
-
-        @pl.when((seq >= 1) & (seq <= 2))
+            sums.spread(lax.max(seq - 2, 0), by_rows=True)
+
+        @pl.when(seq == 1)
         def _():
-            sums.cross(lax.min(seq + 1, 3))
+            sums.cross(3)
 
         rows = seq_rows(seq)
         d_second = second_backward(seq)[0]
@@ -601,10 +712,10 @@
 
     for part in range(4):
         store(4 + part, tall, wide[:, block(part)])
-        if part == 1:
-            sums.spread(3, by_rows=True, last=True)
         if part in (1, 2):
             sums.cross(3 + part)
+        if part in (0, 2):
+            sums.spread(2 + part // 2, by_rows=True, last=part == 2)
     for seq in range(4):
         probs_load(seq).start()
     x_load.start()
@@ -623,7 +734,18 @@
         @pl.when(seq >= 1)
         def _():
             sums.spread(3 + lax.max(seq, 1))
-            sums.cross(5 + lax.max(seq, 1))
+
+        @pl.when((seq == 1) | (seq == 2))
+        def _():
+            sums.cross(5 + lax.min(lax.max(seq, 1), 2))
+
+        @pl.when(seq == 3)
+        def _():
+            sums.relay(4)
+
+        @pl.when(seq == 0)
+        def _():
+            sums.z_first_spread(8)
 
         probs_load(seq).wait()
         d_attended = rows_c[rows]
@@ -677,11 +799,13 @@
     for seq in (0, 1):
         stage_copy(seq, 1).start()
     x_load.wait()
-    sums.spread(7)
     for part in range(3):
         store(9 + part, tall, second_weights[1024 * part:1024 * (part + 1), :])
-        if part == 1:
-            sums.cross(9)
+        if part == 0:
+            sums.relay(5)
+            sums.spread(7)
+        else:
+            sums.cross(8 + part)
 
     bundle, bias_row = rows_small[...], bias_in[...]
     small[...] = jnp.zeros_like(small)
@@ -699,8 +823,6 @@
             device_id=(tower, other), device_id_type=MESH,
         )
 
-    sums.spread(8)
-    sums.cross(10)
 
     @pl.loop(1, n)
     def _(step):
@@ -720,7 +842,10 @@
 
     tokens(0)
     tokens(1)
-    sums.spread(9)
+    sums.relay(6)
+    sums.relay(7)
+    sums.z_first_cross(8)
+    sums.spread(9, straight=True)
     sums.cross(11)
     for seq in (2, 3):
         stage_copy(seq - 2, 2).wait()
@@ -740,12 +865,12 @@
         out_ref[48 * part:48 * (part + 1)] = sums.rows_total(part)
     for chunk in range(4, 8):
         in_ref[:, block(chunk - 4)] = sums.total(chunk)
-    sums.spread(10)
-    attn_ref[...] = sums.total(8)
-    qkv_ref[:, block(0)] = sums.total(9)
-    sums.spread(11)
-    qkv_ref[:, block(1)] = sums.total(10)
-    qkv_ref[:, block(2)] = sums.total(11)
+    attn_ref[...] = sums.z_first_total(8)
+    sums.spread(10, straight=True)
+    qkv_ref[:, block(0)] = sums.straight_total(9)
+    sums.spread(11, straight=True)
+    qkv_ref[:, block(1)] = sums.straight_total(10)
+    qkv_ref[:, block(2)] = sums.straight_total(11)
     for seq in (2, 3):
         stage_copy(seq, 2).wait()
     sums.close()
@@ -768,7 +893,9 @@
         ],
         scratch_shapes=[
             pltpu.VMEM((CHUNKS, 2, 2, 4) + tile, LOW), pltpu.VMEM((CHUNKS, 2, 4) + tile, LOW),
-            pltpu.VMEM((CHUNKS, 4) + tile, LOW), pltpu.VMEM((3, 4) + tile, LOW), pltpu.VMEM((CHUNKS - 4, 3) + tile, LOW),
+            pltpu.VMEM((CHUNKS, 4) + tile, LOW), pltpu.VMEM((3, 4) + tile, LOW),
+            pltpu.VMEM((4, 3) + tile, LOW), pltpu.VMEM((CHUNKS - 4, 3) + tile, LOW),
+            pltpu.VMEM((3, 2) + tile, LOW),
             dma((CHUNKS,)), dma((CHUNKS,)), dma((CHUNKS,)), dma((CHUNKS,)), dma((CHUNKS, 3)), dma((CHUNKS, 3)),
             pltpu.VMEM((3072, 768), LOW), pltpu.VMEM((3072, 768), LOW), pltpu.VMEM((rows, 3072), LOW),
             pltpu.VMEM((768, rows), LOW), pltpu.VMEM((rows, 768), LOW), pltpu.VMEM((rows, 768), LOW),

time: 156 us -> 154 us (0.987)
  Pallas kernels: 155 us -> 153 us
    pallas_call x1, Pallas kernels: 113 us -> 112 us  [backward(): pl.pallas_call(partial(backward_kernel, n), in_specs=[scalars] * 3 + [vme...]
where the time goes in v5:
time: 154 us
  Pallas kernels  153 us (99%)
    pallas_call x1, Pallas kernels, backward(): pl.pallas_call(partial(backward_kernel, n), in_specs=[scalars] * 3 + [vme...  112 us
    pallas_call x1, Pallas kernels, encoder(): pl.pallas_call(encoder_kernel, grid_spec=pltpu.PrefetchScalarGridSpec(num...  36.8 us
    pallas_call x1, Pallas kernels, deliver(): pl.pallas_call(deliver_kernel, in_specs=[anywhere] * 6, out_specs=[anywhe...  4.7 us

profile of v5, /device:TPU:0, one launch (start us, length us, event | category | flops | bytes accessed | tf_op | source)
XLA Modules:
  0.0 154.0 jit_solution(3878563465541131742)
XLA Ops:
  0.6 36.8 %encoder.1 = (f32[4,768]{1,0:T(4,128)}, bf16[1024,3072]{1,0:T(8,128)(2,1)}, bf16[1024,3072]{1,0:T(8,128)(2,1)}, bf16[1024,768]{1,0:T(8,128)(2,1)}, bf16[1024,768...) custom-call(s32[4]{0:T(128)} %bitcast.14, ...), custom_call_target="tpu_custom_call" | custom-call | tf_op jit(solution)/shard_map/encoder/pallas_call | solution.py:200
  37.4 111.7 %backward.1 = (f32[192,768]{1,0:T(8,128)}, f32[48,3072]{1,0:T(8,128)}, f32[48,768]{1,0:T(8,128)}, f32[48,2304]{1,0:T(8,128)}, f32[16,128]{1,0:T(8,128)}, /*index=5*/f32[1024,768]{1,0:T(8,128)}) custom-call(s32[4]{0:T(128)} %bitcast.15, s32[4]{0:T(128)} %positives.1, s32[4]{0:T(128)} %datasets.1, f32[4,768]{1,0:T(4,128)} %get-tuple-element.36.pooled_ref, ...), custom_call_target="tpu_custom_call" | custom-call | tf_op jit(solution)/shard_map/backward/pallas_call | solution.py:886
  149.1 4.7 %deliver.1 = (f32[192,768]{1,0:T(8,128)}, f32[48,3072]{1,0:T(8,128)}, f32[48,768]{1,0:T(8,128)}, f32[48,2304]{1,0:T(8,128)}, f32[1,192]{1,0:T(1,128)}, /*index=5...) custom-call(f32[192,768]{1,0:T(8,128)} %get-tuple-element.49.out_hbm, f32[48,3072]{1,0:T(8,128)} %get-tuple-element.50.in_hbm, ...), custom_call_target="tpu_custom_call" | custom-call | tf_op jit(solution)/shard_map/deliver/pallas_call | solution.py:957

commit v6 on v5

--- a/solution.py
+++ b/solution.py
@@ -953,7 +953,7 @@
     vmem = pl.BlockSpec(memory_space=pltpu.VMEM)
     shapes = [array.shape for array in sums] + [(1, 192), (6, 1, 48), (2, 48), tokens.shape]
     rows, width = tokens.shape
-    parts = 4
+    parts = 16
     return pl.pallas_call(
         deliver_kernel,
         in_specs=[anywhere] * 6,

time: 154 us -> 155 us (level)
  no operation moved by 1% of the time
where the time goes in v6:
time: 155 us
  Pallas kernels  154 us (99%)
    pallas_call x1, Pallas kernels, backward(): pl.pallas_call(partial(backward_kernel, n), in_specs=[scalars] * 3 + [vme...  112 us
    pallas_call x1, Pallas kernels, encoder(): pl.pallas_call(encoder_kernel, grid_spec=pltpu.PrefetchScalarGridSpec(num...  36.8 us
    pallas_call x1, Pallas kernels, deliver(): pl.pallas_call(deliver_kernel, in_specs=[anywhere] * 6, out_specs=[anywhe...  5.4 us

profile of v6, /device:TPU:0, one launch (start us, length us, event | category | flops | bytes accessed | tf_op | source)
XLA Modules:
  0.0 154.7 jit_solution(1070652018190754716)
XLA Ops:
  0.6 36.8 %encoder.1 = (f32[4,768]{1,0:T(4,128)}, bf16[1024,3072]{1,0:T(8,128)(2,1)}, bf16[1024,3072]{1,0:T(8,128)(2,1)}, bf16[1024,768]{1,0:T(8,128)(2,1)}, bf16[1024,768...) custom-call(s32[4]{0:T(128)} %bitcast.14, ...), custom_call_target="tpu_custom_call" | custom-call | tf_op jit(solution)/shard_map/encoder/pallas_call | solution.py:200
  37.4 111.7 %backward.1 = (f32[192,768]{1,0:T(8,128)}, f32[48,3072]{1,0:T(8,128)}, f32[48,768]{1,0:T(8,128)}, f32[48,2304]{1,0:T(8,128)}, f32[16,128]{1,0:T(8,128)}, /*index=5*/f32[1024,768]{1,0:T(8,128)}) custom-call(s32[4]{0:T(128)} %bitcast.15, s32[4]{0:T(128)} %positives.1, s32[4]{0:T(128)} %datasets.1, f32[4,768]{1,0:T(4,128)} %get-tuple-element.36.pooled_ref, ...), custom_call_target="tpu_custom_call" | custom-call | tf_op jit(solution)/shard_map/backward/pallas_call | solution.py:886
  149.1 5.4 %deliver.1 = (f32[192,768]{1,0:T(8,128)}, f32[48,3072]{1,0:T(8,128)}, f32[48,768]{1,0:T(8,128)}, f32[48,2304]{1,0:T(8,128)}, f32[1,192]{1,0:T(1,128)}, /*index=5...) custom-call(f32[192,768]{1,0:T(8,128)} %get-tuple-element.49.out_hbm, f32[48,3072]{1,0:T(8,128)} %get-tuple-element.50.in_hbm, ...), custom_call_target="tpu_custom_call" | custom-call | tf_op jit(solution)/shard_map/deliver/pallas_call | solution.py:957
